TPU v7x, 32 devices: a whole 2x2x4 slice. The times are simulated.
32 devices in a mesh: group: 2 (over y), row: 4 (over x, core), col: 4 (over z).
Axes of the slice: x: 2, y: 2, z: 4, core: 2. Of those that a mesh axis runs over, the one named last changes fastest.
Arguments:
- hidden_in: bfloat16 [4096, 2048], P(('group', 'row'), 'col'), may hold values from -6 to 6
- segments: int32 [2, 2048], P('group'), may hold values from 0 to 7, never falling along the last dimension, each value on 1 to 1024 neighbouring positions
- attn_gain: float32 [2048], P('col'), may hold values from 0.5 to 1.5
- query_weight: bfloat16 [2048, 2048], P('col', 'row'), may hold values from -1.25 to 1.25
- key_matrix: bfloat16 [2048, 512], P('col', 'row'), may hold values from -1.25 to 1.25
- value_matrix: bfloat16 [2048, 512], P('col', 'row'), may hold values from -0.125 to 0.125
- out_weight: bfloat16 [2048, 2048], P('row', 'col'), may hold values from -4 to 4
- ffn_gain: float32 [2048], P('col'), may hold values from 0.5 to 1.5
- gate_weight: bfloat16 [2048, 8192], P('col', 'row'), may hold values from -0.125 to 0.125
- up_weight: bfloat16 [2048, 8192], P('col', 'row'), may hold values from -0.125 to 0.125
- down_weight: bfloat16 [8192, 2048], P('row', 'col'), may hold values from -1.25 to 1.25
- cotangent: bfloat16 [4096, 2048], P(('group', 'row'), 'col'), may hold values from -6 to 6
Outputs:
- layer_out: bfloat16 [4096, 2048], P(('group', 'row'), 'col')
- input_grad: float32 [4096, 2048], P(('group', 'row'), 'col')
- attn_gain_grad: float32 [2048], P('col')
- query_grad: float32 [2048, 2048], P('col', 'row')
- key_grad: float32 [2048, 512], P('col', 'row')
- value_grad: float32 [2048, 512], P('col', 'row')
- out_grad: float32 [2048, 2048], P('row', 'col')
- ffn_gain_grad: float32 [2048], P('col')
- gate_grad: float32 [2048, 8192], P('col', 'row')
- up_grad: float32 [2048, 8192], P('col', 'row')
- down_grad: float32 [8192, 2048], P('row', 'col')
Inputs may be any that keep to these rules, and one draw needn't show every extreme that they name: `segments`: in each sequence the segment numbers start at 0, never fall and take every value up to 7; a document holds 1 to 1024 tokens, and one document of every sequence holds exactly 1024.
All inputs are finite; a program needn't handle non-finite values.
Results may differ from a plain program's by a relative error of at most 0.02.
Values may be sent and summed in bfloat16 or wider, within the bound.
A program may use at most 192 MiB of HBM per device.

v0:
```python
import jax
import jax.numpy as jnp
from jax import lax
from jax.sharding import PartitionSpec as P

MODEL_WIDTH = 2048
QUERY_HEADS = 32
KEY_VALUE_HEADS = 8
HEAD_SIZE = 64
SEQUENCE_LENGTH = 2048


NORM_EPS = 1e-05
ROPE_BASE = 10000000.0
RES_SCALE = 0.22
SCORE_SCALE = 0.015625
FIRST_FIRST = (((0,), (0,)), ((), ()))
FIRST_SECOND = (((0,), (1,)), ((), ()))
SECOND_SECOND = (((1,), (1,)), ((), ()))


def row_gather(operand):
    return lax.all_gather(operand, "row", axis=0, tiled=True)


def row_reduce(operand):
    return lax.psum_scatter(
        operand.astype(jnp.bfloat16), "row", scatter_dimension=0, tiled=True
    ).astype(jnp.float32)


def col_gather(operand):
    return lax.all_gather(operand, "col", axis=1, tiled=True)


def col_reduce(term_fn, row_count):
    return lax.psum_scatter(
        term_fn(jnp.int32(0), row_count * lax.axis_size("col")),
        "col",
        scatter_dimension=0,
        tiled=True,
    )


def col_total(operand):
    return lax.psum(operand, "col")


def feature_sum(operand):
    return lax.psum(operand, "col")


def norm_forward(residual, gain_vec):
    norm_scale = lax.rsqrt(
        feature_sum(jnp.sum(residual * residual, axis=1)) / MODEL_WIDTH + NORM_EPS
    )
    return (norm_scale, (residual * norm_scale[:, None] * gain_vec[None, :]).astype(jnp.bfloat16))


def norm_backward(residual, gain_vec, norm_scale, grad_norm):
    product = feature_sum(jnp.sum(grad_norm * gain_vec[None, :] * residual, axis=1))
    cubed = norm_scale * norm_scale * norm_scale * product / MODEL_WIDTH
    grad_resid = norm_scale[:, None] * gain_vec[None, :] * grad_norm - residual * cubed[:, None]
    grad_gain = jnp.sum(grad_norm * residual * norm_scale[:, None], axis=0)
    return (grad_resid, grad_gain)


def rope_tables(segments):
    length_total = segments.shape[1]
    places = jnp.arange(length_total, dtype=jnp.int32)
    starts = jnp.concatenate(
        [jnp.ones((segments.shape[0], 1), jnp.bool_), segments[:, 1:] != segments[:, :-1]], axis=1
    )
    first_place = lax.cummax(jnp.where(starts, places[None, :], 0), axis=1)
    offset = (places[None, :] - first_place).reshape(-1).astype(jnp.float32)
    half_width = HEAD_SIZE // 2
    inverse = ROPE_BASE ** (-(2.0 * jnp.arange(half_width, dtype=jnp.float32)) / HEAD_SIZE)
    angles = inverse[:, None] * offset[None, :]
    return (jnp.cos(angles), jnp.sin(angles))


def rotate(operand, cosine, sine_table, direction):
    half_width = operand.shape[-2] // 2
    first_half = operand[..., :half_width, :]
    second = operand[..., half_width:, :]
    return jnp.concatenate(
        [
            first_half * cosine - direction * second * sine_table,
            second * cosine + direction * first_half * sine_table,
        ],
        axis=-2,
    )


def live_mask(segment_ids, row_start, key_start, block_rows, length_total):
    query_ids = row_start + jnp.arange(block_rows, dtype=jnp.int32)
    key_ids = key_start + jnp.arange(length_total, dtype=jnp.int32)
    query_seg = lax.dynamic_slice_in_dim(segment_ids, row_start, block_rows)
    return (key_ids[None, :] <= query_ids[:, None]) & (segment_ids[None, :] == query_seg[:, None])


def block_scores(query_rows, key_rotated, segment_ids, block_index, block_rows):
    row_start = block_index * block_rows
    key_start = row_start // SEQUENCE_LENGTH * SEQUENCE_LENGTH
    query_part = lax.dynamic_slice_in_dim(query_rows, row_start, block_rows, 2)
    scores = (
        jnp.einsum("hdq,dk->hqk", query_part, key_rotated, preferred_element_type=jnp.float32)
        * SCORE_SCALE
    )
    scores = jnp.where(
        live_mask(segment_ids, row_start, key_start, block_rows, SEQUENCE_LENGTH)[None],
        scores,
        -1e30,
    )
    return (row_start, key_start, query_part, key_rotated, scores)


def attend_forward(query_rows, key_rotated, value_rows, segment_ids):
    head_count, head_width, tok_total = query_rows.shape
    block_rows = min(512, SEQUENCE_LENGTH)

    def one_block(block_index):
        row_start, key_start, query_part, key_part, scores = block_scores(
            query_rows, key_rotated, segment_ids, block_index, block_rows
        )
        row_max = jnp.max(scores, axis=2, keepdims=True)
        numerator = jnp.exp(scores - row_max)
        denominator = jnp.sum(numerator, axis=2, keepdims=True)
        weights = (numerator / denominator).astype(jnp.bfloat16)
        mixed = jnp.einsum("hqk,dk->hdq", weights, value_rows, preferred_element_type=jnp.float32)
        return (mixed.astype(jnp.bfloat16), (row_max + jnp.log(denominator))[:, :, 0])

    mixed_all, log_all = lax.map(one_block, jnp.arange(tok_total // block_rows, dtype=jnp.int32))
    mixed_all = jnp.transpose(mixed_all, (1, 2, 0, 3)).reshape(head_count, head_width, tok_total)
    log_all = jnp.transpose(log_all, (1, 0, 2)).reshape(head_count, tok_total)
    return (mixed_all, log_all)


def attend_backward(query_rows, key_rotated, value_rows, segment_ids, log_total, grad_out):
    head_count, head_width, tok_total = query_rows.shape
    block_rows = min(512, SEQUENCE_LENGTH)

    def one_block(state_pair, block_index):
        grad_keys, grad_values = state_pair
        row_start, key_start, query_part, key_part, scores = block_scores(
            query_rows, key_rotated, segment_ids, block_index, block_rows
        )
        log_part = lax.dynamic_slice_in_dim(log_total, row_start, block_rows, 1)
        weights = jnp.exp(scores - log_part[:, :, None])
        grad_part = lax.dynamic_slice_in_dim(grad_out, row_start, block_rows, 2)
        grad_weights = jnp.einsum(
            "hdq,dk->hqk", grad_part, value_rows, preferred_element_type=jnp.float32
        )
        center = jnp.sum(weights * grad_weights, axis=2, keepdims=True)
        grad_scores = (weights * (grad_weights - center)).astype(jnp.bfloat16)
        grad_query = (
            jnp.einsum("hqk,dk->hdq", grad_scores, key_part, preferred_element_type=jnp.float32)
            * SCORE_SCALE
        )
        key_term = (
            jnp.einsum("hqk,hdq->dk", grad_scores, query_part, preferred_element_type=jnp.float32)
            * SCORE_SCALE
        )
        value_term = jnp.einsum(
            "hqk,hdq->dk",
            weights.astype(jnp.bfloat16),
            grad_part,
            preferred_element_type=jnp.float32,
        )
        grad_keys = grad_keys + key_term
        grad_values = grad_values + value_term
        return ((grad_keys, grad_values), grad_query)

    empty = jnp.zeros((head_width, tok_total), jnp.float32)
    (grad_keys, grad_values), grad_query = lax.scan(
        one_block, (empty, empty), jnp.arange(tok_total // block_rows, dtype=jnp.int32)
    )
    grad_query = jnp.transpose(grad_query, (1, 2, 0, 3)).reshape(head_count, head_width, tok_total)
    return (grad_keys, grad_values, grad_query)


def on_device(
    hidden_in,
    segments,
    attn_gain,
    query_weight,
    key_matrix,
    value_matrix,
    out_weight,
    ffn_gain,
    gate_weight,
    up_weight,
    down_weight,
    cotangent,
):
    residual = hidden_in.astype(jnp.float32)
    segment_ids = segments.reshape(-1)
    cosine, sine_table = rope_tables(segments)
    col_count = lax.axis_size("col")
    shared_width = key_matrix.shape[1]
    shared_heads = shared_width // HEAD_SIZE
    head_rows = query_weight.shape[1] // col_count
    ffn_rows = gate_weight.shape[1] // col_count
    heads_dev = head_rows // HEAD_SIZE
    heads_per_group = QUERY_HEADS // KEY_VALUE_HEADS
    shared_index = lax.axis_index("col") * heads_dev // heads_per_group
    joint_weight = jnp.concatenate([key_matrix, value_matrix], axis=1)
    scale_one, normed_one = norm_forward(residual, attn_gain)
    gathered_one = row_gather(normed_one)
    tok_total = gathered_one.shape[0]

    def query_term(row_start, row_count):
        return lax.dot_general(
            query_weight, gathered_one, FIRST_SECOND, preferred_element_type=jnp.float32
        )

    query_pre = col_reduce(query_term, head_rows)
    shared_pre = col_total(
        lax.dot_general(
            joint_weight, gathered_one, FIRST_SECOND, preferred_element_type=jnp.float32
        )
    )
    query_rotated = rotate(
        query_pre.reshape(heads_dev, HEAD_SIZE, tok_total), cosine, sine_table, 1.0
    ).astype(jnp.bfloat16)
    key_unrotated = lax.dynamic_index_in_dim(
        shared_pre[:shared_width].reshape(shared_heads, HEAD_SIZE, tok_total),
        shared_index,
        0,
        keepdims=False,
    )
    key_rotated = rotate(key_unrotated, cosine, sine_table, 1.0).astype(jnp.bfloat16)
    value_own = lax.dynamic_index_in_dim(
        shared_pre[shared_width:].reshape(shared_heads, HEAD_SIZE, tok_total),
        shared_index,
        0,
        keepdims=False,
    ).astype(jnp.bfloat16)
    attn_own, log_total = attend_forward(query_rotated, key_rotated, value_own, segment_ids)
    attn_all = col_gather(attn_own.reshape(1, head_rows, tok_total))[0]
    attn_part = lax.dot_general(
        attn_all, out_weight, FIRST_FIRST, preferred_element_type=jnp.float32
    )
    resid_mid = residual + RES_SCALE * row_reduce(attn_part)
    scale_two, normed_two = norm_forward(resid_mid, ffn_gain)
    gathered_two = row_gather(normed_two)

    def ffn_term(row_start, row_count):
        gate_part = lax.dot_general(
            gate_weight, gathered_two, FIRST_SECOND, preferred_element_type=jnp.float32
        )
        up_part = lax.dot_general(
            up_weight, gathered_two, FIRST_SECOND, preferred_element_type=jnp.float32
        )
        return jnp.concatenate([gate_part, up_part], axis=1)

    gate_up = col_reduce(ffn_term, ffn_rows)
    gate_pre = gate_up[:, :tok_total]
    up_pre = gate_up[:, tok_total:]
    gate_sig = jax.nn.sigmoid(gate_pre)
    gate_act = gate_pre * gate_sig
    hidden_act = (gate_act * up_pre).astype(jnp.bfloat16)
    hidden_all = col_gather(hidden_act[None])[0]
    down_part = lax.dot_general(
        hidden_all, down_weight, FIRST_FIRST, preferred_element_type=jnp.float32
    )
    layer_out = (resid_mid + RES_SCALE * row_reduce(down_part)).astype(jnp.bfloat16)
    grad_top = cotangent.astype(jnp.float32)
    grad_ffn = (RES_SCALE * grad_top).astype(jnp.bfloat16)
    branch_all = row_gather(grad_ffn)
    down_grad = jnp.dot(hidden_all, branch_all, preferred_element_type=jnp.float32)

    def hidden_term(row_start, row_count):
        return lax.dot_general(
            down_weight, branch_all, SECOND_SECOND, preferred_element_type=jnp.float32
        )

    grad_hidden = col_reduce(hidden_term, ffn_rows)
    grad_gate = (grad_hidden * up_pre * gate_sig * (1.0 + gate_pre * (1.0 - gate_sig))).astype(
        jnp.bfloat16
    )
    grad_up = (grad_hidden * gate_act).astype(jnp.bfloat16)
    pair_all = col_gather(jnp.stack([grad_gate, grad_up]))
    gate_grad = lax.dot_general(
        gathered_two, pair_all[0], FIRST_SECOND, preferred_element_type=jnp.float32
    )
    up_grad = lax.dot_general(
        gathered_two, pair_all[1], FIRST_SECOND, preferred_element_type=jnp.float32
    )
    grad_normed_two = lax.dot_general(
        pair_all[0], gate_weight, FIRST_SECOND, preferred_element_type=jnp.float32
    ) + lax.dot_general(pair_all[1], up_weight, FIRST_SECOND, preferred_element_type=jnp.float32)
    grad_mid_norm, ffn_gain_part = norm_backward(
        resid_mid, ffn_gain, scale_two, row_reduce(grad_normed_two)
    )
    grad_mid = grad_top + grad_mid_norm
    grad_attn = (RES_SCALE * grad_mid).astype(jnp.bfloat16)
    attn_branch_all = row_gather(grad_attn)
    out_grad = jnp.dot(attn_all, attn_branch_all, preferred_element_type=jnp.float32)

    def heads_term(row_start, row_count):
        return lax.dot_general(
            out_weight, attn_branch_all, SECOND_SECOND, preferred_element_type=jnp.float32
        )

    grad_heads = (
        col_reduce(heads_term, head_rows)
        .astype(jnp.bfloat16)
        .reshape(heads_dev, HEAD_SIZE, tok_total)
    )
    grad_key_rot, grad_value_own, grad_query_rot = attend_backward(
        query_rotated, key_rotated, value_own, segment_ids, log_total, grad_heads
    )
    grad_query_pre = (
        rotate(grad_query_rot, cosine, sine_table, -1.0)
        .astype(jnp.bfloat16)
        .reshape(head_rows, tok_total)
    )
    placed = jnp.zeros((2, shared_heads, HEAD_SIZE, tok_total), jnp.float32)
    placed = lax.dynamic_update_slice_in_dim(
        placed, jnp.stack([grad_key_rot, grad_value_own])[:, None], shared_index, 1
    )
    shared_sum = col_total(placed)
    grad_key_pre = rotate(shared_sum[0], cosine, sine_table, -1.0)
    grad_shared = (
        jnp.concatenate([grad_key_pre, shared_sum[1]], axis=0)
        .astype(jnp.bfloat16)
        .reshape(2 * shared_width, tok_total)
    )
    query_all = col_gather(grad_query_pre[None])[0]
    query_grad = lax.dot_general(
        gathered_one, query_all, FIRST_SECOND, preferred_element_type=jnp.float32
    )
    joint_grad = lax.dot_general(
        gathered_one, grad_shared, FIRST_SECOND, preferred_element_type=jnp.float32
    )
    key_grad = joint_grad[:, :shared_width]
    value_grad = joint_grad[:, shared_width:]
    grad_normed_one = lax.dot_general(
        query_all, query_weight, FIRST_SECOND, preferred_element_type=jnp.float32
    ) + lax.dot_general(grad_shared, joint_weight, FIRST_SECOND, preferred_element_type=jnp.float32)
    grad_in_norm, attn_gain_part = norm_backward(
        residual, attn_gain, scale_one, row_reduce(grad_normed_one)
    )
    input_grad = grad_mid + grad_in_norm
    attn_gain_grad, ffn_gain_grad = lax.psum((attn_gain_part, ffn_gain_part), ("group", "row"))
    query_grad, key_grad, value_grad, out_grad, gate_grad, up_grad, down_grad = (
        lax.psum(query_grad.astype(jnp.bfloat16), "group").astype(jnp.float32),
        lax.psum(key_grad.astype(jnp.bfloat16), "group").astype(jnp.float32),
        lax.psum(value_grad.astype(jnp.bfloat16), "group").astype(jnp.float32),
        lax.psum(out_grad.astype(jnp.bfloat16), "group").astype(jnp.float32),
        lax.psum(gate_grad.astype(jnp.bfloat16), "group").astype(jnp.float32),
        lax.psum(up_grad.astype(jnp.bfloat16), "group").astype(jnp.float32),
        lax.psum(down_grad.astype(jnp.bfloat16), "group").astype(jnp.float32),
    )
    return (
        layer_out,
        input_grad,
        attn_gain_grad,
        query_grad,
        key_grad,
        value_grad,
        out_grad,
        ffn_gain_grad,
        gate_grad,
        up_grad,
        down_grad,
    )


def solution(mesh):
    return jax.shard_map(
        on_device,
        mesh=mesh,
        in_specs=(
            P(("group", "row"), "col"),
            P("group", None),
            P("col"),
            P("col", "row"),
            P("col", "row"),
            P("col", "row"),
            P("row", "col"),
            P("col"),
            P("col", "row"),
            P("col", "row"),
            P("row", "col"),
            P(("group", "row"), "col"),
        ),
        out_specs=(
            P(("group", "row"), "col"),
            P(("group", "row"), "col"),
            P("col"),
            P("col", "row"),
            P("col", "row"),
            P("col", "row"),
            P("row", "col"),
            P("col"),
            P("col", "row"),
            P("col", "row"),
            P("row", "col"),
        ),
        check_vma=False,
    )
```

profile of v0, /device:TPU:0, one launch (start us, length us, event | category | flops | bytes accessed | tf_op | source)
XLA Modules:
  0.0 2349.5 jit_solution(10554518722797190067)
XLA Ops:
  8.6 13.5 psum.105
  26.1 19.0 all-gather.10.cloned.1.call-done
  55.4 80.0 %all-reduce.6.cloned.1.call-done = f32[256,2048]{1,0:T(8,128)} async-done(((f32[256,2048]{1,0:T(8,128)}), f32[256,2048]{1,0:T(8,128)}) %all-reduce.6.cloned.1.call-update) | async-done | bytes 2097168 | tf_op jit(solution)/shard_map/psum | solution.py:46
  139.9 74.2 %reduce-scatter.9.cloned.1.call-done = f32[128,2048]{0,1:T(8,128)} async-done(((f32[512,2048]{0,1:T(8,128)}), f32[128,2048]{0,1:T(8,128)}) %reduce-scatter.9.cloned.1.call-update) | async-done | bytes 1048592 | tf_op jit(solution)/shard_map/reduce_scatter | solution.py:37
  218.1 40.1 %while.31 = (s32[]{:T(128)}, bf16[4,2,64,512]{3,2,1,0:T(8,128)(2,1)}, f32[4,2,512]{2,1,0:T(2,128)S(1)}, s32[4]{0:T(128)S(1)}, s32[1,2048]{1,0:T(1,128)S(1)}, /*i...) while((s32[]{:T(128)}, ...), condition=%wide.region_9.10_spmd, body=%wide.region_6.9_spmd.sunk | while | flops 565249536 | bytes 30215036 | solution.py:133
  262.9 46.5 %all-gather.12.cloned.1.call-done = bf16[1,512,2048]{2,1,0:T(8,128)(2,1)} async-done(((bf16[1,128,2048]{2,1,0:T(8,128)(2,1)}), bf16[1,512,2048]{2,1,0:T(8,128)(2,1)}) %all-gather.12.cloned.1.call-update) | async-done | bytes 2097168 | tf_op jit(solution)/shard_map/all_gather | solution.py:33
  315.8 28.3 %reduce-scatter.11.cloned.1.call-done = bf16[512,512]{1,0:T(8,128)(2,1)} async-done(((bf16[2048,512]{1,0:T(8,128)(2,1)}), bf16[512,512]{1,0:T(8,128)(2,1)}) %reduce-scatter.11.cloned.1.call-update) | async-done | bytes 524304 | tf_op jit(solution)/shard_map/reduce_scatter | solution.py:27
  345.4 11.9 psum.107
  368.7 13.0 convolution_bitcast_fusion.1
  381.8 11.7 all-gather.14.cloned.1.call-done
  409.0 18.9 pad_maximum_fusion
  428.4 248.0 %reduce-scatter.17.cloned.1.call-done = f32[512,2048]{0,1:T(8,128)} async-done(((f32[2048,2048]{0,1:T(8,128)}), f32[512,2048]{0,1:T(8,128)}) %reduce-scatter.17.cloned.1.call-update) | async-done | bytes 4194320 | tf_op jit(solution)/shard_map/reduce_scatter | solution.py:37
  676.4 555.2 %reduce-scatter.13.cloned.1.call-done = f32[512,4096]{0,1:T(8,128)} async-done(((f32[2048,4096]{0,1:T(8,128)}), f32[512,4096]{0,1:T(8,128)}) %reduce-scatter.13.cloned.1.call-update) | async-done | bytes 8388624 | tf_op jit(solution)/shard_map/reduce_scatter | solution.py:37
  1241.1 287.6 %all-gather.18.cloned.1.call-done = bf16[2,2048,2048]{1,2,0:T(8,128)(2,1)} async-done(((bf16[2,512,2048]{1,2,0:T(8,128)(2,1)}), bf16[2,2048,2048]{1,2,0:T(8,128)(2,1)}) %all-gather.18.cloned.1.call-update) | async-done | bytes 16777232 | tf_op jit(solution)/shard_map/all_gather | solution.py:33
  1546.1 29.7 %reduce-scatter.19.cloned.1.call-done = bf16[512,512]{1,0:T(8,128)(2,1)} async-done(((bf16[2048,512]{1,0:T(8,128)(2,1)}), bf16[512,512]{1,0:T(8,128)(2,1)}) %reduce-scatter.19.cloned.1.call-update) | async-done | bytes 524304 | tf_op jit(solution)/shard_map/reduce_scatter | solution.py:27
  1577.9 11.7 psum.108
  1592.0 19.9 all-gather.20.cloned.1.call-done
  1617.1 76.7 %reduce-scatter.21.cloned.1.call-done = f32[128,2048]{0,1:T(8,128)} async-done(((f32[512,2048]{0,1:T(8,128)}), f32[128,2048]{0,1:T(8,128)}) %reduce-scatter.21.cloned.1.call-update) | async-done | bytes 1048592 | tf_op jit(solution)/shard_map/reduce_scatter | solution.py:37
  1695.3 89.4 %while.32 = (s32[]{:T(128)}, f32[64,2048]{1,0:T(8,128)S(1)}, f32[64,2048]{1,0:T(8,128)}, f32[4,2,64,512]{3,2,1,0:T(8,128)}, s32[4]{0:T(128)S(1)}, /*index=5*/bf1...) while((s32[]{:T(128)}, f32[64,2048]{1,0:T(8,128)S(1)}, ...), condition=%wide.region_22.23_spmd.clone, body=%wide.region_20.22_spmd.clone.sunk | while | flops 1377502720 | bytes 121175008 | solution.py:175
  1789.8 85.8 %all-reduce.8.cloned.1.call-done = f32[2,2,64,2048]{3,2,1,0:T(8,128)} async-done(((f32[2,2,64,2048]{3,2,1,0:T(8,128)}), f32[2,2,64,2048]{3,2,1,0:T(8,128)}) %all-reduce.8.cloned.1.call-update) | async-done | bytes 2097168 | tf_op jit(solution)/shard_map/psum | solution.py:46
  1883.9 40.0 %all-gather.22.cloned.1.call-done = bf16[1,512,2048]{2,1,0:T(8,128)(2,1)} async-done(((bf16[1,128,2048]{2,1,0:T(8,128)(2,1)}), bf16[1,512,2048]{2,1,0:T(8,128)(2,1)}) %all-gather.22.cloned.1.call-update) | async-done | bytes 2097168 | tf_op jit(solution)/shard_map/all_gather | solution.py:33
  1929.5 144.8 %all-gather.24.cloned.1.call-done = bf16[2048,2048]{0,1:T(8,128)(2,1)} async-done(((bf16[512,2048]{0,1:T(8,128)(2,1)}), bf16[2048,2048]{0,1:T(8,128)(2,1)}) %all-gather.24.cloned.1.call-update) | async-done | bytes 8388624 | tf_op jit(solution)/shard_map/all_gather | solution.py:33
  2117.4 14.4 all-reduce
  2144.7 184.7 %all-reduce.10.cloned.1.call-done = (bf16[512,512]{1,0:T(8,128)(2,1)}, bf16[512,128]{1,0:T(8,128)(2,1)}, bf16[512,128]{1,0:T(8,128)(2,1)}, bf16[512,512]{1,0:T(8...) async-done(((bf16[512,512]{1,0:T(8,128)(2,1)}, bf16[512,128]{1,0:T(8,128)(2,1)}, bf16[512,128]{1,0:T(8,128)(2,1)}, ...) | async-done | bytes 7602192 | tf_op jit(solution)/shard_map/psum | solution.py:348
  (328 shorter events, 313.1 us)
Async XLA Ops:
  7.2 393.5 %copy-start = (bf16[512,2048]{1,0:T(8,128)(2,1)S(1)}, bf16[512,2048]{1,0:T(8,128)(2,1)}, u32[]{:S(2)}) copy-start(bf16[512,2048]{1,0:T(8,128)(2,1)} %param.24) | copy-start | bytes 6291460
  7.2 38.0 %all-gather.10.cloned.1.call-start = ((), (), s32[]{:S(2)}) async-start(), calls=%async_computation.8 | async-start | bytes 2621440 | tf_op jit(solution)/shard_map/all_gather | solution.py:23
  24.2 111.2 %all-reduce.6.cloned.1.call-start = ((), (), s32[]{:S(2)}) async-start(), calls=%async_computation.10 | async-start | bytes 4194304 | tf_op jit(solution)/shard_map/psum | solution.py:46
  48.8 165.3 %reduce-scatter.9.cloned.1.call-start = ((), (), s32[]{:S(2)}) async-start(), calls=%async_computation.9 | async-start | bytes 5242880 | tf_op jit(solution)/shard_map/reduce_scatter | solution.py:37
  53.8 255.7 %all-gather.12.cloned.1.call-start = ((), (), s32[]{:S(2)}) async-start(), calls=%async_computation.11 | async-start | bytes 2621440 | tf_op jit(solution)/shard_map/all_gather | solution.py:33
  262.9 81.2 %reduce-scatter.11.cloned.1.call-start = ((), (), s32[]{:S(2)}) async-start(), calls=%async_computation.12 | async-start | bytes 2621440 | tf_op jit(solution)/shard_map/reduce_scatter | solution.py:27
  313.7 55.0 %all-gather.16.cloned.1.call-start = ((), (), s32[]{:S(2)}) async-start(), calls=%async_computation.16 | async-start | bytes 2621440 | tf_op jit(solution)/shard_map/all_gather | solution.py:23
  315.7 77.8 %all-gather.14.cloned.1.call-start = ((), (), s32[]{:S(2)}) async-start(), calls=%async_computation.13 | async-start | bytes 2621440 | tf_op jit(solution)/shard_map/all_gather | solution.py:23
  357.3 1232.3 %copy-start.33 = (f32[512]{0:T(512)}, f32[512]{0:T(512)S(1)}, u32[]{:S(2)}) copy-start(f32[512]{0:T(512)S(1)} %add_rsqrt_fusion) | copy-start | bytes 6148
  359.4 317.0 %reduce-scatter.17.cloned.1.call-start = ((), (), s32[]{:S(2)}) async-start(), calls=%async_computation.17 | async-start | bytes 20971520 | tf_op jit(solution)/shard_map/reduce_scatter | solution.py:37
  381.8 849.8 %reduce-scatter.13.cloned.1.call-start = ((), (), s32[]{:S(2)}) async-start(), calls=%async_computation.14 | async-start | bytes 41943040 | tf_op jit(solution)/shard_map/reduce_scatter | solution.py:37
  427.9 1100.7 %all-gather.18.cloned.1.call-start = ((), (), s32[]{:S(2)}) async-start(), calls=%async_computation.18 | async-start | bytes 20971520 | tf_op jit(solution)/shard_map/all_gather | solution.py:33
  1241.0 334.8 %reduce-scatter.19.cloned.1.call-start = ((), (), s32[]{:S(2)}) async-start(), calls=%async_computation.19 | async-start | bytes 2621440 | tf_op jit(solution)/shard_map/reduce_scatter | solution.py:27
  1546.0 65.9 %all-gather.20.cloned.1.call-start = ((), (), s32[]{:S(2)}) async-start(), calls=%async_computation.20 | async-start | bytes 2621440 | tf_op jit(solution)/shard_map/all_gather | solution.py:23
  1591.9 101.8 %reduce-scatter.21.cloned.1.call-start = ((), (), s32[]{:S(2)}) async-start(), calls=%async_computation.21 | async-start | bytes 5242880 | tf_op jit(solution)/shard_map/reduce_scatter | solution.py:37
  1616.8 258.8 %all-reduce.8.cloned.1.call-start = ((), (), s32[]{:S(2)}) async-start(), calls=%async_computation.23 | async-start | bytes 4194304 | tf_op jit(solution)/shard_map/psum | solution.py:46
  1786.3 90.7 %copy-start.16 = (f32[32,2048]{1,0:T(8,128)S(1)}, f32[32,2048]{1,0:T(8,128)}, u32[]{:S(2)}) copy-start(f32[32,2048]{1,0:T(8,128)} %copy-done.15) | copy-start | bytes 786436
  1786.3 90.7 %copy-start.25 = (f32[32,2048]{1,0:T(8,128)S(1)}, f32[32,2048]{1,0:T(8,128)}, u32[]{:S(2)}) copy-start(f32[32,2048]{1,0:T(8,128)} %get-tuple-element.410) | copy-start | bytes 786436
  1788.5 135.5 %all-gather.22.cloned.1.call-start = ((), (), s32[]{:S(2)}) async-start(), calls=%async_computation.22 | async-start | bytes 2621440 | tf_op jit(solution)/shard_map/all_gather | solution.py:33
  1878.9 195.4 %all-gather.24.cloned.1.call-start = ((), (), s32[]{:S(2)}) async-start(), calls=%async_computation.25 | async-start | bytes 10485760 | tf_op jit(solution)/shard_map/all_gather | solution.py:33
  1879.5 235.3 %reduce-scatter.23.cloned.1.call-start = ((), (), s32[]{:S(2)}) async-start(), calls=%async_computation.24 | async-start | bytes 2621440 | tf_op jit(solution)/shard_map/reduce_scatter | solution.py:27
  1929.4 154.8 %copy-start.48 = (bf16[2048,512]{1,0:T(8,128)(2,1)S(1)}, bf16[2048,512]{1,0:T(8,128)(2,1)}, u32[]{:S(2)}) copy-start(bf16[2048,512]{1,0:T(8,128)(2,1)} %all-gather.16.cloned.1.call-done) | copy-start | bytes 6291460
  1929.4 212.1 %reduce-scatter.15.cloned.1.call-start = ((), (), s32[]{:S(2)}) async-start(), calls=%async_computation.15 | async-start | bytes 2621440 | tf_op jit(solution)/shard_map/reduce_scatter | solution.py:27
  2084.2 245.3 %all-reduce.10.cloned.1.call-start = ((), (), s32[]{:S(2)}) async-start(), calls=%async_computation.26 | async-start | bytes 15204352 | tf_op jit(solution)/shard_map/psum | solution.py:348
  (56 other events, 929.2 us)
Sparse Core Ops, SparseCore 0:
  24.3 20.7 all-gather.9
  49.0 86.3 all-reduce.5
  138.4 75.7 reduce-scatter.8
  263.0 46.4 all-gather.11
  313.9 30.1 reduce-scatter.10
  346.1 22.5 all-gather.15
  371.0 22.5 all-gather.13
  396.0 280.3 reduce-scatter.16
  678.8 552.7 reduce-scatter.12
  1241.1 287.5 all-gather.17
  1546.2 29.5 reduce-scatter.18
  1592.1 19.8 all-gather.19
  1617.0 76.7 reduce-scatter.20
  1788.6 86.9 all-reduce.7
  1879.0 44.8 all-gather.21
  1925.9 148.3 all-gather.23
  2077.3 29.6 reduce-scatter.22
  2110.0 31.4 reduce-scatter.14
  2145.8 183.5 all-reduce.9
where the time goes:
time: 2360 us; the launch traced here: 2350 us
  waiting for transfers between devices  1940 us (82%)
  matrix products  192 us (8%)
  other arithmetic  96.3 us (4%)
  blocking collectives  61 us (3%)
  local copies, waits for them, and re-layouts  35.7 us (2%)
    reduce_scatter x4, waiting for transfers between devices, col_reduce(): lax.psum_scatter(term_fn(jnp.int32(0), row_count * lax.axis_size('col')),...  954 us
    all_gather x4, waiting for transfers between devices, col_gather(): return lax.all_gather(operand, 'col', axis=1, tiled=True)  519 us
    psum x1, waiting for transfers between devices, on_device(): lax.psum(query_grad.astype(jnp.bfloat16), 'group').astype(jnp.float32)  185 us
    psum x2, waiting for transfers between devices, col_total(): return lax.psum(operand, 'col')  166 us
    all_gather x4, waiting for transfers between devices, row_gather(): return lax.all_gather(operand, 'row', axis=0, tiled=True)  60 us
    reduce_scatter x4, waiting for transfers between devices, row_reduce(): lax.psum_scatter(operand.astype(jnp.bfloat16), 'row', scatter_dimension=0...  58.2 us
  transfers between devices with their start and end apart: 19, of which 18 were waited for; matrix products, arithmetic and copies ran while one was open for 5% of the time, Pallas kernels for 0%

commit v1 on v0

v1 whole, which is shorter than its diff:
```python
import functools

import jax
import jax.numpy as jnp
from jax import lax
from jax.experimental import pallas as pl
from jax.experimental.pallas import tpu as pltpu
from jax.sharding import PartitionSpec as P

F32, BF16 = jnp.float32, jnp.bfloat16
MESH = pl.DeviceIdType.MESH
DMA = pltpu.SemaphoreType.DMA

MODEL_WIDTH = 2048
HEAD_SIZE = 64
NORM_EPS = 1e-05
ROPE_BASE = 10000000.0
RES_SCALE = 0.22
SCORE_SCALE = 0.015625

NR = 4
BQ = 256
NEG = -1e30


def dot(a, b, dims):
    return lax.dot_general(a, b, (dims, ((), ())), preferred_element_type=F32)


def place():
    group, row, col = lax.axis_index("group"), lax.axis_index("row"), lax.axis_index("col")
    other_core = row + 1 - 2 * lax.rem(row, 2)
    other_x = lax.rem(row + 2, NR)
    both = other_x + 1 - 2 * lax.rem(row, 2)
    return group, row, col, other_core, other_x, both


def greet(devices):
    barrier = pltpu.get_barrier_semaphore()
    for device in devices:
        pl.semaphore_signal(barrier, inc=1, device_id=device, device_id_type=MESH)
    return barrier


def block_at(ref, row, col, shape):
    b0, b1 = shape
    return ref.at[pl.ds(pl.multiple_of(row * b0, b0), b0), pl.ds(pl.multiple_of(col * b1, b1), b1)]


def gather_kernel(n, nz, *refs):
    ins, outs = refs[:n], refs[n : 2 * n]
    local_sem, send_sem, recv_sem = refs[2 * n :]
    g, r, z, rc, rx, rxc = place()
    has_left, has_right = z > 0, z < nz - 1
    barrier = greet([(g, rc, z), (g, rx, z)])

    @pl.when(has_left)
    def _():
        pl.semaphore_signal(barrier, inc=1, device_id=(g, r, z - 1), device_id_type=MESH)

    @pl.when(has_right)
    def _():
        pl.semaphore_signal(barrier, inc=1, device_id=(g, r, z + 1), device_id_type=MESH)

    pl.semaphore_wait(barrier, 2 + has_left.astype(jnp.int32) + has_right.astype(jnp.int32))

    right, left, over_x, to_core = 0, nz - 1, 2 * (nz - 1), 3 * nz - 2

    def slot(i, row, col):
        return block_at(outs[i], row, col, ins[i].shape)

    def copy(i, src, row, col, where, device):
        return pltpu.make_async_remote_copy(
            src_ref=src,
            dst_ref=slot(i, row, col),
            send_sem=send_sem.at[i, where],
            recv_sem=recv_sem.at[i, row, col],
            device_id=device,
            device_id_type=MESH,
        )

    def own(i, where, device):
        return copy(i, ins[i], r, z, where, device)

    def forward(i, row, col, where, device):
        return copy(i, slot(i, row, col), row, col, where, device)

    def rank(col):
        return col - (col > z).astype(jnp.int32)

    def local(i):
        return pltpu.make_async_copy(ins[i], slot(i, r, z), local_sem.at[i])

    for i in range(n):
        local(i).start()

        @pl.when(has_right)
        def _():
            own(i, right, (g, r, z + 1)).start()

        @pl.when(has_left)
        def _():
            own(i, left, (g, r, z - 1)).start()

        own(i, over_x, (g, rx, z)).start()
        own(i, to_core, (g, rc, z)).start()

    def from_x(i, col, where):
        forward(i, rx, col, where, (g, rx, z)).wait_recv()
        forward(i, rx, col, where, (g, rc, z)).start()

    for i in range(n):
        from_x(i, z, to_core + 1)
    for k in range(1, nz):
        for i in range(n):

            @pl.when(z - k >= 0)
            def _():
                col = z - k
                forward(i, r, col, right, (g, rc, z)).wait_recv()
                if k < nz - 1:

                    @pl.when(has_right)
                    def _():
                        forward(i, r, col, right + k, (g, r, z + 1)).start()

                forward(i, r, col, over_x + 1 + rank(col), (g, rx, z)).start()
                forward(i, r, col, to_core + 2 + rank(col), (g, rc, z)).start()

            @pl.when(z + k < nz)
            def _():
                col = z + k
                forward(i, r, col, left, (g, rc, z)).wait_recv()
                if k < nz - 1:

                    @pl.when(has_left)
                    def _():
                        forward(i, r, col, left + k, (g, r, z - 1)).start()

                forward(i, r, col, over_x + 1 + rank(col), (g, rx, z)).start()
                forward(i, r, col, to_core + 2 + rank(col), (g, rc, z)).start()

        for i in range(n):

            @pl.when(z - k >= 0)
            def _():
                from_x(i, z - k, to_core + nz + 1 + z - k)

            @pl.when(z + k < nz)
            def _():
                from_x(i, z + k, to_core + nz + z + k)

    for i in range(n):
        for col in range(nz):
            forward(i, rc, col, to_core, (g, rc, z)).wait_recv()
            forward(i, rxc, col, to_core, (g, rc, z)).wait_recv()
        local(i).wait()
        for where in range(to_core + 2 * nz):

            def sent(where=where):
                own(i, where, (g, rc, z)).wait_send()

            if where < left:
                pl.when(has_right & (z - where >= 0))(sent)
            elif where < over_x:
                pl.when(has_left & (z + (where - left) < nz))(sent)
            else:
                sent()


def gather(arrays, collective_id):
    n, nz = len(arrays), lax.axis_size("col")
    anywhere = pl.BlockSpec(memory_space=pl.ANY)
    return pl.pallas_call(
        functools.partial(gather_kernel, n, nz),
        out_shape=[
            jax.ShapeDtypeStruct((a.shape[0] * NR, a.shape[1] * nz), a.dtype) for a in arrays
        ],
        in_specs=[anywhere] * n,
        out_specs=[anywhere] * n,
        scratch_shapes=[DMA((n,)), DMA((n, 5 * nz - 2)), DMA((n, NR, nz))],
        compiler_params=pltpu.CompilerParams(collective_id=collective_id, has_side_effects=True),
        cost_estimate=pl.CostEstimate(flops=0, bytes_accessed=60 * 2**20, transcendentals=0),
        name="gather",
    )(*arrays)


def in_rows(total, step, body):
    step = min(step, total)
    if total == step:
        body(pl.ds(0, step))
    else:

        def one(i, carry):
            body(pl.ds(pl.multiple_of(i * step, step), step))
            return carry

        lax.fori_loop(0, total // step, one, 0)


def scatter_kernel(n, nz, *refs):
    ins, outs = refs[:n], refs[n : 2 * n]
    bufs = [refs[2 * n + 6 * i : 2 * n + 6 * (i + 1)] for i in range(n)]
    load_sem, core_send, core_recv, x_send, x_recv, z_send, z_recv = refs[8 * n :]
    g, r, z, rc, rx, rxc = place()
    barrier = greet(
        [(g, rc, z), (g, rx, z)] + [(g, r, lax.rem(z + k, nz)) for k in range(1, nz)]
    )
    pl.semaphore_wait(barrier, nz + 1)
    order = [(nz // 2 + k) % nz for k in range(nz // 2)] + list(range(nz // 2 - 1, 0, -1)) + [0]

    def block(i, row, step):
        b0, b1 = ins[i].shape[0] // NR, ins[i].shape[1] // nz
        return block_at(ins[i], row, lax.rem(z + order[step], nz), (b0, b1))

    def load(i, way, step):
        return pltpu.make_async_copy(
            block(i, (rx, r)[way], step), bufs[i][0].at[way, step], load_sem.at[i, way, step]
        )

    def remote(src, dst, send, recv, device):
        return pltpu.make_async_remote_copy(
            src_ref=src,
            dst_ref=dst,
            send_sem=send,
            recv_sem=recv,
            device_id=device,
            device_id_type=MESH,
        )

    def core(i, way, step):
        return remote(
            block(i, (rxc, rc)[way], step),
            bufs[i][1].at[way, step],
            core_send.at[i, way, step],
            core_recv.at[i, way, step],
            (g, rc, z),
        )

    def over_x(i, step):
        return remote(
            bufs[i][2].at[step], bufs[i][3].at[step], x_send.at[i, step], x_recv.at[i, step], (g, rx, z)
        )

    def along_z(i, step):
        return remote(
            bufs[i][4].at[step],
            bufs[i][5].at[step],
            z_send.at[i, step],
            z_recv.at[i, step],
            (g, r, lax.rem(z + order[step], nz)),
        )

    for i in range(n):
        for way in range(2):
            for step in range(nz):
                core(i, way, step).start()
                load(i, way, step).start()
    for i in range(n):
        own, from_core, half, from_x, mine, from_z = bufs[i]
        for step in range(nz):
            load(i, 0, step).wait()
            core(i, 0, step).wait_recv()

            def add(rows):
                half[step, rows, :] = (
                    own[0, step, rows, :].astype(F32) + from_core[0, step, rows, :].astype(F32)
                ).astype(half.dtype)

            in_rows(own.shape[2], 64, add)
            over_x(i, step).start()
    for i in range(n):
        own, from_core, half, from_x, mine, from_z = bufs[i]

        def total(step, rows):
            return (
                own[1, step, rows, :].astype(F32)
                + from_core[1, step, rows, :].astype(F32)
                + from_x[step, rows, :].astype(F32)
            )

        for step in range(nz):
            load(i, 1, step).wait()
            core(i, 1, step).wait_recv()
            over_x(i, step).wait_recv()
            if step < nz - 1:

                def add(rows):
                    mine[step, rows, :] = total(step, rows).astype(mine.dtype)

                in_rows(own.shape[2], 64, add)
                along_z(i, step).start()
    for i in range(n):
        own, from_core, half, from_x, mine, from_z = bufs[i]
        for step in range(nz - 1):
            along_z(i, step).wait_recv()

        def finish(rows):
            result = (
                own[1, nz - 1, rows, :].astype(F32)
                + from_core[1, nz - 1, rows, :].astype(F32)
                + from_x[nz - 1, rows, :].astype(F32)
            )
            for step in range(nz - 1):
                result = result + from_z[step, rows, :].astype(F32)
            outs[i][rows, :] = result

        in_rows(own.shape[2], 64, finish)
    for i in range(n):
        for step in range(nz):
            core(i, 0, step).wait_send()
            core(i, 1, step).wait_send()
            over_x(i, step).wait_send()
            if step < nz - 1:
                along_z(i, step).wait_send()


def reduce_scatter(arrays, collective_id):
    n, nz = len(arrays), lax.axis_size("col")
    scratch = []
    for a in arrays:
        shape = (a.shape[0] // NR, a.shape[1] // nz)
        for lead in ((2, nz), (2, nz), (nz,), (nz,), (nz - 1,), (nz - 1,)):
            scratch.append(pltpu.VMEM(lead + shape, a.dtype))
    scratch += [DMA((n, 2, nz))] * 3 + [DMA((n, nz))] * 4
    return pl.pallas_call(
        functools.partial(scatter_kernel, n, nz),
        out_shape=[
            jax.ShapeDtypeStruct((a.shape[0] // NR, a.shape[1] // nz), F32) for a in arrays
        ],
        in_specs=[pl.BlockSpec(memory_space=pl.ANY)] * n,
        out_specs=[pl.BlockSpec(memory_space=pltpu.VMEM)] * n,
        scratch_shapes=scratch,
        compiler_params=pltpu.CompilerParams(
            collective_id=collective_id, has_side_effects=True, vmem_limit_bytes=48 * 2**20
        ),
        cost_estimate=pl.CostEstimate(flops=0, bytes_accessed=60 * 2**20, transcendentals=0),
        name="reduce_scatter",
    )(*arrays)


def swap64(v):
    parts = []
    for i in range(0, v.shape[1], 128):
        parts += [v[:, i + 64 : i + 128], v[:, i : i + 64]]
    return jnp.concatenate(parts, axis=1)


def lane_in(shape, low, high):
    lane = lax.rem(lax.broadcasted_iota(jnp.int32, shape, 1), 128)
    return (lane >= low) & (lane < high)


def stack_heads(v, half):
    zero = jnp.zeros_like(v)
    return jnp.concatenate(
        [
            jnp.where(lane_in(v.shape, 0, half), v, zero),
            jnp.where(lane_in(v.shape, half, 2 * half), v, zero),
        ],
        axis=0,
    )


def live(first, i, j):
    shape = (BQ, 2 * BQ)
    key = lax.broadcasted_iota(jnp.int32, shape, 0) + j * BQ
    query = lax.rem(lax.broadcasted_iota(jnp.int32, shape, 1), BQ) + i * BQ
    return (key <= query) & (key >= first)


def attend_forward_kernel(low_ref, rot_ref, val_ref, first_ref, out_ref, log_ref, keys_ref):
    i = pl.program_id(0)

    @pl.when(i == 0)
    def _():
        keys_ref[...] = swap64(rot_ref[...])

    query = stack_heads(rot_ref[pl.ds(pl.multiple_of(i * BQ, BQ), BQ), :], 32)
    first = jnp.concatenate([first_ref[0], first_ref[0]], axis=1)

    def step(j, state):
        top, total, acc = state
        rows = pl.ds(pl.multiple_of(j * BQ, BQ), BQ)
        scores = dot(keys_ref[rows, :], query, ((1,), (1,))) * SCORE_SCALE
        scores = jnp.where(live(first, i, j), scores, NEG)
        new_top = jnp.maximum(top, jnp.max(scores, axis=0, keepdims=True))
        weights = jnp.exp(scores - new_top)
        fade = jnp.exp(top - new_top)
        total = total * fade + jnp.sum(weights, axis=0, keepdims=True)
        acc = acc * fade + dot(val_ref[rows, :], weights.astype(BF16), ((0,), (0,)))
        return new_top, total, acc

    state = (
        jnp.full((1, 2 * BQ), NEG, F32),
        jnp.zeros((1, 2 * BQ), F32),
        jnp.zeros((128, 2 * BQ), F32),
    )
    top, total, acc = lax.fori_loop(low_ref[i], i, step, step(i, state))
    acc = (acc / total).T
    out_ref[...] = jnp.where(lane_in((BQ, 128), 0, 64), acc[:BQ], acc[BQ:]).astype(BF16)
    log_ref[0] = top + jnp.log(total)


def attend_backward_kernel(
    low_ref,
    rot_ref,
    val_ref,
    first_ref,
    log_ref,
    out_ref,
    grad_ref,
    grot_ref,
    gval_ref,
    keys_ref,
    gkey_ref,
):
    i, n = pl.program_id(0), pl.num_programs(0)

    @pl.when(i == 0)
    def _():
        keys_ref[...] = swap64(rot_ref[...])
        gkey_ref[...] = jnp.zeros_like(gkey_ref)
        gval_ref[...] = jnp.zeros_like(gval_ref)

    here = pl.ds(pl.multiple_of(i * BQ, BQ), BQ)
    query = stack_heads(rot_ref[here, :], 32)
    grad = grad_ref[...]
    grads = stack_heads(grad, 64)
    first = jnp.concatenate([first_ref[0], first_ref[0]], axis=1)
    log_row = log_ref[0]
    product = (grad.astype(F32) * out_ref[...].astype(F32)).T
    center = jnp.concatenate(
        [
            jnp.sum(product[:64], axis=0, keepdims=True),
            jnp.sum(product[64:], axis=0, keepdims=True),
        ],
        axis=1,
    )

    def step(j, acc):
        rows = pl.ds(pl.multiple_of(j * BQ, BQ), BQ)
        key = keys_ref[rows, :]
        scores = dot(key, query, ((1,), (1,))) * SCORE_SCALE
        weights = jnp.where(live(first, i, j), jnp.exp(scores - log_row), 0.0)
        grad_weights = dot(val_ref[rows, :], grads, ((1,), (1,)))
        grad_scores = (weights * (grad_weights - center)).astype(BF16)
        gval_ref[rows, :] += dot(weights.astype(BF16), grads, ((1,), (0,)))
        gkey_ref[rows, :] += dot(grad_scores, query, ((1,), (0,)))
        return acc + dot(grad_scores, key, ((0,), (0,)))

    acc = lax.fori_loop(low_ref[i], i + 1, step, jnp.zeros((2 * BQ, 256), F32))
    grot_ref[here, :] = jnp.where(lane_in((BQ, 256), 0, 32), acc[:BQ], acc[BQ:]) * SCORE_SCALE

    @pl.when(i == n - 1)
    def _():
        def put(rows):
            moved = swap64(gkey_ref[rows, :] * SCORE_SCALE)
            grot_ref[rows, :] = jnp.where(lane_in((BQ, 256), 0, 64), grot_ref[rows, :], moved)

        in_rows(grot_ref.shape[0], BQ, put)


def attend_forward(low, rot, val, first):
    t = rot.shape[0]
    n = t // BQ
    whole = lambda i, low: (0, 0)
    row = lambda i, low: (i, 0, 0)
    return pl.pallas_call(
        attend_forward_kernel,
        grid_spec=pltpu.PrefetchScalarGridSpec(
            num_scalar_prefetch=1,
            grid=(n,),
            in_specs=[
                pl.BlockSpec((t, 256), whole),
                pl.BlockSpec((t, 128), whole),
                pl.BlockSpec((1, 1, BQ), row),
            ],
            out_specs=[
                pl.BlockSpec((BQ, 128), lambda i, low: (i, 0)),
                pl.BlockSpec((1, 1, 2 * BQ), row),
            ],
            scratch_shapes=[pltpu.VMEM((t, 256), BF16)],
        ),
        out_shape=[
            jax.ShapeDtypeStruct((t, 128), BF16),
            jax.ShapeDtypeStruct((n, 1, 2 * BQ), F32),
        ],
        compiler_params=pltpu.CompilerParams(vmem_limit_bytes=40 * 2**20),
        cost_estimate=pl.CostEstimate(
            flops=12 * 10**9, bytes_accessed=4 * 2**20, transcendentals=4 * 10**6
        ),
        name="attend_forward",
    )(low, rot, val, first)


def attend_backward(low, rot, val, first, log_all, out, grad):
    t = rot.shape[0]
    n = t // BQ
    whole = lambda i, low: (0, 0)
    row = lambda i, low: (i, 0, 0)
    some = lambda i, low: (i, 0)
    return pl.pallas_call(
        attend_backward_kernel,
        grid_spec=pltpu.PrefetchScalarGridSpec(
            num_scalar_prefetch=1,
            grid=(n,),
            in_specs=[
                pl.BlockSpec((t, 256), whole),
                pl.BlockSpec((t, 128), whole),
                pl.BlockSpec((1, 1, BQ), row),
                pl.BlockSpec((1, 1, 2 * BQ), row),
                pl.BlockSpec((BQ, 128), some),
                pl.BlockSpec((BQ, 128), some),
            ],
            out_specs=[pl.BlockSpec((t, 256), whole), pl.BlockSpec((t, 128), whole)],
            scratch_shapes=[pltpu.VMEM((t, 256), BF16), pltpu.VMEM((t, 256), F32)],
        ),
        out_shape=[jax.ShapeDtypeStruct((t, 256), F32), jax.ShapeDtypeStruct((t, 128), F32)],
        compiler_params=pltpu.CompilerParams(vmem_limit_bytes=40 * 2**20),
        cost_estimate=pl.CostEstimate(
            flops=20 * 10**9, bytes_accessed=8 * 2**20, transcendentals=4 * 10**6
        ),
        name="attend_backward",
    )(low, rot, val, first, log_all, out, grad)


def pack_tokens(values):
    rows = values.reshape(-1, 128)
    return jnp.pad(rows, ((0, 8 - rows.shape[0]), (0, 0)))


def pack_all_tokens(values, nz):
    rows = values.reshape(NR, -1, 128)
    rows = jnp.pad(rows, ((0, 0), (0, 8 - rows.shape[1]), (0, 0)))
    return jnp.tile(rows.reshape(NR * 8, 128), (1, nz))


def group_share(operand, axis, parts):
    shape = operand.shape
    groups = lax.axis_size("group")
    width = shape[axis] // parts // groups
    split = operand.reshape(shape[:axis] + (parts, groups, width) + shape[axis + 1 :])
    return lax.dynamic_index_in_dim(split, lax.axis_index("group"), axis + 1, keepdims=False)


def sum_over_group(operand):
    if lax.axis_size("group") == 2:
        other = lax.ppermute(operand, "group", [(0, 1), (1, 0)])
        return operand.astype(F32) + other.astype(F32)
    return lax.psum(operand, "group").astype(F32)


def on_device(
    hidden_in,
    segments,
    attn_gain,
    query_weight,
    key_matrix,
    value_matrix,
    out_weight,
    ffn_gain,
    gate_weight,
    up_weight,
    down_weight,
    cotangent,
):
    row, col = lax.axis_index("row"), lax.axis_index("col")
    nz, groups = lax.axis_size("col"), lax.axis_size("group")
    rows_dev, cols_dev = hidden_in.shape
    tokens = rows_dev * NR
    width = cols_dev * nz
    ffn = gate_weight.shape[1] // nz
    part = ffn // groups

    seg = segments.reshape(-1)
    places = jnp.arange(tokens, dtype=jnp.int32)
    first = jnp.sum((seg[None, :] < seg[:, None]).astype(jnp.int32), axis=1)
    low = first[::BQ] // BQ
    first_rows = first.reshape(-1, 1, BQ)
    offset = (places - first).astype(F32)
    half_width = HEAD_SIZE // 2
    inverse = ROPE_BASE ** (-(2.0 * jnp.arange(half_width, dtype=F32)) / HEAD_SIZE)
    angles = offset[:, None] * inverse[None, :]
    cosine = jnp.tile(jnp.cos(angles), (1, 4))
    sine = jnp.tile(jnp.sin(angles), (1, 4))

    q = query_weight.reshape(cols_dev, nz, 2, 2, half_width)
    kv_of = lambda m: jnp.repeat(m.reshape(cols_dev, 2, HEAD_SIZE), nz // 2, axis=1)
    k = kv_of(key_matrix).reshape(cols_dev, nz, 2, half_width)
    v = kv_of(value_matrix)
    qkv_send = jnp.concatenate(
        [q[:, :, 0, 0], q[:, :, 1, 0], k[:, :, 0], q[:, :, 0, 1], q[:, :, 1, 1], k[:, :, 1], v],
        axis=2,
    ).reshape(cols_dev, nz * 256)
    qkv = lax.all_to_all(qkv_send, "col", 1, 0, tiled=True)
    joint = jnp.concatenate(
        [
            qkv[:, :96],
            qkv[:, 64:96],
            qkv[:, 96:192],
            qkv[:, 160:192],
            qkv[:, 192:],
            qkv[:, 192:],
        ],
        axis=1,
    )
    out_rows = lax.all_to_all(out_weight, "col", 0, 1, tiled=True)
    gate_up_send = jnp.concatenate(
        [group_share(gate_weight, 1, nz), group_share(up_weight, 1, nz)], axis=2
    ).reshape(cols_dev, nz * 2 * part)
    gate_up_part = lax.all_to_all(gate_up_send, "col", 1, 0, tiled=True)
    gate_up = lax.all_gather(gate_up_part, "group", axis=1, tiled=True)
    down_send = group_share(down_weight, 0, nz).reshape(nz * part, cols_dev)
    down_part = lax.all_to_all(down_send, "col", 0, 1, tiled=True)
    down = lax.all_gather(down_part, "group", axis=0, tiled=True)

    def gates(a):
        return a.reshape(-1, groups, 2, part)[:, :, 0].reshape(-1, ffn)

    def ups(a):
        return a.reshape(-1, groups, 2, part)[:, :, 1].reshape(-1, ffn)

    residual = hidden_in.astype(F32)
    grad_top = cotangent.astype(F32)
    grad_ffn = (RES_SCALE * grad_top).astype(BF16)
    x_all, gain_all, grad_ffn_all = gather(
        [hidden_in, jnp.broadcast_to(attn_gain[None, :], (8, cols_dev)), grad_ffn], 0
    )
    wide = x_all.astype(F32)
    scale_one = lax.rsqrt(jnp.mean(wide * wide, axis=1) + NORM_EPS)
    normed_one = (wide * scale_one[:, None] * gain_all[:1]).astype(BF16)

    pre = dot(normed_one, joint, ((1,), (0,)))
    pre_one, pre_two = pre[:, :128], pre[:, 128:256]
    rot = jnp.concatenate(
        [pre_one * cosine - pre_two * sine, pre_two * cosine + pre_one * sine], axis=1
    ).astype(BF16)
    val = pre[:, 256:].astype(BF16)
    heads_out, log_all = attend_forward(low, rot, val, first_rows)
    attn_part = dot(heads_out, out_rows, ((1,), (0,))).astype(BF16)
    (attn_sum,) = reduce_scatter([attn_part], 1)
    resid_mid = residual + RES_SCALE * attn_sum

    squares = jnp.sum(resid_mid * resid_mid, axis=1)
    raw_two, square_all = gather(
        [(resid_mid * ffn_gain[None, :]).astype(BF16), pack_tokens(squares)], 2
    )
    square_sum = jnp.sum(square_all.reshape(NR, 8, nz, 128), axis=2)[:, : rows_dev // 128]
    scale_two = lax.rsqrt(square_sum.reshape(tokens) / width + NORM_EPS)

    both = dot(raw_two, gate_up, ((1,), (0,))) * scale_two[:, None]
    gate_pre, up_pre = gates(both), ups(both)
    gate_sig = jax.nn.sigmoid(gate_pre)
    gate_act = gate_pre * gate_sig
    hidden_act = (gate_act * up_pre).astype(BF16)
    down_part_sum = dot(hidden_act, down, ((1,), (0,))).astype(BF16)
    grad_hidden = dot(grad_ffn_all, down, ((1,), (1,)))
    grad_gate = grad_hidden * up_pre * gate_sig * (1.0 + gate_pre * (1.0 - gate_sig))
    grad_up = grad_hidden * gate_act
    inner_two = jnp.sum(grad_gate * gate_pre + grad_up * up_pre, axis=1)

    def pair(a, b):
        return jnp.stack([a.reshape(tokens, groups, part), b.reshape(tokens, groups, part)], axis=2).reshape(
            tokens, 2 * ffn
        )

    grad_pair = pair(grad_gate.astype(BF16), grad_up.astype(BF16))
    grad_pair_scaled = pair(
        (grad_gate * scale_two[:, None]).astype(BF16), (grad_up * scale_two[:, None]).astype(BF16)
    )
    grad_two_part = dot(grad_pair, gate_up, ((1,), (1,))).astype(BF16)
    down_sum, grad_two, inner_two_sum = reduce_scatter(
        [down_part_sum, grad_two_part, pack_all_tokens(inner_two, nz)], 3
    )
    layer_out = (resid_mid + RES_SCALE * down_sum).astype(BF16)
    scale_two_own = lax.dynamic_slice_in_dim(scale_two, row * rows_dev, rows_dev)[:, None]
    inner_two_own = inner_two_sum[: rows_dev // 128].reshape(rows_dev, 1)
    grad_mid = (
        grad_top
        + scale_two_own * ffn_gain[None, :] * grad_two
        - resid_mid * (scale_two_own * scale_two_own * inner_two_own / width)
    )
    ffn_gain_part = jnp.sum(grad_two * resid_mid * scale_two_own, axis=0)
    grad_attn = (RES_SCALE * grad_mid).astype(BF16)
    (grad_attn_all,) = gather([grad_attn], 4)

    down_grad_part = dot(hidden_act, grad_ffn_all, ((0,), (0,))).astype(BF16)
    down_grad_part = lax.psum_scatter(down_grad_part, "group", scatter_dimension=0, tiled=True)
    down_grad_part = lax.all_to_all(
        down_grad_part.reshape(part, nz, cols_dev), "col", 1, 0, tiled=True
    ).reshape(nz, part, cols_dev)
    down_grad = (
        lax.all_gather(down_grad_part, "group", axis=1, tiled=True)
        .reshape(nz * ffn, cols_dev)
        .astype(F32)
    )
    pair_grad_part = dot(raw_two, grad_pair_scaled, ((0,), (0,))).astype(BF16)
    pair_grad_part = lax.psum_scatter(pair_grad_part, "group", scatter_dimension=1, tiled=True)
    pair_grad_part = lax.all_to_all(pair_grad_part, "col", 0, 1, tiled=True).reshape(
        cols_dev, nz, 2 * part
    )
    pair_grad = lax.all_gather(pair_grad_part, "group", axis=2, tiled=True).reshape(
        cols_dev, nz, groups, 2, part
    )
    gate_grad = pair_grad[:, :, :, 0].reshape(cols_dev, nz * ffn).astype(F32)
    up_grad = pair_grad[:, :, :, 1].reshape(cols_dev, nz * ffn).astype(F32)

    grad_heads = dot(grad_attn_all, out_rows, ((1,), (1,))).astype(BF16)
    out_grad_part = dot(heads_out, grad_attn_all, ((0,), (0,))).astype(BF16)
    out_grad = sum_over_group(
        lax.all_to_all(out_grad_part, "col", 1, 0, tiled=True)
    )
    grad_rot, grad_val = attend_backward(
        low, rot, val, first_rows, log_all, heads_out, grad_heads
    )
    inner_one = jnp.sum(grad_rot * rot.astype(F32), axis=1) + jnp.sum(
        grad_val * val.astype(F32), axis=1
    )
    grot_one, grot_two = grad_rot[:, :128], grad_rot[:, 128:]
    grad_pre = jnp.concatenate(
        [grot_one * cosine + grot_two * sine, grot_two * cosine - grot_one * sine, grad_val], axis=1
    ).astype(BF16)
    grad_one_part = dot(grad_pre, joint, ((1,), (1,))).astype(BF16)
    grad_one, inner_one_sum = reduce_scatter([grad_one_part, pack_all_tokens(inner_one, nz)], 5)
    scale_one_own = lax.dynamic_slice_in_dim(scale_one, row * rows_dev, rows_dev)[:, None]
    inner_one_own = inner_one_sum[: rows_dev // 128].reshape(rows_dev, 1)
    input_grad = (
        grad_mid
        + scale_one_own * attn_gain[None, :] * grad_one
        - residual * (scale_one_own * scale_one_own * inner_one_own / width)
    )
    attn_gain_part = jnp.sum(grad_one * residual * scale_one_own, axis=0)
    attn_gain_grad, ffn_gain_grad = lax.psum((attn_gain_part, ffn_gain_part), ("group", "row"))

    joint_grad = dot(normed_one, grad_pre, ((0,), (0,)))
    qkv_grad = jnp.concatenate(
        [
            joint_grad[:, :64],
            joint_grad[:, 64:96] + joint_grad[:, 96:128],
            joint_grad[:, 128:192],
            joint_grad[:, 192:224] + joint_grad[:, 224:256],
            joint_grad[:, 256:320] + joint_grad[:, 320:],
        ],
        axis=1,
    ).astype(BF16)
    qkv_grad = sum_over_group(
        lax.all_to_all(qkv_grad, "col", 0, 1, tiled=True).reshape(cols_dev, nz * 256)
    ).reshape(cols_dev, nz, 256)
    query_grad = jnp.stack(
        [
            jnp.concatenate([qkv_grad[:, :, :32], qkv_grad[:, :, 96:128]], axis=2),
            jnp.concatenate([qkv_grad[:, :, 32:64], qkv_grad[:, :, 128:160]], axis=2),
        ],
        axis=2,
    ).reshape(cols_dev, nz * 128)

    def kv_grad(a):
        return jnp.sum(a.reshape(cols_dev, 2, nz // 2, HEAD_SIZE), axis=2).reshape(cols_dev, 2 * HEAD_SIZE)

    key_grad = kv_grad(jnp.concatenate([qkv_grad[:, :, 64:96], qkv_grad[:, :, 160:192]], axis=2))
    value_grad = kv_grad(qkv_grad[:, :, 192:])
    return (
        layer_out,
        input_grad,
        attn_gain_grad,
        query_grad,
        key_grad,
        value_grad,
        out_grad,
        ffn_gain_grad,
        gate_grad,
        up_grad,
        down_grad,
    )


def solution(mesh):
    return jax.shard_map(
        on_device,
        mesh=mesh,
        in_specs=(
            P(("group", "row"), "col"),
            P("group", None),
            P("col"),
            P("col", "row"),
            P("col", "row"),
            P("col", "row"),
            P("row", "col"),
            P("col"),
            P("col", "row"),
            P("col", "row"),
            P("row", "col"),
            P(("group", "row"), "col"),
        ),
        out_specs=(
            P(("group", "row"), "col"),
            P(("group", "row"), "col"),
            P("col"),
            P("col", "row"),
            P("col", "row"),
            P("col", "row"),
            P("row", "col"),
            P("col"),
            P("col", "row"),
            P("col", "row"),
            P("row", "col"),
        ),
        check_vma=False,
    )
```

time: 2360 us -> 963 us (0.41)
  waiting for transfers between devices: 1940 us -> 76.4 us
  Pallas kernels: 0 us -> 520 us
  matrix products: 192 us -> 110 us
  local copies, waits for them, and re-layouts: 35.7 us -> 113 us
  starting transfers between devices: 1.58 us -> 48.7 us
  blocking collectives: 61 us -> 14.3 us
  other arithmetic: 96.3 us -> 54.8 us
    reduce_scatter x8 -> x2, waiting for transfers between devices: 1010 us -> 0.01 us  [the longest x1 0.01 us: on_device(): lax.psum_scatter(down_grad_part, 'group', scatter_dimension=0, tiled=True)]
    all_gather x8 -> x4, waiting for transfers between devices: 579 us -> 16.7 us  [the longest x1 16.7 us: on_device(): down = lax.all_gather(down_part, 'group', axis=0, tiled=True)]
    pallas_call x0 -> x8, Pallas kernels: none -> 520 us  [the longest x3 246 us: gather(): pl.pallas_call(functools.partial(gather_kernel, n, nz), out_shape=[jax.Sh...]
    psum x3 -> x0, waiting for transfers between devices: 350 us -> none  [the longest x1 185 us: on_device(): lax.psum(query_grad.astype(jnp.bfloat16), 'group').astype(jnp.float32)]
    dot_general x46 -> x12, matrix products: 192 us -> 110 us  [dot(): return lax.dot_general(a, b, (dims, ((), ())), preferred_element_type=F32)]
    all_to_all x0 -> x8, waiting for transfers between devices: none -> 58.4 us  [the longest x1 31.4 us: on_device(): lax.all_to_all(pair_grad_part, 'col', 0, 1, tiled=True)]
    psum x4 -> x0, blocking collectives: 46.6 us -> none  [feature_sum(): return lax.psum(operand, 'col')]
    all_to_all x0 -> x8, starting transfers between devices: none -> 45 us  [the longest x1 12 us: on_device(): down_part = lax.all_to_all(down_send, 'col', 0, 1, tiled=True)]
  transfers between devices with their start and end apart: 19 -> 16, of which waited for: 18 -> 5; matrix products, arithmetic and copies ran while one was open for 5% -> 21% of each run, Pallas kernels for 0% -> 29%
where the time goes in v1:
time: 963 us; the launch traced here: 952 us
  Pallas kernels  520 us (54%)
  local copies, waits for them, and re-layouts  113 us (12%)
  matrix products  110 us (11%)
  waiting for transfers between devices  76.4 us (8%)
  other arithmetic  54.8 us (6%)
  starting transfers between devices  48.7 us (5%)
  between operations  15.4 us (2%)
  blocking collectives  14.3 us (1%)
    pallas_call x3, Pallas kernels, gather(): pl.pallas_call(functools.partial(gather_kernel, n, nz), out_shape=[jax.Sh...  246 us
    pallas_call x3, Pallas kernels, reduce_scatter(): pl.pallas_call(functools.partial(scatter_kernel, n, nz), out_shape=[jax.S...  245 us
    dot_general x12, matrix products, dot(): return lax.dot_general(a, b, (dims, ((), ())), preferred_element_type=F32)  110 us
    unnamed x111, local copies, waits for them, and re-layouts  33.6 us
    all_to_all x1, waiting for transfers between devices, on_device(): lax.all_to_all(pair_grad_part, 'col', 0, 1, tiled=True)  31.4 us
  transfers between devices with their start and end apart: 16, of which 5 were waited for; matrix products, arithmetic and copies ran while one was open for 21% of the time, Pallas kernels for 29%

profile of v1, /device:TPU:0, one launch (start us, length us, event | category | flops | bytes accessed | tf_op | source)
XLA Modules:
  0.0 952.4 jit_solution(1350943427767066157)
XLA Ops:
  83.1 116.0 %gather.3 = (bf16[2048,2048]{1,0:T(8,128)(2,1)}, f32[32,2048]{1,0:T(8,128)}, bf16[2048,2048]{1,0:T(8,128)(2,1)}) custom-call(bf16[512,512]{1,0:T(8,128)(2,1)} %refs_0_.1, f32[8,512]{1,0:T(8,128)} %broadcast_in_dim.6.refs_1_, bf16[512,512]{1,0:T(8,128)(2,1)} %fusion.16.refs_2_), custom_call_target="tpu_custom_call" | custom-call | bytes 62914560 | tf_op jit(solution)/shard_map/gather/pallas_call | solution.py:174
  208.9 12.0 %all-to-all-start.3 = ((bf16[4,256,512]{1,2,0:T(8,128)(2,1)}), bf16[4,256,512]{1,2,0:T(8,128)(2,1)}, u32[]{:S(2)}, u32[]{:S(2)}) async-start(bf16[4,256,512]{1,2,0:T(8,128)(2,1)} %bitcast.35), calls=%async_computation.3 | async-start | bytes 2097152 | tf_op jit(solution)/shard_map/all_to_all | solution.py:615
  221.8 7.8 fusion.14
  231.6 12.0 %attend_forward.1 = (bf16[2048,128]{1,0:T(8,128)(2,1)S(1)}, f32[8,1,512]{2,1,0:T(1,128)S(1)}) custom-call(s32[8]{0:T(128)S(1)} %and_select_fusion.low_ref, bf16[2048,256]{1,0:T(8,128)(2,1)S(1)} %pad_maximum_fusion.5.rot_ref, bf16[2048,128]{1,0:T(8,128)(2,1)S(1)} %slice.231.val_ref, s32[8,1,256]{2,1,0:T(1,128)S(1)} %bitcast.208), custom_call_target="tpu_custom_call" | custom-call | flops 12000000000 | bytes 4194304 | tf_op jit(solution)/shard_map/attend_forward/pallas_call | solution.py:469
  250.2 65.3 %reduce_scatter.25 = f32[512,512]{1,0:T(8,128)S(1)} custom-call(bf16[2048,2048]{1,0:T(8,128)(2,1)} %convolution_convert_fusion.3.refs_0_), custom_call_target="tpu_custom_call" | custom-call | bytes 62914560 | tf_op jit(solution)/shard_map/reduce_scatter/pallas_call | solution.py:326
  317.1 66.1 %gather.4 = (bf16[2048,2048]{1,0:T(8,128)(2,1)}, f32[32,512]{1,0:T(8,128)}) custom-call(bf16[512,512]{1,0:T(8,128)(2,1)} %get-tuple-element.130.refs_0_, f32[8,128]{1,0:T(8,128)} %pad.11.refs_1_), custom_call_target="tpu_custom_call" | custom-call | bytes 62914560 | tf_op jit(solution)/shard_map/gather/pallas_call | solution.py:174
  384.4 13.1 %convolution_multiply_fusion = f32[2048,1024]{0,1:T(8,128)S(1)} fusion(bf16[2048,2048]{1,0:T(8,128)(2,1)} %get-tuple-element.28, bf16[2048,1024]{1,0:T(8,128)(2,1)} %all-gather.6.cloned.1.call-done, f32[2048]{0:T(1024)S(1)} %bitcast.252), kind=kOutput, calls=%fused_computation.10 | convolution fusion | flops 8592031744 | bytes 20979712 | tf_op jit(solution)/shard_map/dot_general | solution.py:27
  401.6 16.7 %all-gather.8.cloned.1.call-done = bf16[512,2048]{0,1:T(8,128)(2,1)} async-done(((bf16[256,2048]{0,1:T(8,128)(2,1)}), bf16[512,2048]{0,1:T(8,128)(2,1)}) %all-gather.8.cloned.1.call-update) | async-done | bytes 2097168 | tf_op jit(solution)/shard_map/all_gather | solution.py:616
  418.2 14.0 %multiply_convert_fusion.1 = (bf16[2048,512]{0,1:T(8,128)(2,1)S(1)}, f32[2048,512]{0,1:T(8,128)}, bf16[2048,512]{0,1:T(8,128)(2,1)}, bf16[2048,512]{0,1:T(8,128)...) fusion(f32[2048]{0:T(1024)S(1)} %bitcast.253, f32[2048,2,1,256]{0,3,2,1:T(8,128)} %get-tuple-element.107, ...), kind=kOutput, calls=%fused_computation.30 | convolution fusion | flops 4313841664 | bytes 35659776 | tf_op jit(solution)/shard_map/dot_general | solution.py:27
  433.5 9.1 convolution_convert_fusion.5
  445.1 12.6 %convolution_convert_fusion.4 = bf16[2048,1024]{1,0:T(8,128)(2,1)} fusion(bf16[2048,2048]{1,0:T(8,128)(2,1)} %get-tuple-element.28, bf16[2048,1024]{0,1:T(8,128)(2,1)S(1)} %bitcast.222), kind=kOutput, calls=%fused_computation.31 | convolution fusion | flops 8592031744 | bytes 16777216 | tf_op jit(solution)/shard_map/dot_general | solution.py:27
  457.7 8.4 fusion.7
  475.3 11.6 %convolution_convert_fusion.1.refs_1_ = bf16[2048,2048]{1,0:T(8,128)(2,1)} fusion(bf16[2048,1024]{0,1:T(8,128)(2,1)S(1)} %bitcast.221, bf16[2048,1024]{1,0:T(8,128)(2,1)S(1)} %copy-done.43), kind=kOutput, calls=%fused_computation.7 | convolution fusion | flops 8594128896 | bytes 16777216 | tf_op jit(solution)/shard_map/dot_general | solution.py:27
  486.9 112.5 %reduce_scatter.26 = (f32[512,512]{1,0:T(8,128)S(1)}, f32[512,512]{1,0:T(8,128)S(1)}, f32[8,128]{1,0:T(8,128)S(1)}) custom-call(bf16[2048,2048]{1,0:T(8,128)(2,1)} %convolution_convert_fusion.2.refs_0_, bf16[2048,2048]{1,0:T(8,128)(2,1)} %convolution_convert_fusion.1.refs_1_, f32[32,512]{1,0:T(8,128)S(1)} %bitcast.206), custom_call_target="tpu_custom_call" | custom-call | bytes 62914560 | tf_op jit(solution)/shard_map/reduce_scatter/pallas_call | solution.py:326
  602.6 63.5 %gather.5 = bf16[2048,2048]{1,0:T(8,128)(2,1)} custom-call(bf16[512,512]{1,0:T(8,128)(2,1)} %multiply_convert_fusion.2.refs_0_), custom_call_target="tpu_custom_call" | custom-call | bytes 62914560 | tf_op jit(solution)/shard_map/gather/pallas_call | solution.py:174
  683.5 17.2 %attend_backward.1 = (f32[2048,256]{1,0:T(8,128)S(1)}, f32[2048,128]{1,0:T(8,128)S(1)}) custom-call(s32[8]{0:T(128)S(1)} %and_select_fusion.low_ref, bf16[2048,256]{1,0:T(8,128)(2,1)S(1)} %copy-done.7, bf16[2048,128]{1,0:T(8,128)(2,1)S(1)} %copy-done.12, s32[8,1,256]{2,1,0:T(1,128)S(1)} %bitcast.209, f32[8,1,512]{2,1,0:T(1,128)S(1)} %get-tuple-element.34.log_ref, ...), custom_call_target="tpu_custom_call" | custom-call | flops 20000000000 | bytes 8388608 | tf_op jit(solution)/shard_map/attend_backward/pallas_call | solution.py:503
  710.5 7.7 fusion.39
  727.1 31.4 %all-to-all-done.6 = bf16[4,512,512]{2,1,0:T(8,128)(2,1)} async-done(((bf16[4,512,512]{2,1,0:T(8,128)(2,1)}), bf16[4,512,512]{2,1,0:T(8,128)(2,1)}, u32[]{:S(2)}, u32[]{:S(2)}) %all-to-all-start.6) | async-done | bytes 2097184 | tf_op jit(solution)/shard_map/all_to_all | solution.py:700
  769.0 19.0 %all-to-all-done.4 = bf16[4,512,256]{1,2,0:T(8,128)(2,1)} async-done(((bf16[4,512,256]{1,2,0:T(8,128)(2,1)}), bf16[4,512,256]{1,2,0:T(8,128)(2,1)}, u32[]{:S(2)}, u32[]{:S(2)}) %all-to-all-start.4) | async-done | bytes 1048608 | tf_op jit(solution)/shard_map/all_to_all | solution.py:748
  792.2 10.0 %convolution_convert_fusion.refs_0_ = bf16[2048,2048]{1,0:T(8,128)(2,1)} fusion(bf16[2048,128]{1,0:T(8,128)(2,1)} %get-tuple-element.132, bf16[2048,128]{1,0:T(8,128)(2,1)} %get-tuple-element.114, bf16[2048,128]{1,0:T(8,128)(2,1)} %get-tuple-element.113, bf16[2048,64]{1,0:T(8,128)(2,1)} %copy-done.32, bf16[2048,96]{1,0:T(8,128)(2,1)} %get-tuple-element.134, ...), kind=kOutput, calls=%fused_computation.6 | convolution fusion | flops 3236429824 | bytes 11534336 | tf_op jit(solution)/shard_map/dot_general | solution.py:27
  805.2 67.0 %reduce_scatter.27 = (f32[512,512]{1,0:T(8,128)S(1)}, f32[8,128]{1,0:T(8,128)S(1)}) custom-call(bf16[2048,2048]{1,0:T(8,128)(2,1)} %convolution_convert_fusion.refs_0_, f32[32,512]{1,0:T(8,128)S(1)} %bitcast.207), custom_call_target="tpu_custom_call" | custom-call | bytes 62914560 | tf_op jit(solution)/shard_map/reduce_scatter/pallas_call | solution.py:326
  877.4 14.3 %all-reduce.3 = (f32[512]{0:T(512)}, f32[512]{0:T(512)}) all-reduce(f32[512]{0:T(512)S(1)} %get-tuple-element.95, f32[512]{0:T(512)S(1)} %get-tuple-element.94), channel_id=1, replica_groups=mesh['group'=2,'row'=4,'col'=4] {'group','row'}, use_global_device_ids=true, to_apply=%region_8.9 | all-reduce | flops 1024 | bytes 8192 | tf_op jit(solution)/shard_map/psum | solution.py:734
  904.1 7.8 reshape.286
  911.9 9.8 %fusion.35 = (bf16[512,4,2,1,256]{4,3,2,0,1:T(2,128)(2,1)S(1)}, bf16[512,4,2,1,256]{4,3,2,0,1:T(2,128)(2,1)}) fusion(bf16[512,4,2,2,256]{4,3,2,0,1:T(2,128)(2,1)} %reshape.286), kind=kLoop, calls=%fused_computation.123 | loop fusion | bytes 8388608 | tf_op jit(solution)/shard_map/slice | solution.py:707
  (228 shorter events, 212.2 us)
Async XLA Ops:
  7.2 70.0 %copy-start = (bf16[2048,512]{1,0:T(8,128)(2,1)S(1)}, bf16[2048,512]{1,0:T(8,128)(2,1)}, u32[]{:S(2)}) copy-start(bf16[2048,512]{1,0:T(8,128)(2,1)} %param.22) | copy-start | bytes 6291460
  7.2 26.0 %all-to-all-start.1 = ((bf16[4,128,512]{2,1,0:T(8,128)(2,1)}), bf16[4,128,512]{2,1,0:T(8,128)(2,1)}, u32[]{:S(2)}, u32[]{:S(2)}) async-start(bf16[4,128,512]{2,1,0:T(8,128)(2,1)} %bitcast.247), calls=%async_computation.1 | async-start | bytes 1048576 | tf_op jit(solution)/shard_map/all_to_all | solution.py:608
  33.2 30.3 %all-to-all-start = ((bf16[512,4,256]{2,0,1:T(8,128)(2,1)}), bf16[512,4,256]{2,0,1:T(8,128)(2,1)S(1)}, u32[]{:S(2)}, u32[]{:S(2)}) async-start(bf16[512,4,256]{2,0,1:T(8,128)(2,1)} %concatenate.42), calls=%async_computation | async-start | bytes 2097152 | tf_op jit(solution)/shard_map/all_to_all | solution.py:596
  63.5 145.4 %all-to-all-start.2 = ((bf16[512,4,512]{2,0,1:T(8,128)(2,1)}), bf16[512,4,512]{2,0,1:T(8,128)(2,1)}, u32[]{:S(2)}, u32[]{:S(2)}) async-start(bf16[512,4,512]{2,0,1:T(8,128)(2,1)} %pad_maximum_fusion.2), calls=%async_computation.2 | async-start | bytes 4194304 | tf_op jit(solution)/shard_map/all_to_all | solution.py:612
  73.5 156.2 %copy-start.14 = (f32[2048,128]{1,0:T(8,128)}, f32[2048,128]{1,0:T(8,128)S(1)}, u32[]{:S(2)}) copy-start(f32[2048,128]{1,0:T(8,128)S(1)} %copy.216) | copy-start | bytes 3145732
  208.9 175.3 %all-to-all-start.3 = ((bf16[4,256,512]{1,2,0:T(8,128)(2,1)}), bf16[4,256,512]{1,2,0:T(8,128)(2,1)}, u32[]{:S(2)}, u32[]{:S(2)}) async-start(bf16[4,256,512]{1,2,0:T(8,128)(2,1)} %bitcast.35), calls=%async_computation.3 | async-start | bytes 2097152 | tf_op jit(solution)/shard_map/all_to_all | solution.py:615
  220.8 163.6 %all-gather.6.cloned.1.call-start = ((), (), s32[]{:S(2)}) async-start(), calls=%async_computation.10 | async-start | bytes 6291456 | tf_op jit(solution)/shard_map/all_gather | solution.py:613
  221.6 196.7 %all-gather.8.cloned.1.call-start = ((), (), s32[]{:S(2)}) async-start(), calls=%async_computation.11 | async-start | bytes 3145728 | tf_op jit(solution)/shard_map/all_gather | solution.py:616
  384.2 288.5 %reduce-scatter.5.cloned.1.call-start = ((), (), s32[]{:S(2)}) async-start(), calls=%async_computation.14 | async-start | bytes 3145728 | tf_op jit(solution)/shard_map/reduce_scatter | solution.py:689
  442.6 263.1 %reduce-scatter.3.cloned.1.call-start = ((), (), s32[]{:S(2)}) async-start(), calls=%async_computation.12 | async-start | bytes 6291456 | tf_op jit(solution)/shard_map/reduce_scatter | solution.py:699
  486.9 114.5 %copy-start.21 = (bf16[512,512]{1,0:T(8,128)(2,1)S(1)}, bf16[512,512]{1,0:T(8,128)(2,1)}, u32[]{:S(2)}) copy-start(bf16[512,512]{1,0:T(8,128)(2,1)} %refs_0_.1) | copy-start | bytes 1572868
  486.9 114.5 %copy-start.26 = (bf16[512,512]{1,0:T(8,128)(2,1)S(1)}, bf16[512,512]{1,0:T(8,128)(2,1)}, u32[]{:S(2)}) copy-start(bf16[512,512]{1,0:T(8,128)(2,1)} %param.23) | copy-start | bytes 1572868
  674.9 30.9 %all-to-all-start.7 = ((bf16[256,4,512]{2,0,1:T(8,128)(2,1)}), bf16[256,4,512]{2,0,1:T(8,128)(2,1)}, u32[]{:S(2)}, u32[]{:S(2)}) async-start(bf16[256,4,512]{2,0,1:T(8,128)(2,1)} %bitcast.201), calls=%async_computation.9 | async-start | bytes 2097152 | tf_op jit(solution)/shard_map/all_to_all | solution.py:690
  705.8 52.7 %all-to-all-start.6 = ((bf16[4,512,512]{2,1,0:T(8,128)(2,1)}), bf16[4,512,512]{2,1,0:T(8,128)(2,1)}, u32[]{:S(2)}, u32[]{:S(2)}) async-start(bf16[4,512,512]{2,1,0:T(8,128)(2,1)} %bitcast.228), calls=%async_computation.7 | async-start | bytes 4194304 | tf_op jit(solution)/shard_map/all_to_all | solution.py:700
  710.2 189.2 %all-gather.12.cloned.1.call-start = ((), (), s32[]{:S(2)}) async-start(), calls=%async_computation.15 | async-start | bytes 3145728 | tf_op jit(solution)/shard_map/all_gather | solution.py:694
  758.5 29.5 %all-to-all-start.4 = ((bf16[4,512,256]{1,2,0:T(8,128)(2,1)}), bf16[4,512,256]{1,2,0:T(8,128)(2,1)}, u32[]{:S(2)}, u32[]{:S(2)}) async-start(bf16[4,512,256]{1,2,0:T(8,128)(2,1)} %bitcast_dynamic-update-slice_fusion), calls=%async_computation.4 | async-start | bytes 2097152 | tf_op jit(solution)/shard_map/all_to_all | solution.py:748
  762.7 141.4 %all-gather.10.cloned.1.call-start = ((), (), s32[]{:S(2)}) async-start(), calls=%async_computation.13 | async-start | bytes 6291456 | tf_op jit(solution)/shard_map/all_gather | solution.py:703
  788.0 85.2 %all-to-all-start.5 = ((bf16[128,4,512]{2,0,1:T(8,128)(2,1)}), bf16[128,4,512]{2,0,1:T(8,128)(2,1)}, u32[]{:S(2)}, u32[]{:S(2)}) async-start(bf16[128,4,512]{2,0,1:T(8,128)(2,1)} %bitcast.229), calls=%async_computation.5 | async-start | bytes 1048576 | tf_op jit(solution)/shard_map/all_to_all | solution.py:712
  802.2 91.8 %collective-permute-start = (bf16[512,1024]{0,1:T(8,128)(2,1)}, bf16[512,1024]{0,1:T(8,128)(2,1)}, u32[]{:S(2)}, u32[]{:S(2)}) collective-permute-start(bf16[512,1024]{0,1:T(8,128)(2,1)} %bitcast.50), channel_id=1, source_target_pairs={{0,16},{16,0},{1,17},{17,1},{2,18},{18,2},{3,19},{19,3},{4,20},{20... | collective-permute-start | bytes 3145736 | tf_op jit(solution)/shard_map/ppermute | solution.py:549
  805.2 68.8 %copy-start.5 = (f32[512,512]{1,0:T(8,128)S(1)}, f32[512,512]{1,0:T(8,128)}, u32[]{:S(2)}) copy-start(f32[512,512]{1,0:T(8,128)} %copy-done.4) | copy-start | bytes 3145732
  805.2 68.8 %copy-start.9 = (f32[512,512]{1,0:T(8,128)S(1)}, f32[512,512]{1,0:T(8,128)}, u32[]{:S(2)}) copy-start(f32[512,512]{1,0:T(8,128)} %copy-done.8) | copy-start | bytes 3145732
  805.2 68.8 %copy-start.36 = (f32[512]{0:T(512)S(1)}, f32[512]{0:T(512)}, u32[]{:S(2)}) copy-start(f32[512]{0:T(512)} %param.19) | copy-start | bytes 6148
  805.2 68.7 %copy-start.40 = (f32[512]{0:T(512)S(1)}, f32[512]{0:T(512)}, u32[]{:S(2)}) copy-start(f32[512]{0:T(512)} %param.14) | copy-start | bytes 6148
  873.2 18.6 %collective-permute-start.1 = (bf16[512,512]{1,0:T(8,128)(2,1)}, bf16[512,512]{1,0:T(8,128)(2,1)}, u32[]{:S(2)}, u32[]{:S(2)}) collective-permute-start(bf16[512,512]{1,0:T(8,128)(2,1)} %bitcast.62), channel_id=1, source_target_pairs={{0,16},{16,0},{1,17},{17,1},{2,18},{18,2},{3,19},{19,3},{4,20},{20... | collective-permute-start | bytes 1572872 | tf_op jit(solution)/shard_map/ppermute | solution.py:549
  (40 other events, 518.4 us)
Sparse Core Ops, SparseCore 0:
  223.2 57.2 all-gather.5
  384.3 33.9 all-gather.7
  442.8 31.8 reduce-scatter.4
  476.9 54.3 reduce-scatter.2
  723.9 35.0 all-gather.11
  764.8 77.4 all-gather.9

commit v2 on v1

v2 whole, which is shorter than its diff:
```python
import functools

import jax
import jax.numpy as jnp
from jax import lax
from jax.experimental import pallas as pl
from jax.experimental.pallas import tpu as pltpu
from jax.sharding import PartitionSpec as P

F32, BF16 = jnp.float32, jnp.bfloat16
MESH = pl.DeviceIdType.MESH
DMA = pltpu.SemaphoreType.DMA

MODEL_WIDTH = 2048
HEAD_SIZE = 64
NORM_EPS = 1e-05
ROPE_BASE = 10000000.0
RES_SCALE = 0.22
SCORE_SCALE = 0.015625

NR = 4
BQ = 256
NEG = -1e30


def dot(a, b, dims):
    return lax.dot_general(a, b, (dims, ((), ())), preferred_element_type=F32)


def place():
    group, row, col = lax.axis_index("group"), lax.axis_index("row"), lax.axis_index("col")
    other_core = row + 1 - 2 * lax.rem(row, 2)
    other_x = lax.rem(row + 2, NR)
    both = other_x + 1 - 2 * lax.rem(row, 2)
    return group, row, col, other_core, other_x, both


def greet(devices):
    barrier = pltpu.get_barrier_semaphore()
    for device in devices:
        pl.semaphore_signal(barrier, inc=1, device_id=device, device_id_type=MESH)
    return barrier


def block_at(ref, row, col, shape):
    b0, b1 = shape
    return ref.at[pl.ds(pl.multiple_of(row * b0, b0), b0), pl.ds(pl.multiple_of(col * b1, b1), b1)]


class Spread:
    def __init__(self, arrays, pieces, outs, mode):
        self.arrays, self.pieces, self.mode = list(arrays), pieces, mode
        self.base = [jax.ShapeDtypeStruct(o, arrays[0].dtype) for o in outs]
        self.outs = self.base + (self.base if mode == "twin" else [])
        n, nz = len(pieces), lax.axis_size("col")
        self.scratch = [DMA((n, 2))] + [DMA((n, nz))] * (2 if mode == "plain" else 4)

    def bind(self, ins, outs, sems):
        self.i, self.o, self.sems = ins, outs, sems
        self.g, self.r, self.z = place()[:3]

    def src(self, n, col, half):
        which, src, _, _ = self.pieces[n]
        return self.i[which].at[src(col, half)]

    def dst(self, n, col, half, twin=False):
        _, _, which, dst = self.pieces[n]
        return self.o[which + (len(self.base) if twin else 0)].at[dst(col, half)]

    def half(self):
        return self.g if self.mode in ("share", "sum") else 0

    def send(self, n, col):
        return pltpu.make_async_remote_copy(
            src_ref=self.src(n, col, self.half()),
            dst_ref=self.dst(n, self.z, self.half()),
            send_sem=self.sems[1].at[n, col],
            recv_sem=self.sems[2].at[n, self.z],
            device_id=(self.g, self.r, col),
            device_id_type=MESH,
        )

    def arrived(self, n, col):
        return pltpu.make_async_remote_copy(
            src_ref=self.src(n, col, self.half()),
            dst_ref=self.dst(n, col, self.half()),
            send_sem=self.sems[1].at[n, col],
            recv_sem=self.sems[2].at[n, col],
            device_id=(self.g, self.r, col),
            device_id_type=MESH,
        )

    def cross(self, n, col, own=False):
        src = self.src(n, self.z, self.half()) if own else self.dst(n, col, self.half())
        return pltpu.make_async_remote_copy(
            src_ref=src,
            dst_ref=self.dst(n, col, self.half(), self.mode == "twin"),
            send_sem=self.sems[3].at[n, col],
            recv_sem=self.sems[4].at[n, col],
            device_id=(1 - self.g, self.r, self.z),
            device_id_type=MESH,
        )

    def crossed(self, n, col):
        half = 1 - self.g if self.mode in ("share", "sum") else 0
        place_there = self.dst(n, col, half, self.mode == "twin")
        return pltpu.make_async_remote_copy(
            src_ref=place_there,
            dst_ref=place_there,
            send_sem=self.sems[3].at[n, col],
            recv_sem=self.sems[4].at[n, col],
            device_id=(1 - self.g, self.r, self.z),
            device_id_type=MESH,
        )

    def local(self, n):
        halves = (0, 1) if self.mode == "share" else (self.half(),)
        return [
            pltpu.make_async_copy(
                self.src(n, self.z, h), self.dst(n, self.z, h), self.sems[0].at[n, m]
            )
            for m, h in enumerate(halves)
        ]

    def start(self, nz):
        for k in range(1, nz):
            for n in range(len(self.pieces)):
                self.send(n, lax.rem(self.z + k, nz)).start()
        for n in range(len(self.pieces)):
            for copy in self.local(n):
                copy.start()
            if self.mode in ("sum", "twin"):
                self.cross(n, self.z, own=True).start()

    def step(self, k, nz):
        for n in range(len(self.pieces)):
            for near, col in ((self.z - k >= 0, self.z - k), (self.z + k < nz, self.z + k)):

                @pl.when(near)
                def _():
                    self.arrived(n, col).wait_recv()
                    if self.mode != "plain":
                        self.cross(n, col).start()

    def finish(self, nz):
        for n in range(len(self.pieces)):
            for copy in self.local(n):
                copy.wait()
            for k in range(1, nz):
                col = lax.rem(self.z + k, nz)
                self.send(n, col).wait_send()
                if self.mode != "plain":
                    self.crossed(n, col).wait_recv()
                    self.crossed(n, col).wait_send()
            if self.mode in ("sum", "twin"):
                self.crossed(n, self.z).wait_recv()
                self.cross(n, self.z, own=True).wait_send()


class Swap:
    def __init__(self, array, pieces, out):
        self.arrays, self.pieces = [array], pieces
        self.outs = [jax.ShapeDtypeStruct(out, array.dtype)]
        self.scratch = [DMA((len(pieces),))] * 2

    def bind(self, ins, outs, sems):
        self.i, self.o, self.sems = ins[0], outs[0], sems
        self.g, self.r, self.z = place()[:3]

    def copy(self, n):
        src, dst = self.pieces[n]
        return pltpu.make_async_remote_copy(
            src_ref=self.i.at[src(1 - self.g)],
            dst_ref=self.o.at[dst],
            send_sem=self.sems[0].at[n],
            recv_sem=self.sems[1].at[n],
            device_id=(1 - self.g, self.r, self.z),
            device_id_type=MESH,
        )

    def start(self, nz):
        for n in range(len(self.pieces)):
            self.copy(n).start()

    def step(self, k, nz):
        pass

    def finish(self, nz):
        for n in range(len(self.pieces)):
            self.copy(n).wait()


def bind_extras(extras, ins, outs, sems):
    for extra in extras:
        n, m, k = len(extra.arrays), len(extra.outs), len(extra.scratch)
        extra.bind(ins[:n], outs[:m], sems[:k])
        ins, outs, sems = ins[n:], outs[m:], sems[k:]


def greetings(extras, nz, devices):
    g, r, z = place()[:3]
    if any(isinstance(extra, Spread) for extra in extras):
        devices = devices[:2] + [(g, r, lax.rem(z + k, nz)) for k in range(1, nz)]
    if any(isinstance(extra, Swap) or extra.mode != "plain" for extra in extras):
        devices = devices + [(1 - g, r, z)]
    return devices


def gather_kernel(n, nz, units, extras, *refs):
    n_in, n_out = n + sum(len(e.arrays) for e in extras), n + sum(len(e.outs) for e in extras)
    ins, outs, sems = refs[:n], refs[n_in : n_in + n], refs[n_in + n_out :]
    local_sem, send_sem, recv_sem = sems[:3]
    bind_extras(extras, refs[n:n_in], refs[n_in + n : n_in + n_out], sems[3:])
    g, r, z, rc, rx, rxc = place()
    has_left, has_right = z > 0, z < nz - 1
    if any(isinstance(extra, Spread) for extra in extras):
        devices = greetings(extras, nz, [(g, rc, z), (g, rx, z)])
        barrier = greet(devices)
        pl.semaphore_wait(barrier, len(devices))
    else:
        devices = greetings(extras, nz, [(g, rc, z), (g, rx, z)])
        barrier = greet(devices)

        @pl.when(has_left)
        def _():
            pl.semaphore_signal(barrier, inc=1, device_id=(g, r, z - 1), device_id_type=MESH)

        @pl.when(has_right)
        def _():
            pl.semaphore_signal(barrier, inc=1, device_id=(g, r, z + 1), device_id_type=MESH)

        count = has_left.astype(jnp.int32) + has_right.astype(jnp.int32)
        pl.semaphore_wait(barrier, len(devices) + count)

    right, left, over_x, to_core = 0, nz - 1, 2 * (nz - 1), 3 * nz - 2

    def own_part(u):
        i, start, size = units[u]
        return ins[i].at[pl.ds(start, size), :]

    def slot(u, row, col):
        i, start, size = units[u]
        b0, b1 = ins[i].shape
        return outs[i].at[
            pl.ds(pl.multiple_of(row * b0 + start, size), size),
            pl.ds(pl.multiple_of(col * b1, b1), b1),
        ]

    def copy(u, src, row, col, where, device):
        return pltpu.make_async_remote_copy(
            src_ref=src,
            dst_ref=slot(u, row, col),
            send_sem=send_sem.at[u, where],
            recv_sem=recv_sem.at[u, row, col],
            device_id=device,
            device_id_type=MESH,
        )

    def own(u, where, device):
        return copy(u, own_part(u), r, z, where, device)

    def forward(u, row, col, where, device):
        return copy(u, slot(u, row, col), row, col, where, device)

    def rank(col):
        return col - (col > z).astype(jnp.int32)

    def local(u):
        return pltpu.make_async_copy(own_part(u), slot(u, r, z), local_sem.at[u])

    every = range(len(units))
    for u in every:

        @pl.when(has_right)
        def _():
            own(u, right, (g, r, z + 1)).start()

        @pl.when(has_left)
        def _():
            own(u, left, (g, r, z - 1)).start()

        own(u, over_x, (g, rx, z)).start()
    for u in every:
        own(u, to_core, (g, rc, z)).start()
        local(u).start()
    for extra in extras:
        extra.start(nz)

    def from_x(u, k):
        for near, col, where in (
            (z - k >= 0, z - k, to_core + 1 if k == 0 else to_core + nz + 1 + z - k),
            (z + k < nz, z + k, to_core + nz + z + k),
        )[: 1 if k == 0 else 2]:

            @pl.when(near)
            def _():
                forward(u, rx, col, where, (g, rx, z)).wait_recv()
                forward(u, rx, col, where, (g, rc, z)).start()

    def from_z(u, k):
        for near, more, col, device, flow in (
            (z - k >= 0, has_right, z - k, (g, r, z + 1), right),
            (z + k < nz, has_left, z + k, (g, r, z - 1), left),
        ):

            @pl.when(near)
            def _():
                forward(u, r, col, flow, (g, rc, z)).wait_recv()
                if k < nz - 1:

                    @pl.when(more)
                    def _():
                        forward(u, r, col, flow + k, device).start()

                forward(u, r, col, over_x + 1 + rank(col), (g, rx, z)).start()
                forward(u, r, col, to_core + 2 + rank(col), (g, rc, z)).start()

    for k in range(1, nz):
        for u in every:
            from_z(u, k)
            from_x(u, k - 1)
        if k > 1:
            for extra in extras:
                extra.step(k - 1, nz)
    for u in every:
        from_x(u, nz - 1)
    for extra in extras:
        extra.step(nz - 1, nz)

    for u in every:
        for col in range(nz):
            forward(u, rc, col, to_core, (g, rc, z)).wait_recv()
            forward(u, rxc, col, to_core, (g, rc, z)).wait_recv()
        local(u).wait()
        for where in range(to_core + 2 * nz):

            def sent(where=where):
                own(u, where, (g, rc, z)).wait_send()

            if where < left:
                pl.when(has_right & (z - where >= 0))(sent)
            elif where < over_x:
                pl.when(has_left & (z + (where - left) < nz))(sent)
            else:
                sent()
    for extra in extras:
        extra.finish(nz)


def flat(lists):
    return [item for some in lists for item in some]


def gather(arrays, collective_id, extras=()):
    n, nz = len(arrays), lax.axis_size("col")
    units = []
    for i, a in enumerate(arrays):
        parts = 2 if a.shape[0] % 256 == 0 else 1
        units += [(i, m * (a.shape[0] // parts), a.shape[0] // parts) for m in range(parts)]
    anywhere = pl.BlockSpec(memory_space=pl.ANY)
    extra_in, extra_out = flat(e.arrays for e in extras), flat(e.outs for e in extras)
    outs = pl.pallas_call(
        functools.partial(gather_kernel, n, nz, units, extras),
        out_shape=[
            jax.ShapeDtypeStruct((a.shape[0] * NR, a.shape[1] * nz), a.dtype) for a in arrays
        ]
        + extra_out,
        in_specs=[anywhere] * (n + len(extra_in)),
        out_specs=[anywhere] * (n + len(extra_out)),
        scratch_shapes=[DMA((len(units),)), DMA((len(units), 5 * nz - 2)), DMA((len(units), NR, nz))]
        + flat(e.scratch for e in extras),
        compiler_params=pltpu.CompilerParams(collective_id=collective_id, has_side_effects=True),
        cost_estimate=pl.CostEstimate(flops=0, bytes_accessed=60 * 2**20, transcendentals=0),
        name="gather",
    )(*arrays, *extra_in)
    return outs[:n], outs[n:]


def in_rows(total, step, body):
    step = min(step, total)
    if total == step:
        body(pl.ds(0, step))
    else:

        def one(i, carry):
            body(pl.ds(pl.multiple_of(i * step, step), step))
            return carry

        lax.fori_loop(0, total // step, one, 0)


def scatter_kernel(n, nz, extras, *refs):
    n_in, n_out = n + sum(len(e.arrays) for e in extras), n + sum(len(e.outs) for e in extras)
    ins, outs, rest = refs[:n], refs[n_in : n_in + n], refs[n_in + n_out :]
    bufs = [rest[6 * i : 6 * (i + 1)] for i in range(n)]
    load_sem, core_send, core_recv, x_send, x_recv, z_send, z_recv = rest[6 * n : 6 * n + 7]
    bind_extras(extras, refs[n:n_in], refs[n_in + n : n_in + n_out], rest[6 * n + 7 :])
    g, r, z, rc, rx, rxc = place()
    pair = z + 1 - 2 * lax.rem(z, 2)
    far, far_pair = lax.rem(z + 2, nz), lax.rem(pair + 2, nz)
    devices = greetings(extras, nz, [(g, rc, z), (g, rx, z), (g, r, pair), (g, r, far)])
    barrier = greet(devices)
    pl.semaphore_wait(barrier, len(devices))
    order = (far_pair, pair, far, z)
    steps = range(len(order))

    def block(i, row, step):
        b0, b1 = ins[i].shape[0] // NR, ins[i].shape[1] // nz
        return block_at(ins[i], row, order[step], (b0, b1))

    def load(i, way, step):
        return pltpu.make_async_copy(
            block(i, (rx, r)[way], step), bufs[i][0].at[way, step], load_sem.at[i, way, step]
        )

    def remote(src, dst, send, recv, device):
        return pltpu.make_async_remote_copy(
            src_ref=src,
            dst_ref=dst,
            send_sem=send,
            recv_sem=recv,
            device_id=device,
            device_id_type=MESH,
        )

    def core(i, way, step):
        return remote(
            block(i, (rxc, rc)[way], step),
            bufs[i][1].at[way, step],
            core_send.at[i, way, step],
            core_recv.at[i, way, step],
            (g, rc, z),
        )

    def over_x(i, step):
        return remote(
            bufs[i][2].at[step], bufs[i][3].at[step], x_send.at[i, step], x_recv.at[i, step], (g, rx, z)
        )

    def along_z(i, step):
        return remote(
            bufs[i][4].at[step],
            bufs[i][5].at[step],
            z_send.at[i, step],
            z_recv.at[i, step],
            (g, r, far if step == 2 else pair),
        )

    for i in range(n):
        for way in range(2):
            for step in steps:
                core(i, way, step).start()
                load(i, way, step).start()
    for i in range(n):
        own, from_core, half, from_x, mine, from_z = bufs[i]
        for step in steps:
            load(i, 0, step).wait()
            core(i, 0, step).wait_recv()

            def add(rows):
                half[step, rows, :] = (
                    own[0, step, rows, :].astype(F32) + from_core[0, step, rows, :].astype(F32)
                ).astype(half.dtype)

            in_rows(own.shape[2], 64, add)
            over_x(i, step).start()
        if i == 0:
            for extra in extras:
                extra.start(nz)
    for i in range(n):
        own, from_core, half, from_x, mine, from_z = bufs[i]

        def total(step, rows):
            result = (
                own[1, step, rows, :].astype(F32)
                + from_core[1, step, rows, :].astype(F32)
                + from_x[step, rows, :].astype(F32)
            )
            if step == 2:
                result = result + from_z[0, rows, :].astype(F32)
            if step == 3:
                result = result + from_z[1, rows, :].astype(F32) + from_z[2, rows, :].astype(F32)
            return result

        for step in steps:
            load(i, 1, step).wait()
            core(i, 1, step).wait_recv()
            over_x(i, step).wait_recv()
            if step == 2:
                along_z(i, 0).wait_recv()
            if step == 3:
                along_z(i, 1).wait_recv()
                along_z(i, 2).wait_recv()

            def add(rows):
                if step == 3:
                    outs[i][rows, :] = total(step, rows)
                else:
                    mine[step, rows, :] = total(step, rows).astype(mine.dtype)

            in_rows(own.shape[2], 64, add)
            if step < 3:
                along_z(i, step).start()
            if i == 0 and 1 <= step:
                for extra in extras:
                    extra.step(step, nz)
    for i in range(n):
        for step in steps:
            core(i, 0, step).wait_send()
            core(i, 1, step).wait_send()
            over_x(i, step).wait_send()
            if step < 3:
                along_z(i, step).wait_send()
    for extra in extras:
        extra.finish(nz)


def reduce_scatter(arrays, collective_id, extras=()):
    n, nz = len(arrays), lax.axis_size("col")
    scratch = []
    for a in arrays:
        shape = (a.shape[0] // NR, a.shape[1] // nz)
        for lead in ((2, nz), (2, nz), (nz,), (nz,), (nz - 1,), (nz - 1,)):
            scratch.append(pltpu.VMEM(lead + shape, a.dtype))
    scratch += [DMA((n, 2, nz))] * 3 + [DMA((n, nz))] * 4
    anywhere = pl.BlockSpec(memory_space=pl.ANY)
    extra_in, extra_out = flat(e.arrays for e in extras), flat(e.outs for e in extras)
    outs = pl.pallas_call(
        functools.partial(scatter_kernel, n, nz, extras),
        out_shape=[
            jax.ShapeDtypeStruct((a.shape[0] // NR, a.shape[1] // nz), F32) for a in arrays
        ]
        + extra_out,
        in_specs=[anywhere] * (n + len(extra_in)),
        out_specs=[pl.BlockSpec(memory_space=pltpu.VMEM)] * n + [anywhere] * len(extra_out),
        scratch_shapes=scratch + flat(e.scratch for e in extras),
        compiler_params=pltpu.CompilerParams(
            collective_id=collective_id, has_side_effects=True, vmem_limit_bytes=48 * 2**20
        ),
        cost_estimate=pl.CostEstimate(flops=0, bytes_accessed=60 * 2**20, transcendentals=0),
        name="reduce_scatter",
    )(*arrays, *extra_in)
    return outs[:n], outs[n:]


def swap64(v):
    parts = []
    for i in range(0, v.shape[1], 128):
        parts += [v[:, i + 64 : i + 128], v[:, i : i + 64]]
    return jnp.concatenate(parts, axis=1)


def lane_in(shape, low, high):
    lane = lax.rem(lax.broadcasted_iota(jnp.int32, shape, 1), 128)
    return (lane >= low) & (lane < high)


def stack_heads(v, half):
    zero = jnp.zeros_like(v)
    return jnp.concatenate(
        [
            jnp.where(lane_in(v.shape, 0, half), v, zero),
            jnp.where(lane_in(v.shape, half, 2 * half), v, zero),
        ],
        axis=0,
    )


def live(first, i, j):
    shape = (BQ, 2 * BQ)
    key = lax.broadcasted_iota(jnp.int32, shape, 0) + j * BQ
    query = lax.rem(lax.broadcasted_iota(jnp.int32, shape, 1), BQ) + i * BQ
    return (key <= query) & (key >= first)


def attend_forward_kernel(low_ref, rot_ref, val_ref, first_ref, out_ref, log_ref, keys_ref):
    i = pl.program_id(0)

    @pl.when(i == 0)
    def _():
        keys_ref[...] = swap64(rot_ref[...])

    query = stack_heads(rot_ref[pl.ds(pl.multiple_of(i * BQ, BQ), BQ), :], 32)
    first = jnp.concatenate([first_ref[0], first_ref[0]], axis=1)

    def step(j, state):
        top, total, acc = state
        rows = pl.ds(pl.multiple_of(j * BQ, BQ), BQ)
        scores = dot(keys_ref[rows, :], query, ((1,), (1,))) * SCORE_SCALE
        scores = jnp.where(live(first, i, j), scores, NEG)
        new_top = jnp.maximum(top, jnp.max(scores, axis=0, keepdims=True))
        weights = jnp.exp(scores - new_top)
        fade = jnp.exp(top - new_top)
        total = total * fade + jnp.sum(weights, axis=0, keepdims=True)
        acc = acc * fade + dot(val_ref[rows, :], weights.astype(BF16), ((0,), (0,)))
        return new_top, total, acc

    state = (
        jnp.full((1, 2 * BQ), NEG, F32),
        jnp.zeros((1, 2 * BQ), F32),
        jnp.zeros((128, 2 * BQ), F32),
    )
    top, total, acc = lax.fori_loop(low_ref[i], i, step, step(i, state))
    acc = (acc / total).T
    out_ref[...] = jnp.where(lane_in((BQ, 128), 0, 64), acc[:BQ], acc[BQ:]).astype(BF16)
    log_ref[0] = top + jnp.log(total)


def attend_backward_kernel(
    low_ref,
    rot_ref,
    val_ref,
    first_ref,
    log_ref,
    out_ref,
    grad_ref,
    grot_ref,
    gval_ref,
    keys_ref,
    gkey_ref,
):
    i, n = pl.program_id(0), pl.num_programs(0)

    @pl.when(i == 0)
    def _():
        keys_ref[...] = swap64(rot_ref[...])
        gkey_ref[...] = jnp.zeros_like(gkey_ref)
        gval_ref[...] = jnp.zeros_like(gval_ref)

    here = pl.ds(pl.multiple_of(i * BQ, BQ), BQ)
    query = stack_heads(rot_ref[here, :], 32)
    grad = grad_ref[...]
    grads = stack_heads(grad, 64)
    first = jnp.concatenate([first_ref[0], first_ref[0]], axis=1)
    log_row = log_ref[0]
    product = (grad.astype(F32) * out_ref[...].astype(F32)).T
    center = jnp.concatenate(
        [
            jnp.sum(product[:64], axis=0, keepdims=True),
            jnp.sum(product[64:], axis=0, keepdims=True),
        ],
        axis=1,
    )

    def step(j, acc):
        rows = pl.ds(pl.multiple_of(j * BQ, BQ), BQ)
        key = keys_ref[rows, :]
        scores = dot(key, query, ((1,), (1,))) * SCORE_SCALE
        weights = jnp.where(live(first, i, j), jnp.exp(scores - log_row), 0.0)
        grad_weights = dot(val_ref[rows, :], grads, ((1,), (1,)))
        grad_scores = (weights * (grad_weights - center)).astype(BF16)
        gval_ref[rows, :] += dot(weights.astype(BF16), grads, ((1,), (0,)))
        gkey_ref[rows, :] += dot(grad_scores, query, ((1,), (0,)))
        return acc + dot(grad_scores, key, ((0,), (0,)))

    acc = lax.fori_loop(low_ref[i], i + 1, step, jnp.zeros((2 * BQ, 256), F32))
    grot_ref[here, :] = jnp.where(lane_in((BQ, 256), 0, 32), acc[:BQ], acc[BQ:]) * SCORE_SCALE

    @pl.when(i == n - 1)
    def _():
        def put(rows):
            moved = swap64(gkey_ref[rows, :] * SCORE_SCALE)
            grot_ref[rows, :] = jnp.where(lane_in((BQ, 256), 0, 64), grot_ref[rows, :], moved)

        in_rows(grot_ref.shape[0], BQ, put)


def attend_forward(low, rot, val, first):
    t = rot.shape[0]
    n = t // BQ
    whole = lambda i, low: (0, 0)
    row = lambda i, low: (i, 0, 0)
    return pl.pallas_call(
        attend_forward_kernel,
        grid_spec=pltpu.PrefetchScalarGridSpec(
            num_scalar_prefetch=1,
            grid=(n,),
            in_specs=[
                pl.BlockSpec((t, 256), whole),
                pl.BlockSpec((t, 128), whole),
                pl.BlockSpec((1, 1, BQ), row),
            ],
            out_specs=[
                pl.BlockSpec((BQ, 128), lambda i, low: (i, 0)),
                pl.BlockSpec((1, 1, 2 * BQ), row),
            ],
            scratch_shapes=[pltpu.VMEM((t, 256), BF16)],
        ),
        out_shape=[
            jax.ShapeDtypeStruct((t, 128), BF16),
            jax.ShapeDtypeStruct((n, 1, 2 * BQ), F32),
        ],
        compiler_params=pltpu.CompilerParams(vmem_limit_bytes=40 * 2**20),
        cost_estimate=pl.CostEstimate(
            flops=12 * 10**9, bytes_accessed=4 * 2**20, transcendentals=4 * 10**6
        ),
        name="attend_forward",
    )(low, rot, val, first)


def attend_backward(low, rot, val, first, log_all, out, grad):
    t = rot.shape[0]
    n = t // BQ
    whole = lambda i, low: (0, 0)
    row = lambda i, low: (i, 0, 0)
    some = lambda i, low: (i, 0)
    return pl.pallas_call(
        attend_backward_kernel,
        grid_spec=pltpu.PrefetchScalarGridSpec(
            num_scalar_prefetch=1,
            grid=(n,),
            in_specs=[
                pl.BlockSpec((t, 256), whole),
                pl.BlockSpec((t, 128), whole),
                pl.BlockSpec((1, 1, BQ), row),
                pl.BlockSpec((1, 1, 2 * BQ), row),
                pl.BlockSpec((BQ, 128), some),
                pl.BlockSpec((BQ, 128), some),
            ],
            out_specs=[pl.BlockSpec((t, 256), whole), pl.BlockSpec((t, 128), whole)],
            scratch_shapes=[pltpu.VMEM((t, 256), BF16), pltpu.VMEM((t, 256), F32)],
        ),
        out_shape=[jax.ShapeDtypeStruct((t, 256), F32), jax.ShapeDtypeStruct((t, 128), F32)],
        compiler_params=pltpu.CompilerParams(vmem_limit_bytes=40 * 2**20),
        cost_estimate=pl.CostEstimate(
            flops=20 * 10**9, bytes_accessed=8 * 2**20, transcendentals=4 * 10**6
        ),
        name="attend_backward",
    )(low, rot, val, first, log_all, out, grad)


def pack(values, rows=8):
    lines = values.reshape(-1, 128)
    return jnp.pad(lines, ((0, rows - lines.shape[0]), (0, 0)))


def by_row(values):
    return values.reshape(NR, -1, 128)


def by_col(values, nz):
    return values.reshape(nz, -1, 128)


def sum_over_group(operand):
    if lax.axis_size("group") == 2:
        other = lax.ppermute(operand, "group", [(0, 1), (1, 0)])
        return operand.astype(F32) + other.astype(F32)
    return lax.psum(operand, "group").astype(F32)


def at(start, size):
    return pl.ds(pl.multiple_of(start, size), size)


def on_device(
    hidden_in,
    segments,
    attn_gain,
    query_weight,
    key_matrix,
    value_matrix,
    out_weight,
    ffn_gain,
    gate_weight,
    up_weight,
    down_weight,
    cotangent,
):
    row, col = lax.axis_index("row"), lax.axis_index("col")
    nz, groups = lax.axis_size("col"), lax.axis_size("group")
    two = groups == 2
    share = "share" if two else "plain"
    parts = 2 if two else 1
    rows_dev, cols_dev = hidden_in.shape
    tokens = rows_dev * NR
    width = cols_dev * nz
    ffn = gate_weight.shape[1] // nz
    ffn_part = ffn // parts
    depth = cols_dev // parts
    heads = query_weight.shape[1] // nz
    head_part = heads // parts
    every = slice(None)

    seg = segments.reshape(-1)
    numbers = jnp.arange(8, dtype=jnp.int32)
    sizes = jnp.sum((seg[None, :] == numbers[:, None]).astype(jnp.int32), axis=1)
    first = jnp.sum(jnp.where(numbers[:, None] < seg[None, :], sizes[:, None], 0), axis=0)
    places = jnp.arange(tokens, dtype=jnp.int32)
    low = first[::BQ] // BQ
    first_rows = first.reshape(-1, 1, BQ)
    offset = (places - first).astype(F32)
    half_width = HEAD_SIZE // 2
    inverse = ROPE_BASE ** (-(2.0 * jnp.arange(half_width, dtype=F32)) / HEAD_SIZE)
    angles = offset[:, None] * inverse[None, :]
    cosine = jnp.tile(jnp.cos(angles), (1, 4))
    sine = jnp.tile(jnp.sin(angles), (1, 4))

    names = jnp.arange(4 * HEAD_SIZE).reshape(4, 2, half_width)
    order = jnp.concatenate(
        [names[(0, 1, 2, 2), 0].reshape(-1), names[(0, 1, 2, 2), 1].reshape(-1)]
        + [names[3].reshape(-1)] * 2
    )
    permutation = (jnp.arange(4 * HEAD_SIZE)[:, None] == order[None, :]).astype(BF16)

    residual = hidden_in.astype(F32)
    grad_top = cotangent.astype(F32)
    grad_ffn = (RES_SCALE * grad_top).astype(BF16)
    joint_kv = jnp.concatenate(
        [
            key_matrix[:, :HEAD_SIZE],
            value_matrix[:, :HEAD_SIZE],
            key_matrix[:, HEAD_SIZE:],
            value_matrix[:, HEAD_SIZE:],
        ],
        axis=1,
    )
    kv = 2 * HEAD_SIZE
    spread_heads = Spread(
        [query_weight, joint_kv],
        [
            (
                0,
                lambda c, h: (at(h * depth, depth), at(c * heads, heads)),
                0,
                lambda c, h: (at(c * cols_dev + h * depth, depth), pl.ds(0, heads)),
            ),
            (
                1,
                lambda c, h: (at(h * depth, depth), at(c * 2 // nz * kv, kv)),
                0,
                lambda c, h: (at(c * cols_dev + h * depth, depth), pl.ds(heads, kv)),
            ),
        ],
        [(width, heads + kv)],
        share,
    )
    spread_out = Spread(
        [out_weight],
        [
            (
                0,
                lambda c, h: (at(c * heads + h * head_part, head_part), every),
                0,
                lambda c, h: (at(h * head_part, head_part), at(c * cols_dev, cols_dev)),
            )
        ],
        [(heads, width)],
        share,
    )
    (x_all, gain_all, grad_ffn_all), (natural, out_rows) = gather(
        [hidden_in, jnp.broadcast_to(attn_gain[None, :], (8, cols_dev)), grad_ffn],
        0,
        [spread_heads, spread_out],
    )
    joint = dot(natural, permutation, ((1,), (0,))).astype(BF16)

    wide = x_all.astype(F32)
    scale_one = lax.rsqrt(jnp.mean(wide * wide, axis=1) + NORM_EPS)
    normed_one = (wide * scale_one[:, None] * gain_all[:1]).astype(BF16)

    pre = dot(normed_one, joint, ((1,), (0,)))
    pre_one, pre_two = pre[:, :128], pre[:, 128:256]
    rot = jnp.concatenate(
        [pre_one * cosine - pre_two * sine, pre_two * cosine + pre_one * sine], axis=1
    ).astype(BF16)
    val = pre[:, 256:].astype(BF16)
    heads_out, log_all = attend_forward(low, rot, val, first_rows)
    attn_part = dot(heads_out, out_rows, ((1,), (0,))).astype(BF16)

    def units_piece(which):
        return (
            which,
            lambda c, h: (at(h * depth, depth), at(c * ffn, ffn)),
            0,
            lambda c, h: (at(c * cols_dev + h * depth, depth), pl.ds(which * ffn, ffn)),
        )

    spread_gate_up = Spread(
        [gate_weight, up_weight], [units_piece(0), units_piece(1)], [(width, 2 * ffn)], share
    )
    (attn_sum,), (gate_up,) = reduce_scatter([attn_part], 1, [spread_gate_up])
    resid_mid = residual + RES_SCALE * attn_sum

    squares = jnp.sum(resid_mid * resid_mid, axis=1)
    spread_down = Spread(
        [down_weight],
        [
            (
                0,
                lambda c, h: (at(c * ffn + h * ffn_part, ffn_part), every),
                0,
                lambda c, h: (at(h * ffn_part, ffn_part), at(c * cols_dev, cols_dev)),
            )
        ],
        [(ffn, width)],
        share,
    )
    (raw_two, square_all), (down,) = gather(
        [(resid_mid * ffn_gain[None, :]).astype(BF16), pack(squares)], 2, [spread_down]
    )
    square_sum = jnp.sum(square_all.reshape(NR, 8, nz, 128), axis=2)[:, : rows_dev // 128]
    scale_two = lax.rsqrt(square_sum.reshape(tokens) / width + NORM_EPS)

    both = dot(raw_two, gate_up, ((1,), (0,))) * scale_two[:, None]
    gate_pre, up_pre = both[:, :ffn], both[:, ffn:]
    gate_sig = jax.nn.sigmoid(gate_pre)
    gate_act = gate_pre * gate_sig
    hidden_act = (gate_act * up_pre).astype(BF16)
    down_part_sum = dot(hidden_act, down, ((1,), (0,))).astype(BF16)
    down_grad_part = dot(hidden_act, grad_ffn_all, ((0,), (0,))).astype(BF16)
    swaps = []
    if two:
        swaps = [
            Swap(
                down_grad_part,
                [(lambda h: (at(h * ffn_part, ffn_part), every), (every, every))],
                (ffn_part, width),
            )
        ]
    (down_sum,), others = reduce_scatter([down_part_sum], 3, swaps)
    layer_out = (resid_mid + RES_SCALE * down_sum).astype(BF16)

    def half_of(a, axis):
        size = a.shape[axis] // parts
        return lax.dynamic_slice_in_dim(a, lax.axis_index("group") * size, size, axis)

    def plus(a, b):
        return (a.astype(F32) + b.astype(F32)).astype(BF16)

    if two:
        down_grad_part = plus(half_of(down_grad_part, 0), others[0])
    spread_down_grad = Spread(
        [down_grad_part],
        [
            (
                0,
                lambda c, h: (every, at(c * cols_dev, cols_dev)),
                0,
                lambda c, h: (at(c * ffn + h * ffn_part, ffn_part), every),
            )
        ],
        [(ffn * nz, cols_dev)],
        "sum" if two else "plain",
    )

    grad_hidden = dot(grad_ffn_all, down, ((1,), (1,)))
    grad_gate = grad_hidden * up_pre * gate_sig * (1.0 + gate_pre * (1.0 - gate_sig))
    grad_up = grad_hidden * gate_act
    inner_two = jnp.sum(grad_gate * gate_pre + grad_up * up_pre, axis=1)
    grad_pair = jnp.concatenate([grad_gate, grad_up], axis=1)
    grad_pair_scaled = (grad_pair * scale_two[:, None]).astype(BF16)
    grad_two_part = dot(grad_pair.astype(BF16), gate_up, ((1,), (1,))).astype(BF16)
    pair_grad_part = dot(raw_two, grad_pair_scaled, ((0,), (0,))).astype(BF16)
    stats = jnp.tile(
        jnp.pad(by_row(inner_two), ((0, 0), (0, 4), (0, 0))).reshape(NR * 8, 128), (1, nz)
    )
    extras = [spread_down_grad]
    if two:
        extras.append(
            Swap(
                pair_grad_part,
                [
                    (
                        lambda h, m=m: (every, at((2 * m + h) * ffn_part, ffn_part)),
                        (every, pl.ds(m * ffn_part, ffn_part)),
                    )
                    for m in range(2)
                ],
                (width, 2 * ffn_part),
            )
        )
    (grad_two, inner_two_sum), others = reduce_scatter([grad_two_part, stats], 4, extras)
    down_grad = others[0]
    if two:
        pair_grad_part = plus(
            jnp.concatenate(
                [half_of(pair_grad_part[:, :ffn], 1), half_of(pair_grad_part[:, ffn:], 1)], axis=1
            ),
            others[1],
        )
    scale_two_own = lax.dynamic_slice_in_dim(scale_two, row * rows_dev, rows_dev)[:, None]
    inner_two_own = inner_two_sum[: rows_dev // 128].reshape(rows_dev, 1)
    grad_mid = (
        grad_top
        + scale_two_own * ffn_gain[None, :] * grad_two
        - resid_mid * (scale_two_own * scale_two_own * inner_two_own / width)
    )
    ffn_gain_part = jnp.sum(grad_two * resid_mid * scale_two_own, axis=0)
    grad_attn = (RES_SCALE * grad_mid).astype(BF16)

    def grad_piece(which):
        return (
            0,
            lambda c, h: (at(c * cols_dev, cols_dev), pl.ds(which * ffn_part, ffn_part)),
            which,
            lambda c, h: (every, at(c * ffn + h * ffn_part, ffn_part)),
        )

    spread_pair_grad = Spread(
        [pair_grad_part],
        [grad_piece(0), grad_piece(1)],
        [(cols_dev, ffn * nz)] * 2,
        "sum" if two else "plain",
    )
    (grad_attn_all,), (gate_grad, up_grad) = gather([grad_attn], 5, [spread_pair_grad])

    grad_heads = dot(grad_attn_all, out_rows, ((1,), (1,))).astype(BF16)
    out_grad_part = dot(heads_out, grad_attn_all, ((0,), (0,))).astype(BF16)
    grad_rot, grad_val = attend_backward(
        low, rot, val, first_rows, log_all, heads_out, grad_heads
    )
    inner_one = jnp.sum(grad_rot * rot.astype(F32), axis=1) + jnp.sum(
        grad_val * val.astype(F32), axis=1
    )
    grot_one, grot_two = grad_rot[:, :128], grad_rot[:, 128:]
    grad_pre = jnp.concatenate(
        [grot_one * cosine + grot_two * sine, grot_two * cosine - grot_one * sine, grad_val], axis=1
    ).astype(BF16)
    grad_natural = dot(grad_pre, permutation, ((1,), (1,))).astype(BF16)
    grad_one_part = dot(grad_natural, natural, ((1,), (1,))).astype(BF16)
    natural_grad = dot(normed_one, grad_natural, ((0,), (0,)))
    attn_gain_part = jnp.sum(natural_grad * natural.astype(F32), axis=1) / gain_all[0]
    natural_grad = natural_grad.astype(BF16)
    mine = (jnp.arange(nz) == col)[:, None, None]
    gain_lines = jnp.concatenate(
        [by_col(attn_gain_part, nz), jnp.where(mine, pack(ffn_gain_part, 4)[None], 0.0)], axis=1
    )
    lines = jnp.concatenate(
        [
            jnp.broadcast_to(by_row(inner_one)[:, None], (NR, nz, 4, 128)),
            jnp.broadcast_to(gain_lines[None], (NR, nz, 8, 128)),
            jnp.zeros((NR, nz, 4, 128), F32),
        ],
        axis=2,
    )
    stats = jnp.transpose(lines, (0, 2, 1, 3)).reshape(NR * 16, nz * 128)
    spread_small = Spread(
        [out_grad_part, natural_grad],
        [
            (
                0,
                lambda c, h: (every, at(c * cols_dev, cols_dev)),
                0,
                lambda c, h: (at(c * heads, heads), every),
            ),
            (
                1,
                lambda c, h: (at(c * cols_dev, cols_dev), pl.ds(0, heads)),
                1,
                lambda c, h: (every, at(c * heads, heads)),
            ),
            (
                1,
                lambda c, h: (at(c * cols_dev, cols_dev), pl.ds(heads, kv)),
                2,
                lambda c, h: (every, at(c * kv, kv)),
            ),
        ],
        [(heads * nz, cols_dev), (cols_dev, heads * nz), (cols_dev, kv * nz)],
        "twin" if two else "plain",
    )
    (grad_one, last), small = reduce_scatter([grad_one_part, stats], 6, [spread_small])
    scale_one_own = lax.dynamic_slice_in_dim(scale_one, row * rows_dev, rows_dev)[:, None]
    inner_one_own = last[:4].reshape(rows_dev, 1)
    input_grad = (
        grad_mid
        + scale_one_own * attn_gain[None, :] * grad_one
        - residual * (scale_one_own * scale_one_own * inner_one_own / width)
    )
    gain_grads = sum_over_group(last[4:12])
    if two:
        out_grad, query_grad, kv_grad = (
            small[m].astype(F32) + small[m + 3].astype(F32) for m in range(3)
        )
        down_grad, gate_grad, up_grad = (
            a.astype(F32) for a in (down_grad, gate_grad, up_grad)
        )
    else:
        out_grad, query_grad, kv_grad, down_grad, gate_grad, up_grad = (
            lax.psum(a, "group").astype(F32) for a in (*small, down_grad, gate_grad, up_grad)
        )
    kv_grad = jnp.sum(kv_grad.reshape(cols_dev, 2, nz // 2, 2, HEAD_SIZE), axis=2)
    key_grad = kv_grad[:, :, 0].reshape(cols_dev, 2 * HEAD_SIZE)
    value_grad = kv_grad[:, :, 1].reshape(cols_dev, 2 * HEAD_SIZE)
    return (
        layer_out,
        input_grad,
        gain_grads[:4].reshape(cols_dev),
        query_grad,
        key_grad,
        value_grad,
        out_grad,
        gain_grads[4:].reshape(cols_dev),
        gate_grad,
        up_grad,
        down_grad,
    )


def solution(mesh):
    return jax.shard_map(
        on_device,
        mesh=mesh,
        in_specs=(
            P(("group", "row"), "col"),
            P("group", None),
            P("col"),
            P("col", "row"),
            P("col", "row"),
            P("col", "row"),
            P("row", "col"),
            P("col"),
            P("col", "row"),
            P("col", "row"),
            P("row", "col"),
            P(("group", "row"), "col"),
        ),
        out_specs=(
            P(("group", "row"), "col"),
            P(("group", "row"), "col"),
            P("col"),
            P("col", "row"),
            P("col", "row"),
            P("col", "row"),
            P("row", "col"),
            P("col"),
            P("col", "row"),
            P("col", "row"),
            P("row", "col"),
        ),
        check_vma=False,
    )
```

time: 963 us -> 824 us (0.86)
  Pallas kernels: 520 us -> 626 us
  local copies, waits for them, and re-layouts: 113 us -> 28.8 us
  waiting for transfers between devices: 76.4 us -> 0.01 us
  starting transfers between devices: 48.7 us -> 2.48 us
  blocking collectives: 14.3 us -> 0 us
  between operations: 15.4 us -> 1.84 us
  other arithmetic: 54.8 us -> 45.1 us
    pallas_call x6 -> x7, Pallas kernels: 490 us -> 592 us  [the longest x4 309 us: reduce_scatter(): pl.pallas_call(functools.partial(scatter_kernel, n, nz, extras), out_shap...]
    all_to_all x8 -> x0, waiting for transfers between devices: 58.4 us -> none  [the longest x1 31.4 us: on_device(): lax.all_to_all(pair_grad_part, 'col', 0, 1, tiled=True)]
    all_to_all x8 -> x0, starting transfers between devices: 45 us -> none  [the longest x1 12 us: on_device(): down_part = lax.all_to_all(down_send, 'col', 0, 1, tiled=True)]
    unnamed x111 -> x108, local copies, waits for them, and re-layouts: 33.6 us -> 10.9 us
    all_gather x4 -> x0, waiting for transfers between devices: 16.7 us -> none  [the longest x1 16.7 us: on_device(): down = lax.all_gather(down_part, 'group', axis=0, tiled=True)]
    psum x1 -> x0, blocking collectives: 14.3 us -> none  [on_device(): lax.psum((attn_gain_part, ffn_gain_part), ('group', 'row'))]
    convert_element_type x2 -> x0, local copies, waits for them, and re-layouts: 12.8 us -> none  [the longest x1 6.41 us: on_device(): up_grad = pair_grad[:, :, :, 1].reshape(cols_dev, nz * ffn).astype(F32)]
    slice x7 -> x5, local copies, waits for them, and re-layouts: 16.4 us -> 3.61 us  [the longest x1 2.34 us: on_device(): pair_grad_part[:, :ffn]]
  transfers between devices with their start and end apart: 16 -> 1, of which waited for: 5 -> 0; matrix products, arithmetic and copies ran while one was open for 21% -> 3% of each run, Pallas kernels for 29% -> 0%
where the time goes in v2:
time: 824 us; the launch traced here: 815 us
  Pallas kernels  626 us (76%)
  matrix products  111 us (13%)
  other arithmetic  45.1 us (5%)
  local copies, waits for them, and re-layouts  28.8 us (3%)
    pallas_call x4, Pallas kernels, reduce_scatter(): pl.pallas_call(functools.partial(scatter_kernel, n, nz, extras), out_shap...  309 us
    pallas_call x3, Pallas kernels, gather(): pl.pallas_call(functools.partial(gather_kernel, n, nz, units, extras), ou...  283 us
    dot_general x13, matrix products, dot(): return lax.dot_general(a, b, (dims, ((), ())), preferred_element_type=F32)  111 us
    pallas_call x1, Pallas kernels, attend_backward(): pl.pallas_call(attend_backward_kernel, grid_spec=pltpu.PrefetchScalarGrid...  19.6 us
  transfers between devices with their start and end apart: 1, of which 0 were waited for; matrix products, arithmetic and copies ran while one was open for 3% of the time, Pallas kernels for 0%

profile of v2, /device:TPU:0, one launch (start us, length us, event | category | flops | bytes accessed | tf_op | source)
XLA Modules:
  0.0 814.6 jit_solution(5588005784254998551)
XLA Ops:
  7.7 106.5 %gather.13 = (bf16[2048,2048]{1,0:T(8,128)(2,1)}, f32[32,2048]{1,0:T(8,128)}, bf16[2048,2048]{1,0:T(8,128)(2,1)}, bf16[2048,256]{1,0:T(8,128)(2,1)}, bf16[128,2048]{1,0:T(8,128)(2,1)}) custom-call(bf16[512,512]{1,0:T(8,128)(2,1)} %refs_0_.1, f32[8,512]{1,0:T(8,128)} %broadcast_in_dim.48.refs_1_, bf16[512,512]{1,0:T(8,128)(2,1)} %fusion.19.refs_2_, ...), custom_call_target="tpu_custom_call" | custom-call | bytes 62914560 | tf_op jit(solution)/shard_map/gather/pallas_call | solution.py:362
  114.3 5.1 fusion
  124.3 10.4 %fusion.11 = f32[2048,384]{1,0:T(8,128)} fusion(bf16[2048,2048]{1,0:T(8,128)(2,1)} %get-tuple-element.42, f32[2048]{0:T(1024)S(1)} %bitcast.73, f32[2048]{0:T(1024)S(1)} %add_rsqrt_fusion, bf16[2048,256]{1,0:T(8,128)(2,1)} %get-tuple-element.44, s32[384]{0:T(512)S(1)} %pad_add_fusion), kind=kOutput, calls=%fused_computation.28 | convolution fusion | flops 3641540608 | bytes 12600832 | tf_op jit(solution)/shard_map/dot_general | solution.py:27
  138.8 13.9 %attend_forward.1 = (bf16[2048,128]{1,0:T(8,128)(2,1)S(1)}, f32[8,1,512]{2,1,0:T(1,128)S(1)}) custom-call(s32[8]{0:T(128)S(1)} %and_select_fusion.low_ref, bf16[2048,256]{1,0:T(8,128)(2,1)S(1)} %pad_maximum_fusion.1.rot_ref, bf16[2048,128]{1,0:T(8,128)(2,1)S(1)} %slice.144.val_ref, s32[8,1,256]{2,1,0:T(1,128)S(1)} %bitcast.63), custom_call_target="tpu_custom_call" | custom-call | flops 12000000000 | bytes 4194304 | tf_op jit(solution)/shard_map/attend_forward/pallas_call | solution.py:673
  152.7 5.6 convolution_convert_fusion.3.refs_0_
  158.4 85.7 %reduce_scatter.4 = (f32[512,512]{1,0:T(8,128)S(1)}, bf16[2048,1024]{1,0:T(8,128)(2,1)}) custom-call(bf16[2048,2048]{1,0:T(8,128)(2,1)} %convolution_convert_fusion.3.refs_0_, bf16[512,2048]{1,0:T(8,128)(2,1)S(1)} %copy-done.4, bf16[512,2048]{1,0:T(8,128)(2,1)S(1)} %copy-done.5), custom_call_target="tpu_custom_call" | custom-call | bytes 62914560 | tf_op jit(solution)/shard_map/reduce_scatter/pallas_call | solution.py:528
  245.7 74.1 %gather.14 = (bf16[2048,2048]{1,0:T(8,128)(2,1)}, f32[32,512]{1,0:T(8,128)}, bf16[512,2048]{1,0:T(8,128)(2,1)}) custom-call(bf16[512,512]{1,0:T(8,128)(2,1)} %get-tuple-element.127.refs_0_, f32[8,128]{1,0:T(8,128)} %pad.10.refs_1_, bf16[2048,512]{1,0:T(8,128)(2,1)} %refs_2_.3), custom_call_target="tpu_custom_call" | custom-call | bytes 62914560 | tf_op jit(solution)/shard_map/gather/pallas_call | solution.py:362
  320.7 13.7 %convolution_multiply_fusion = f32[2048,1024]{0,1:T(8,128)S(1)} fusion(bf16[2048,2048]{1,0:T(8,128)(2,1)} %get-tuple-element.48, bf16[2048,1024]{1,0:T(8,128)(2,1)} %get-tuple-element.49, f32[2048]{0:T(1024)S(1)} %bitcast.78), kind=kOutput, calls=%fused_computation.14 | convolution fusion | flops 8592031744 | bytes 20979712 | tf_op jit(solution)/shard_map/dot_general | solution.py:27
  334.4 12.2 %add_reduce_fusion = (f32[2048]{0:T(1024)S(1)}, f32[2048,512]{0,1:T(8,128)}, f32[2048,512]{0,1:T(8,128)}, bf16[2048,512]{0,1:T(8,128)(2,1)S(1)}) fusion(f32[2048,1024]{0,1:T(8,128)S(1)} %convolution_multiply_fusion, bf16[2048,2048]{1,0:T(8,128)(2,1)} %get-tuple-element.52, bf16[512,2048]{1,0:T(8,128)(2,1)S(1)} %copy-done.51), kind=kOutput, calls=%fused_computation.17 | convolution fusion | flops 4312791040 | bytes 29368320 | tf_op jit(solution)/shard_map/dot_general | solution.py:27
  346.6 9.0 %convolution_convert_fusion.4.refs_1_ = bf16[512,2048]{1,0:T(8,128)(2,1)} fusion(bf16[2048,512]{0,1:T(8,128)(2,1)S(1)} %get-tuple-element.113, bf16[2048,2048]{1,0:T(8,128)(2,1)} %get-tuple-element.52), kind=kOutput, calls=%fused_computation.24 | convolution fusion | flops 4296015872 | bytes 12582912 | tf_op jit(solution)/shard_map/dot_general | solution.py:27
  355.7 6.8 convolution_convert_fusion.2.refs_0_
  362.5 14.1 %fusion.8.refs_3_ = bf16[2048,1024]{1,0:T(8,128)(2,1)S(1)} fusion(bf16[2048,2048]{1,0:T(8,128)(2,1)} %get-tuple-element.48, f32[2048,512]{0,1:T(8,128)} %get-tuple-element.112, f32[2048,512]{0,1:T(8,128)} %get-tuple-element.111, f32[2048]{0:T(1024)S(1)} %bitcast.79), kind=kOutput, calls=%fused_computation.23 | convolution fusion | flops 8598323200 | bytes 20979712 | tf_op jit(solution)/shard_map/dot_general | solution.py:27
  376.6 16.3 %convolution_convert_fusion.1.refs_0_ = bf16[2048,2048]{1,0:T(8,128)(2,1)} fusion(bf16[2048,1024]{1,0:T(8,128)(2,1)S(1)} %copy-done.50, f32[2048,512]{0,1:T(8,128)} %get-tuple-element.112, f32[2048,512]{0,1:T(8,128)} %get-tuple-element.111), kind=kOutput, calls=%fused_computation.10 | convolution fusion | flops 8602517504 | bytes 20971520 | tf_op jit(solution)/shard_map/dot_general | solution.py:27
  399.9 65.2 %reduce_scatter.5 = (f32[512,512]{1,0:T(8,128)S(1)}, bf16[256,2048]{1,0:T(8,128)(2,1)S(1)}) custom-call(bf16[2048,2048]{1,0:T(8,128)(2,1)} %convolution_convert_fusion.2.refs_0_, bf16[512,2048]{1,0:T(8,128)(2,1)S(1)} %copy-done), custom_call_target="tpu_custom_call" | custom-call | bytes 62914560 | tf_op jit(solution)/shard_map/reduce_scatter/pallas_call | solution.py:528
  467.8 76.1 %reduce_scatter.6 = (f32[512,512]{1,0:T(8,128)S(1)}, f32[8,128]{1,0:T(8,128)S(1)}, bf16[2048,512]{1,0:T(8,128)(2,1)S(1)}, bf16[2048,512]{1,0:T(8,128)(2,1)}) custom-call(bf16[2048,2048]{1,0:T(8,128)(2,1)} %convolution_convert_fusion.1.refs_0_, f32[32,512]{1,0:T(8,128)S(1)} %bitcast.62, bf16[256,2048]{1,0:T(8,128)(2,1)S(1)} %copy-done.1, ...), custom_call_target="tpu_custom_call" | custom-call | bytes 62914560 | tf_op jit(solution)/shard_map/reduce_scatter/pallas_call | solution.py:528
  544.0 4.2 add_convert_fusion.refs_1_
  549.6 102.9 %gather.15 = (bf16[2048,2048]{1,0:T(8,128)(2,1)}, bf16[512,2048]{1,0:T(8,128)(2,1)}, bf16[512,2048]{1,0:T(8,128)(2,1)}) custom-call(bf16[512,512]{1,0:T(8,128)(2,1)} %get-tuple-element.121.refs_0_, bf16[2048,512]{1,0:T(8,128)(2,1)} %add_convert_fusion.refs_1_), custom_call_target="tpu_custom_call" | custom-call | bytes 62914560 | tf_op jit(solution)/shard_map/gather/pallas_call | solution.py:362
  652.5 4.8 convolution_convert_fusion.7.refs_2_
  660.7 19.6 %attend_backward.1 = (f32[2048,256]{1,0:T(8,128)S(1)}, f32[2048,128]{1,0:T(8,128)S(1)}) custom-call(s32[8]{0:T(128)S(1)} %and_select_fusion.low_ref, bf16[2048,256]{1,0:T(8,128)(2,1)S(1)} %copy-done.8, bf16[2048,128]{1,0:T(8,128)(2,1)S(1)} %copy-done.13, s32[8,1,256]{2,1,0:T(1,128)S(1)} %bitcast.64, f32[8,1,512]{2,1,0:T(1,128)S(1)} %get-tuple-element.57.log_ref, ...), custom_call_target="tpu_custom_call" | custom-call | flops 20000000000 | bytes 8388608 | tf_op jit(solution)/shard_map/attend_backward/pallas_call | solution.py:707
  686.9 7.9 fusion.34
  694.8 5.7 convolution_convert_fusion.refs_0_
  702.0 81.8 %reduce_scatter.7 = (f32[512,512]{1,0:T(8,128)S(1)}, f32[16,128]{1,0:T(8,128)S(1)}, bf16[512,512]{1,0:T(8,128)(2,1)S(1)}, bf16[512,512]{1,0:T(8,128)(2,1)S(1)}, ...) custom-call(bf16[2048,2048]{1,0:T(8,128)(2,1)} %convolution_convert_, ...), custom_call_target="tpu_custom_call" | custom-call | bytes 62914560 | tf_op jit(solution)/shard_map/reduce_scatter/pallas_call | solution.py:528
  799.1 3.4 fusion.18
  804.2 4.1 convert_element_type.177
  (178 shorter events, 63.7 us)
Async XLA Ops:
  114.2 6.0 copy-start.46
  114.2 6.7 copy-start.47
  119.4 15.3 %copy-start.43 = (f32[2048]{0:T(1024)}, f32[2048]{0:T(1024)S(1)}, u32[]{:S(2)}) copy-start(f32[2048]{0:T(1024)S(1)} %add_rsqrt_fusion) | copy-start | bytes 24580
  120.2 14.4 %copy-start.40 = (f32[1,2048]{1,0:T(1,128)}, f32[1,2048]{1,0:T(1,128)S(1)}, u32[]{:S(2)}) copy-start(f32[1,2048]{1,0:T(1,128)S(1)} %slice.81) | copy-start | bytes 24580
  123.1 12.9 %copy-start.20 = (f32[2048,128]{1,0:T(8,128)}, f32[2048,128]{1,0:T(8,128)S(1)}, u32[]{:S(2)}) copy-start(f32[2048,128]{1,0:T(8,128)S(1)} %copy.69) | copy-start | bytes 3145732
  123.5 12.4 %copy-start.22 = (f32[2048,128]{1,0:T(8,128)}, f32[2048,128]{1,0:T(8,128)S(1)}, u32[]{:S(2)}) copy-start(f32[2048,128]{1,0:T(8,128)S(1)} %copy.71) | copy-start | bytes 3145732
  135.9 16.8 %copy-start.12 = (bf16[2048,128]{1,0:T(8,128)(2,1)}, bf16[2048,128]{1,0:T(8,128)(2,1)S(1)}, u32[]{:S(2)}) copy-start(bf16[2048,128]{1,0:T(8,128)(2,1)S(1)} %slice.144.val_ref) | copy-start | bytes 1572868
  138.0 14.7 %copy-start.29 = (bf16[2048,128]{1,0:T(8,128)(2,1)}, bf16[2048,128]{1,0:T(8,128)(2,1)S(1)}, u32[]{:S(2)}) copy-start(bf16[2048,128]{1,0:T(8,128)(2,1)S(1)} %get-tuple-element.114) | copy-start | bytes 1572868
  138.7 14.0 %copy-start.7 = (bf16[2048,256]{1,0:T(8,128)(2,1)}, bf16[2048,256]{1,0:T(8,128)(2,1)S(1)}, u32[]{:S(2)}) copy-start(bf16[2048,256]{1,0:T(8,128)(2,1)S(1)} %pad_maximum_fusion.1.rot_ref) | copy-start | bytes 3145732
  138.7 14.0 %copy-start.38 = (bf16[128,2048]{1,0:T(8,128)(2,1)S(1)}, bf16[128,2048]{1,0:T(8,128)(2,1)}, u32[]{:S(2)}) copy-start(bf16[128,2048]{1,0:T(8,128)(2,1)} %get-tuple-element.46) | copy-start | bytes 1572868
  158.4 85.7 %copy-start.24 = (bf16[512,512]{1,0:T(8,128)(2,1)S(1)}, bf16[512,512]{1,0:T(8,128)(2,1)}, u32[]{:S(2)}) copy-start(bf16[512,512]{1,0:T(8,128)(2,1)} %refs_0_.1) | copy-start | bytes 1572868
  158.4 85.7 %copy-start.42 = (f32[512]{0:T(512)S(1)}, f32[512]{0:T(512)}, u32[]{:S(2)}) copy-start(f32[512]{0:T(512)} %param.21) | copy-start | bytes 6148
  320.7 13.8 %copy-start.51 = (bf16[512,2048]{1,0:T(8,128)(2,1)S(1)}, bf16[512,2048]{1,0:T(8,128)(2,1)}, u32[]{:S(2)}) copy-start(bf16[512,2048]{1,0:T(8,128)(2,1)} %get-tuple-element.51) | copy-start | bytes 6291460
  362.5 14.1 %copy-start.50 = (bf16[2048,1024]{1,0:T(8,128)(2,1)S(1)}, bf16[2048,1024]{1,0:T(8,128)(2,1)}, u32[]{:S(2)}) copy-start(bf16[2048,1024]{1,0:T(8,128)(2,1)} %get-tuple-element.49) | copy-start | bytes 12582916
  376.6 16.3 %copy-start.19 = (bf16[2048,1024]{1,0:T(8,128)(2,1)}, bf16[2048,1024]{1,0:T(8,128)(2,1)S(1)}, u32[]{:S(2)}) copy-start(bf16[2048,1024]{1,0:T(8,128)(2,1)S(1)} %fusion.8.refs_3_) | copy-start | bytes 12582916
  467.8 76.3 %copy-start.33 = (bf16[2048,256]{1,0:T(8,128)(2,1)S(1)}, bf16[2048,256]{1,0:T(8,128)(2,1)}, u32[]{:S(2)}) copy-start(bf16[2048,256]{1,0:T(8,128)(2,1)} %constant_dynamic-slice_fusion) | copy-start | bytes 3145732
  467.8 76.3 %copy-start.34 = (bf16[2048,256]{1,0:T(8,128)(2,1)S(1)}, bf16[2048,256]{1,0:T(8,128)(2,1)}, u32[]{:S(2)}) copy-start(bf16[2048,256]{1,0:T(8,128)(2,1)} %constant_dynamic-slice_fusion.1) | copy-start | bytes 3145732
  660.7 20.6 %copy-start.30 = (bf16[2048,128]{1,0:T(8,128)(2,1)S(1)}, bf16[2048,128]{1,0:T(8,128)(2,1)}, u32[]{:S(2)}) copy-start(bf16[2048,128]{1,0:T(8,128)(2,1)} %copy-done.29) | copy-start | bytes 1572868
  660.7 20.6 %copy-start.32 = (bf16[2048,128]{1,0:T(8,128)(2,1)S(1)}, bf16[2048,128]{1,0:T(8,128)(2,1)}, u32[]{:S(2)}) copy-start(bf16[2048,128]{1,0:T(8,128)(2,1)} %copy-done.31) | copy-start | bytes 1572868
  660.7 20.9 %copy-start.21 = (f32[2048,128]{1,0:T(8,128)S(1)}, f32[2048,128]{1,0:T(8,128)}, u32[]{:S(2)}) copy-start(f32[2048,128]{1,0:T(8,128)} %copy-done.20) | copy-start | bytes 3145732
  660.7 20.9 %copy-start.23 = (f32[2048,128]{1,0:T(8,128)S(1)}, f32[2048,128]{1,0:T(8,128)}, u32[]{:S(2)}) copy-start(f32[2048,128]{1,0:T(8,128)} %copy-done.22) | copy-start | bytes 3145732
  787.2 10.8 %copy-start.15 = (bf16[512,512]{1,0:T(8,128)(2,1)S(1)}, bf16[512,512]{1,0:T(8,128)(2,1)}, u32[]{:S(2)}) copy-start(bf16[512,512]{1,0:T(8,128)(2,1)} %copy-done.14) | copy-start | bytes 1572868
  787.2 26.3 %collective-permute-start = (f32[8,128]{1,0:T(8,128)S(1)}, f32[8,128]{1,0:T(8,128)S(1)}, u32[]{:S(2)}, u32[]{:S(2)}) collective-permute-start(f32[8,128]{1,0:T(8,128)S(1)} %slice.95), channel_id=1, source_target_pairs={{0,16},{16,0},{1,17},{17,1},{2,18},{18,2},{3,19},{19,3},{4,20},{20... | collective-permute-start | bytes 12296 | tf_op jit(solution)/shard_map/ppermute | solution.py:747
  790.9 8.2 %copy-start.45 = (f32[512]{0:T(512)S(1)}, f32[512]{0:T(512)}, u32[]{:S(2)}) copy-start(f32[512]{0:T(512)} %param.16) | copy-start | bytes 6148
  (29 other events, 92.2 us)

commit v3 on v2

--- a/solution.py
+++ b/solution.py
@@ -21,6 +21,7 @@
 NR = 4
 BQ = 256
 NEG = -1e30
+SHORT = pl.CostEstimate(flops=0, bytes_accessed=2**20, transcendentals=0)
 
 
 def dot(a, b, dims):
@@ -206,87 +207,71 @@
     return devices
 
 
-def gather_kernel(n, nz, units, extras, *refs):
-    n_in, n_out = n + sum(len(e.arrays) for e in extras), n + sum(len(e.outs) for e in extras)
-    ins, outs, sems = refs[:n], refs[n_in : n_in + n], refs[n_in + n_out :]
-    local_sem, send_sem, recv_sem = sems[:3]
-    bind_extras(extras, refs[n:n_in], refs[n_in + n : n_in + n_out], sems[3:])
-    g, r, z, rc, rx, rxc = place()
-    has_left, has_right = z > 0, z < nz - 1
-    if any(isinstance(extra, Spread) for extra in extras):
-        devices = greetings(extras, nz, [(g, rc, z), (g, rx, z)])
-        barrier = greet(devices)
-        pl.semaphore_wait(barrier, len(devices))
-    else:
-        devices = greetings(extras, nz, [(g, rc, z), (g, rx, z)])
-        barrier = greet(devices)
-
-        @pl.when(has_left)
-        def _():
-            pl.semaphore_signal(barrier, inc=1, device_id=(g, r, z - 1), device_id_type=MESH)
-
-        @pl.when(has_right)
-        def _():
-            pl.semaphore_signal(barrier, inc=1, device_id=(g, r, z + 1), device_id_type=MESH)
-
-        count = has_left.astype(jnp.int32) + has_right.astype(jnp.int32)
-        pl.semaphore_wait(barrier, len(devices) + count)
-
-    right, left, over_x, to_core = 0, nz - 1, 2 * (nz - 1), 3 * nz - 2
-
-    def own_part(u):
-        i, start, size = units[u]
-        return ins[i].at[pl.ds(start, size), :]
-
-    def slot(u, row, col):
-        i, start, size = units[u]
-        b0, b1 = ins[i].shape
-        return outs[i].at[
+class Gather:
+    def __init__(self, nz, units, ins, outs, sems):
+        self.nz, self.units, self.ins, self.outs, self.sems = nz, units, ins, outs, sems
+        self.at = place()
+        z = self.at[2]
+        self.has_left, self.has_right = z > 0, z < nz - 1
+        self.right, self.left, self.over_x, self.to_core = 0, nz - 1, 2 * (nz - 1), 3 * nz - 2
+
+    def own_part(self, u):
+        i, start, size = self.units[u]
+        return self.ins[i].at[pl.ds(start, size), :]
+
+    def slot(self, u, row, col):
+        i, start, size = self.units[u]
+        b0, b1 = self.ins[i].shape
+        return self.outs[i].at[
             pl.ds(pl.multiple_of(row * b0 + start, size), size),
             pl.ds(pl.multiple_of(col * b1, b1), b1),
         ]
 
-    def copy(u, src, row, col, where, device):
+    def copy(self, u, src, row, col, where, device):
         return pltpu.make_async_remote_copy(
             src_ref=src,
-            dst_ref=slot(u, row, col),
-            send_sem=send_sem.at[u, where],
-            recv_sem=recv_sem.at[u, row, col],
+            dst_ref=self.slot(u, row, col),
+            send_sem=self.sems[1].at[u, where],
+            recv_sem=self.sems[2].at[u, row, col],
             device_id=device,
             device_id_type=MESH,
         )
 
-    def own(u, where, device):
-        return copy(u, own_part(u), r, z, where, device)
-
-    def forward(u, row, col, where, device):
-        return copy(u, slot(u, row, col), row, col, where, device)
-
-    def rank(col):
-        return col - (col > z).astype(jnp.int32)
-
-    def local(u):
-        return pltpu.make_async_copy(own_part(u), slot(u, r, z), local_sem.at[u])
-
-    every = range(len(units))
-    for u in every:
-
-        @pl.when(has_right)
-        def _():
-            own(u, right, (g, r, z + 1)).start()
-
-        @pl.when(has_left)
-        def _():
-            own(u, left, (g, r, z - 1)).start()
-
-        own(u, over_x, (g, rx, z)).start()
-    for u in every:
-        own(u, to_core, (g, rc, z)).start()
-        local(u).start()
-    for extra in extras:
-        extra.start(nz)
-
-    def from_x(u, k):
+    def own(self, u, where, device):
+        g, r, z, rc, rx, rxc = self.at
+        return self.copy(u, self.own_part(u), r, z, where, device)
+
+    def forward(self, u, row, col, where, device):
+        return self.copy(u, self.slot(u, row, col), row, col, where, device)
+
+    def rank(self, col):
+        return col - (col > self.at[2]).astype(jnp.int32)
+
+    def local(self, u):
+        g, r, z, rc, rx, rxc = self.at
+        return pltpu.make_async_copy(self.own_part(u), self.slot(u, r, z), self.sems[0].at[u])
+
+    def begin(self):
+        g, r, z, rc, rx, rxc = self.at
+        every = range(len(self.units))
+        for u in every:
+
+            @pl.when(self.has_right)
+            def _():
+                self.own(u, self.right, (g, r, z + 1)).start()
+
+            @pl.when(self.has_left)
+            def _():
+                self.own(u, self.left, (g, r, z - 1)).start()
+
+            self.own(u, self.over_x, (g, rx, z)).start()
+        for u in every:
+            self.own(u, self.to_core, (g, rc, z)).start()
+            self.local(u).start()
+
+    def from_x(self, u, k):
+        g, r, z, rc, rx, rxc = self.at
+        to_core, nz = self.to_core, self.nz
         for near, col, where in (
             (z - k >= 0, z - k, to_core + 1 if k == 0 else to_core + nz + 1 + z - k),
             (z + k < nz, z + k, to_core + nz + z + k),
@@ -294,55 +279,95 @@
 
             @pl.when(near)
             def _():
-                forward(u, rx, col, where, (g, rx, z)).wait_recv()
-                forward(u, rx, col, where, (g, rc, z)).start()
-
-    def from_z(u, k):
+                self.forward(u, rx, col, where, (g, rx, z)).wait_recv()
+                self.forward(u, rx, col, where, (g, rc, z)).start()
+
+    def from_z(self, u, k):
+        g, r, z, rc, rx, rxc = self.at
         for near, more, col, device, flow in (
-            (z - k >= 0, has_right, z - k, (g, r, z + 1), right),
-            (z + k < nz, has_left, z + k, (g, r, z - 1), left),
+            (z - k >= 0, self.has_right, z - k, (g, r, z + 1), self.right),
+            (z + k < self.nz, self.has_left, z + k, (g, r, z - 1), self.left),
         ):
 
             @pl.when(near)
             def _():
-                forward(u, r, col, flow, (g, rc, z)).wait_recv()
-                if k < nz - 1:
+                self.forward(u, r, col, flow, (g, rc, z)).wait_recv()
+                if k < self.nz - 1:
 
                     @pl.when(more)
                     def _():
-                        forward(u, r, col, flow + k, device).start()
-
-                forward(u, r, col, over_x + 1 + rank(col), (g, rx, z)).start()
-                forward(u, r, col, to_core + 2 + rank(col), (g, rc, z)).start()
-
+                        self.forward(u, r, col, flow + k, device).start()
+
+                self.forward(u, r, col, self.over_x + 1 + self.rank(col), (g, rx, z)).start()
+                self.forward(u, r, col, self.to_core + 2 + self.rank(col), (g, rc, z)).start()
+
+    def finish(self, u):
+        g, r, z, rc, rx, rxc = self.at
+        for col in range(self.nz):
+            self.forward(u, rc, col, self.to_core, (g, rc, z)).wait_recv()
+            self.forward(u, rxc, col, self.to_core, (g, rc, z)).wait_recv()
+        self.local(u).wait()
+
+    def sent(self, u):
+        g, r, z, rc, rx, rxc = self.at
+        for where in range(self.to_core + 2 * self.nz):
+
+            def wait(where=where):
+                self.own(u, where, (g, rc, z)).wait_send()
+
+            if where < self.left:
+                pl.when(self.has_right & (z - where >= 0))(wait)
+            elif where < self.over_x:
+                pl.when(self.has_left & (z + (where - self.left) < self.nz))(wait)
+            else:
+                wait()
+
+
+def gather_sems(units, nz):
+    return [DMA((units,)), DMA((units, 5 * nz - 2)), DMA((units, NR, nz))]
+
+
+def gather_kernel(n, nz, units, extras, *refs):
+    n_in, n_out = n + sum(len(e.arrays) for e in extras), n + sum(len(e.outs) for e in extras)
+    ins, outs, sems = refs[:n], refs[n_in : n_in + n], refs[n_in + n_out :]
+    bind_extras(extras, refs[n:n_in], refs[n_in + n : n_in + n_out], sems[3:])
+    work = Gather(nz, units, ins, outs, sems[:3])
+    g, r, z, rc, rx, rxc = place()
+    devices = greetings(extras, nz, [(g, rc, z), (g, rx, z)])
+    barrier = greet(devices)
+    if any(isinstance(extra, Spread) for extra in extras):
+        pl.semaphore_wait(barrier, len(devices))
+    else:
+
+        @pl.when(z > 0)
+        def _():
+            pl.semaphore_signal(barrier, inc=1, device_id=(g, r, z - 1), device_id_type=MESH)
+
+        @pl.when(z < nz - 1)
+        def _():
+            pl.semaphore_signal(barrier, inc=1, device_id=(g, r, z + 1), device_id_type=MESH)
+
+        count = (z > 0).astype(jnp.int32) + (z < nz - 1).astype(jnp.int32)
+        pl.semaphore_wait(barrier, len(devices) + count)
+
+    every = range(len(units))
+    work.begin()
+    for extra in extras:
+        extra.start(nz)
     for k in range(1, nz):
         for u in every:
-            from_z(u, k)
-            from_x(u, k - 1)
+            work.from_z(u, k)
+            work.from_x(u, k - 1)
         if k > 1:
             for extra in extras:
                 extra.step(k - 1, nz)
     for u in every:
-        from_x(u, nz - 1)
+        work.from_x(u, nz - 1)
     for extra in extras:
         extra.step(nz - 1, nz)
-
     for u in every:
-        for col in range(nz):
-            forward(u, rc, col, to_core, (g, rc, z)).wait_recv()
-            forward(u, rxc, col, to_core, (g, rc, z)).wait_recv()
-        local(u).wait()
-        for where in range(to_core + 2 * nz):
-
-            def sent(where=where):
-                own(u, where, (g, rc, z)).wait_send()
-
-            if where < left:
-                pl.when(has_right & (z - where >= 0))(sent)
-            elif where < over_x:
-                pl.when(has_left & (z + (where - left) < nz))(sent)
-            else:
-                sent()
+        work.finish(u)
+        work.sent(u)
     for extra in extras:
         extra.finish(nz)
 
@@ -367,10 +392,9 @@
         + extra_out,
         in_specs=[anywhere] * (n + len(extra_in)),
         out_specs=[anywhere] * (n + len(extra_out)),
-        scratch_shapes=[DMA((len(units),)), DMA((len(units), 5 * nz - 2)), DMA((len(units), NR, nz))]
-        + flat(e.scratch for e in extras),
+        scratch_shapes=gather_sems(len(units), nz) + flat(e.scratch for e in extras),
         compiler_params=pltpu.CompilerParams(collective_id=collective_id, has_side_effects=True),
-        cost_estimate=pl.CostEstimate(flops=0, bytes_accessed=60 * 2**20, transcendentals=0),
+        cost_estimate=SHORT,
         name="gather",
     )(*arrays, *extra_in)
     return outs[:n], outs[n:]
@@ -389,31 +413,41 @@
         lax.fori_loop(0, total // step, one, 0)
 
 
-def scatter_kernel(n, nz, extras, *refs):
-    n_in, n_out = n + sum(len(e.arrays) for e in extras), n + sum(len(e.outs) for e in extras)
-    ins, outs, rest = refs[:n], refs[n_in : n_in + n], refs[n_in + n_out :]
-    bufs = [rest[6 * i : 6 * (i + 1)] for i in range(n)]
-    load_sem, core_send, core_recv, x_send, x_recv, z_send, z_recv = rest[6 * n : 6 * n + 7]
-    bind_extras(extras, refs[n:n_in], refs[n_in + n : n_in + n_out], rest[6 * n + 7 :])
-    g, r, z, rc, rx, rxc = place()
-    pair = z + 1 - 2 * lax.rem(z, 2)
-    far, far_pair = lax.rem(z + 2, nz), lax.rem(pair + 2, nz)
-    devices = greetings(extras, nz, [(g, rc, z), (g, rx, z), (g, r, pair), (g, r, far)])
-    barrier = greet(devices)
-    pl.semaphore_wait(barrier, len(devices))
-    order = (far_pair, pair, far, z)
-    steps = range(len(order))
-
-    def block(i, row, step):
-        b0, b1 = ins[i].shape[0] // NR, ins[i].shape[1] // nz
-        return block_at(ins[i], row, order[step], (b0, b1))
-
-    def load(i, way, step):
+class Scatter:
+    def __init__(self, nz, source, out, bufs, sems, load):
+        self.nz, self.source, self.out, self.load_it = nz, source, out, load
+        self.own = bufs[0] if load else None
+        self.from_core, self.half, self.from_x, self.mine, self.from_z = bufs[-5:]
+        self.core_send, self.core_recv, self.x_send, self.x_recv, self.z_send, self.z_recv = sems[:6]
+        self.load_sem = sems[6] if load else None
+        self.at = g, r, z, rc, rx, rxc = place()
+        self.pair = z + 1 - 2 * lax.rem(z, 2)
+        self.far = lax.rem(z + 2, nz)
+        self.order = (lax.rem(self.pair + 2, nz), self.pair, self.far, z)
+
+    def partners(self):
+        g, r, z, rc, rx, rxc = self.at
+        return [(g, rc, z), (g, rx, z), (g, r, self.pair), (g, r, self.far)]
+
+    def shape(self):
+        return self.source.shape[0] // NR, self.source.shape[1] // self.nz
+
+    def block(self, row, step):
+        return block_at(self.source, row, self.order[step], self.shape())
+
+    def load(self, way, step):
+        g, r, z, rc, rx, rxc = self.at
         return pltpu.make_async_copy(
-            block(i, (rx, r)[way], step), bufs[i][0].at[way, step], load_sem.at[i, way, step]
+            self.block((rx, r)[way], step), self.own.at[way, step], self.load_sem.at[way, step]
         )
 
-    def remote(src, dst, send, recv, device):
+    def part(self, way, step, rows):
+        g, r, z, rc, rx, rxc = self.at
+        if self.load_it:
+            return self.own[way, step, rows, :].astype(F32)
+        return self.block((rx, r)[way], step)[rows, :].astype(F32)
+
+    def remote(self, src, dst, send, recv, device):
         return pltpu.make_async_remote_copy(
             src_ref=src,
             dst_ref=dst,
@@ -423,94 +457,124 @@
             device_id_type=MESH,
         )
 
-    def core(i, way, step):
-        return remote(
-            block(i, (rxc, rc)[way], step),
-            bufs[i][1].at[way, step],
-            core_send.at[i, way, step],
-            core_recv.at[i, way, step],
+    def core(self, way, step):
+        g, r, z, rc, rx, rxc = self.at
+        return self.remote(
+            self.block((rxc, rc)[way], step),
+            self.from_core.at[way, step],
+            self.core_send.at[way, step],
+            self.core_recv.at[way, step],
             (g, rc, z),
         )
 
-    def over_x(i, step):
-        return remote(
-            bufs[i][2].at[step], bufs[i][3].at[step], x_send.at[i, step], x_recv.at[i, step], (g, rx, z)
+    def over_x(self, step):
+        g, r, z, rc, rx, rxc = self.at
+        return self.remote(
+            self.half.at[step],
+            self.from_x.at[step],
+            self.x_send.at[step],
+            self.x_recv.at[step],
+            (g, rx, z),
         )
 
-    def along_z(i, step):
-        return remote(
-            bufs[i][4].at[step],
-            bufs[i][5].at[step],
-            z_send.at[i, step],
-            z_recv.at[i, step],
-            (g, r, far if step == 2 else pair),
+    def along_z(self, step):
+        g, r, z, rc, rx, rxc = self.at
+        return self.remote(
+            self.mine.at[step],
+            self.from_z.at[step],
+            self.z_send.at[step],
+            self.z_recv.at[step],
+            (g, r, self.far if step == 2 else self.pair),
         )
 
-    for i in range(n):
+    def begin(self):
         for way in range(2):
-            for step in steps:
-                core(i, way, step).start()
-                load(i, way, step).start()
-    for i in range(n):
-        own, from_core, half, from_x, mine, from_z = bufs[i]
-        for step in steps:
-            load(i, 0, step).wait()
-            core(i, 0, step).wait_recv()
-
-            def add(rows):
-                half[step, rows, :] = (
-                    own[0, step, rows, :].astype(F32) + from_core[0, step, rows, :].astype(F32)
-                ).astype(half.dtype)
-
-            in_rows(own.shape[2], 64, add)
-            over_x(i, step).start()
-        if i == 0:
+            for step in range(4):
+                self.core(way, step).start()
+                if self.load_it:
+                    self.load(way, step).start()
+
+    def to_x(self, step):
+        if self.load_it:
+            self.load(0, step).wait()
+        self.core(0, step).wait_recv()
+
+        def add(rows):
+            self.half[step, rows, :] = (
+                self.part(0, step, rows) + self.from_core[0, step, rows, :].astype(F32)
+            ).astype(self.half.dtype)
+
+        in_rows(self.shape()[0], 64, add)
+        self.over_x(step).start()
+
+    def to_z(self, step):
+        if self.load_it:
+            self.load(1, step).wait()
+        self.core(1, step).wait_recv()
+        self.over_x(step).wait_recv()
+        for earlier in {2: (0,), 3: (1, 2)}.get(step, ()):
+            self.along_z(earlier).wait_recv()
+
+        def add(rows):
+            total = (
+                self.part(1, step, rows)
+                + self.from_core[1, step, rows, :].astype(F32)
+                + self.from_x[step, rows, :].astype(F32)
+            )
+            for earlier in {2: (0,), 3: (1, 2)}.get(step, ()):
+                total = total + self.from_z[earlier, rows, :].astype(F32)
+            if step == 3:
+                self.out[rows, :] = total
+            else:
+                self.mine[step, rows, :] = total.astype(self.mine.dtype)
+
+        in_rows(self.shape()[0], 64, add)
+        if step < 3:
+            self.along_z(step).start()
+
+    def finish(self):
+        for step in range(4):
+            self.core(0, step).wait_send()
+            self.core(1, step).wait_send()
+            self.over_x(step).wait_send()
+            if step < 3:
+                self.along_z(step).wait_send()
+
+
+def scatter_scratch(shape, dtype, nz, load):
+    block = (shape[0] // NR, shape[1] // nz)
+    leads = [(2, nz)] * (2 if load else 1) + [(nz,), (nz,), (nz - 1,), (nz - 1,)]
+    sems = [DMA((2, nz))] * 2 + [DMA((nz,))] * 4 + ([DMA((2, nz))] if load else [])
+    return [pltpu.VMEM(lead + block, dtype) for lead in leads], sems
+
+
+def scatter_kernel(n, nz, extras, *refs):
+    n_in, n_out = n + sum(len(e.arrays) for e in extras), n + sum(len(e.outs) for e in extras)
+    ins, outs, rest = refs[:n], refs[n_in : n_in + n], refs[n_in + n_out :]
+    works = [
+        Scatter(nz, ins[i], outs[i], rest[13 * i : 13 * i + 6], rest[13 * i + 6 : 13 * i + 13], True)
+        for i in range(n)
+    ]
+    bind_extras(extras, refs[n:n_in], refs[n_in + n : n_in + n_out], rest[13 * n :])
+    devices = greetings(extras, nz, works[0].partners())
+    barrier = greet(devices)
+    pl.semaphore_wait(barrier, len(devices))
+    for work in works:
+        work.begin()
+    for work in works:
+        for step in range(4):
+            work.to_x(step)
+        if work is works[0]:
             for extra in extras:
                 extra.start(nz)
-    for i in range(n):
-        own, from_core, half, from_x, mine, from_z = bufs[i]
-
-        def total(step, rows):
-            result = (
-                own[1, step, rows, :].astype(F32)
-                + from_core[1, step, rows, :].astype(F32)
-                + from_x[step, rows, :].astype(F32)
-            )
-            if step == 2:
-                result = result + from_z[0, rows, :].astype(F32)
-            if step == 3:
-                result = result + from_z[1, rows, :].astype(F32) + from_z[2, rows, :].astype(F32)
-            return result
-
-        for step in steps:
-            load(i, 1, step).wait()
-            core(i, 1, step).wait_recv()
-            over_x(i, step).wait_recv()
-            if step == 2:
-                along_z(i, 0).wait_recv()
-            if step == 3:
-                along_z(i, 1).wait_recv()
-                along_z(i, 2).wait_recv()
-
-            def add(rows):
-                if step == 3:
-                    outs[i][rows, :] = total(step, rows)
-                else:
-                    mine[step, rows, :] = total(step, rows).astype(mine.dtype)
-
-            in_rows(own.shape[2], 64, add)
-            if step < 3:
-                along_z(i, step).start()
-            if i == 0 and 1 <= step:
+    for work in works:
+        for step in range(4):
+            work.to_z(step)
+            if work is works[0] and 1 <= step:
                 for extra in extras:
                     extra.step(step, nz)
-    for i in range(n):
-        for step in steps:
-            core(i, 0, step).wait_send()
-            core(i, 1, step).wait_send()
-            over_x(i, step).wait_send()
-            if step < 3:
-                along_z(i, step).wait_send()
+    for work in works:
+        work.finish()
     for extra in extras:
         extra.finish(nz)
 
@@ -519,10 +583,7 @@
     n, nz = len(arrays), lax.axis_size("col")
     scratch = []
     for a in arrays:
-        shape = (a.shape[0] // NR, a.shape[1] // nz)
-        for lead in ((2, nz), (2, nz), (nz,), (nz,), (nz - 1,), (nz - 1,)):
-            scratch.append(pltpu.VMEM(lead + shape, a.dtype))
-    scratch += [DMA((n, 2, nz))] * 3 + [DMA((n, nz))] * 4
+        scratch += flat(scatter_scratch(a.shape, a.dtype, nz, True))
     anywhere = pl.BlockSpec(memory_space=pl.ANY)
     extra_in, extra_out = flat(e.arrays for e in extras), flat(e.outs for e in extras)
     outs = pl.pallas_call(
@@ -537,10 +598,335 @@
         compiler_params=pltpu.CompilerParams(
             collective_id=collective_id, has_side_effects=True, vmem_limit_bytes=48 * 2**20
         ),
-        cost_estimate=pl.CostEstimate(flops=0, bytes_accessed=60 * 2**20, transcendentals=0),
+        cost_estimate=SHORT,
         name="reduce_scatter",
     )(*arrays, *extra_in)
     return outs[:n], outs[n:]
+
+
+def feed_forward_kernel(
+    nz,
+    early,
+    late,
+    raw_ref,
+    inverse_ref,
+    gate_up_ref,
+    grad_ref,
+    *refs,
+):
+    n_in, n_out = sum(len(e.arrays) for e in early), sum(len(e.outs) for e in early + late)
+    raw_all, down_out, scale_out, grad_two_a, grad_two_b, inner_out, pair_grad, down_grad = refs[
+        n_in : n_in + 8
+    ]
+    down_ref = refs[n_in + 8]
+    rest = refs[n_in + 8 + n_out :]
+    gate_up, down, x_buf, g_buf, d_buf, unit_a, unit_b, inner, hidden_t, scaled = rest[:10]
+    left_buf, right_buf, pair_buf, down_buf = rest[10:14]
+    load_sem, in_sem, out_sem, tile_sem, done_sem = rest[14:19]
+    sems, rest = rest[19:22], rest[22:]
+    units = [(0, 0, raw_ref.shape[0] // 2), (0, raw_ref.shape[0] // 2, raw_ref.shape[0] // 2)]
+    size = units[0][2]
+    gather_work = Gather(nz, units, [raw_ref], [raw_all], sems)
+    works = []
+    for source, out in ((unit_a, grad_two_a), (unit_b, grad_two_b), (inner, inner_out)):
+        works.append(Scatter(nz, source, out, rest[:5], rest[5:11], False))
+        rest = rest[11:]
+    bind_extras(
+        early + late,
+        list(refs[:n_in]) + [down_grad] * len(late),
+        refs[n_in + 8 : n_in + 8 + n_out],
+        rest,
+    )
+    g, r, z, rc, rx, rxc = place()
+    devices = greetings(early + late, nz, [(g, rc, z), (g, rx, z)])
+    barrier = greet(devices)
+    pl.semaphore_wait(barrier, len(devices))
+
+    gather_work.begin()
+    load_gate_up = pltpu.make_async_copy(gate_up_ref, gate_up, load_sem.at[0])
+    load_gate_up.start()
+    load_down = pltpu.make_async_copy(down_ref, down, load_sem.at[1])
+    for extra in early:
+        extra.start(nz)
+    inner[...] = jnp.zeros_like(inner)
+    for k in range(1, nz):
+        for u in range(2):
+            gather_work.from_z(u, k)
+            gather_work.from_x(u, k - 1)
+        if k > 1:
+            for extra in early:
+                extra.step(k - 1, nz)
+    gather_work.from_x(0, nz - 1)
+    for extra in early:
+        extra.step(nz - 1, nz)
+    ffn, width = down.shape
+    tile, block = left_buf.shape[2], raw_ref.shape[1]
+    tiles = width // tile
+    parts = pair_grad.shape[0]
+
+    def tokens_of(u, row):
+        return pl.ds(row * 2 * size + u * size, size)
+
+    def fetch(u, row):
+        slot = (u * NR + row) % 2
+        return [
+            pltpu.make_async_copy(
+                raw_all.at[tokens_of(u, row), :], x_buf.at[slot], in_sem.at[0, slot]
+            ),
+        ] + [
+            pltpu.make_async_copy(
+                grad_ref.at[row * nz + col, pl.ds(u * size, size), :],
+                g_buf.at[slot, :, pl.ds(col * block, block)],
+                in_sem.at[1 + col, slot],
+            )
+            for col in range(nz)
+        ]
+
+    def put(u, row):
+        slot = (u * NR + row) % 2
+        same_core, same_x = lax.rem(r + row, 2), lax.rem(r // 2 + row // 2, 2)
+        return [
+            pltpu.make_async_copy(
+                d_buf.at[slot, :, pl.ds(pl.multiple_of(col * block, block), block)],
+                down_out.at[same_core, same_x, step, pl.ds(u * size, size), :],
+                out_sem.at[step, slot],
+            )
+            for step, col in enumerate(works[0].order)
+        ]
+
+    def chunk(u, row):
+        slot = (u * NR + row) % 2
+        for copy in fetch(u, row):
+            copy.wait()
+        if row + 1 < NR:
+            for copy in fetch(u, row + 1):
+                copy.start()
+        if u * NR + row >= 2:
+            before = u * NR + row - 2
+            for copy in put(before // NR, before % NR):
+                copy.wait()
+        here = tokens_of(u, row)
+        unit = (unit_a, unit_b)[u]
+        x = x_buf[slot]
+        plain = x.astype(F32) * inverse_ref[...]
+        scale = lax.rsqrt(jnp.sum(plain * plain, axis=1, keepdims=True) / width + NORM_EPS)
+        scale_out[here, :] = jnp.broadcast_to(scale, (size, 128))
+        gate = dot(x, gate_up[:, :ffn], ((1,), (0,))) * scale
+        up = dot(x, gate_up[:, ffn:], ((1,), (0,))) * scale
+        sig = jax.nn.sigmoid(gate)
+        act = gate * sig
+        hidden = (act * up).astype(BF16)
+        hidden_t[:, here] = hidden.T
+        d_buf[slot] = dot(hidden, down[...], ((1,), (0,))).astype(BF16)
+        for copy in put(u, row):
+            copy.start()
+        grad_hidden = dot(g_buf[slot], down[...], ((1,), (1,)))
+        grad_gate = grad_hidden * up * sig * (1.0 + gate * (1.0 - sig))
+        grad_up = grad_hidden * act
+        total = jnp.sum(grad_gate * gate + grad_up * up, axis=1, keepdims=True)
+        turned = jnp.broadcast_to(total, (size, 128)).T
+        for m in range(size // 128):
+            line = turned[:8, m * 128 : (m + 1) * 128]
+            at_line = u * (size // 128) + m
+            pick = lax.broadcasted_iota(jnp.int32, line.shape, 0) == at_line
+            for col in range(nz):
+                part = (slice(row * 8, row * 8 + 8), slice(col * 128, col * 128 + 128))
+                inner[part] = jnp.where(pick, line, inner[part])
+        scaled[here, :ffn] = (grad_gate * scale).astype(BF16)
+        scaled[here, ffn:] = (grad_up * scale).astype(BF16)
+        back = dot(grad_gate.astype(BF16), gate_up[:, :ffn], ((1,), (1,)))
+        back = back + dot(grad_up.astype(BF16), gate_up[:, ffn:], ((1,), (1,)))
+        unit[row * size : (row + 1) * size, :] = back.astype(BF16)
+
+    def tile_in(kind, n):
+        slot = lax.rem(n, 2)
+        if kind == 1:
+            return [
+                pltpu.make_async_copy(
+                    raw_all.at[:, pl.ds(pl.multiple_of(n * tile, tile), tile)],
+                    left_buf.at[slot],
+                    tile_sem.at[NR, slot],
+                )
+            ]
+        col, inside = n // (block // tile), lax.rem(n, block // tile)
+        return [
+            pltpu.make_async_copy(
+                grad_ref.at[row * nz + col, :, pl.ds(pl.multiple_of(inside * tile, tile), tile)],
+                right_buf.at[slot, pl.ds(row * 2 * size, 2 * size), :],
+                tile_sem.at[row, slot],
+            )
+            for row in range(NR)
+        ]
+
+    def tile_out(kind, n):
+        slot = lax.rem(n, 2)
+        where = pl.ds(pl.multiple_of(n * tile, tile), tile)
+        half = ffn // parts
+        copies = []
+        for h in range(parts):
+            part = lax.rem(h + g, 2) if parts == 2 else 0
+            if kind == 0:
+                copies.append((down_buf.at[slot, pl.ds(h * half, half), :], down_grad.at[part, :, where]))
+            else:
+                for m in range(2):
+                    copies.append(
+                        (
+                            pair_buf.at[slot, :, pl.ds(m * ffn + h * half, half)],
+                            pair_grad.at[part, where, pl.ds(m * half, half)],
+                        )
+                    )
+        return [
+            pltpu.make_async_copy(src, dst, done_sem.at[kind, m, slot])
+            for m, (src, dst) in enumerate(copies)
+        ]
+
+    def weight_tiles(kind, low, high):
+        def one(n, carry):
+            slot = lax.rem(n, 2)
+            for copy in tile_in(kind, n):
+                copy.wait()
+
+            @pl.when(n + 1 < tiles)
+            def _():
+                for copy in tile_in(kind, n + 1):
+                    copy.start()
+
+            @pl.when(n >= 2)
+            def _():
+                for copy in tile_out(kind, n - 2):
+                    copy.wait()
+
+            if kind == 0:
+                down_buf[slot] = dot(hidden_t[...], right_buf[slot], ((1,), (0,))).astype(BF16)
+            else:
+                pair_buf[slot] = dot(left_buf[slot], scaled[...], ((0,), (0,))).astype(BF16)
+            for copy in tile_out(kind, n):
+                copy.start()
+            return carry
+
+        lax.fori_loop(low, high, one, 0)
+
+    gather_work.finish(0)
+    for copy in fetch(0, 0):
+        copy.start()
+    for extra in early:
+        extra.finish(nz)
+    load_down.start()
+    gather_work.from_x(1, nz - 1)
+    load_gate_up.wait()
+    load_down.wait()
+    for row in range(NR):
+        chunk(0, row)
+    first, second, third = works
+    first.begin()
+    gather_work.finish(1)
+    for copy in fetch(1, 0):
+        copy.start()
+    for step in range(4):
+        first.to_x(step)
+    chunk(1, 0)
+    chunk(1, 1)
+    first.to_z(0)
+    chunk(1, 2)
+    first.to_z(1)
+    for copy in tile_in(0, 0) + tile_in(1, 0):
+        copy.start()
+    chunk(1, 3)
+    second.begin()
+    third.begin()
+    first.to_z(2)
+    for step in range(4):
+        second.to_x(step)
+    for step in range(4):
+        third.to_x(step)
+    first.to_z(3)
+    third.to_z(0)
+    third.to_z(1)
+    weight_tiles(0, 0, tiles)
+    third.to_z(2)
+    for n in (tiles - 2, tiles - 1):
+        for copy in tile_out(0, n):
+            copy.wait()
+    for extra in late:
+        extra.start(nz)
+    second.to_z(0)
+    weight_tiles(1, 0, tiles // 4)
+    second.to_z(1)
+    weight_tiles(1, tiles // 4, tiles // 2)
+    second.to_z(2)
+    weight_tiles(1, tiles // 2, 3 * tiles // 4)
+    weight_tiles(1, 3 * tiles // 4, tiles)
+    second.to_z(3)
+    third.to_z(3)
+    for u in range(2):
+        gather_work.sent(u)
+    for work in works:
+        work.finish()
+    for row in (NR - 2, NR - 1):
+        for copy in put(1, row):
+            copy.wait()
+    for n in (tiles - 2, tiles - 1):
+        for copy in tile_out(1, n):
+            copy.wait()
+    for extra in late:
+        extra.finish(nz)
+
+
+def feed_forward(raw, inverse, gate_up, grad, collective_id, early, late):
+    nz = lax.axis_size("col")
+    width, ffn = gate_up.shape[0], gate_up.shape[1] // 2
+    tokens, size, tile = raw.shape[0] * NR, raw.shape[0] // 2, 256
+    parts = 2 if lax.axis_size("group") == 2 else 1
+    anywhere, vmem = pl.BlockSpec(memory_space=pl.ANY), pl.BlockSpec(memory_space=pltpu.VMEM)
+    shape = jax.ShapeDtypeStruct
+    scatters = [((NR * size, width), BF16)] * 2 + [((NR * 8, nz * 128), F32)]
+    extra_in, extra_out = flat(e.arrays for e in early), flat(e.outs for e in early + late)
+    outs = pl.pallas_call(
+        functools.partial(feed_forward_kernel, nz, early, late),
+        out_shape=[
+            shape((tokens, width), BF16),
+            shape((2, 2, nz) + raw.shape, BF16),
+            shape((tokens, 128), F32),
+            shape((size, raw.shape[1]), F32),
+            shape((size, raw.shape[1]), F32),
+            shape((8, 128), F32),
+            shape((parts, width, 2 * ffn // parts), BF16),
+            shape((parts, ffn // parts, width), BF16),
+        ]
+        + extra_out,
+        in_specs=[anywhere, vmem, anywhere, anywhere] + [anywhere] * len(extra_in),
+        out_specs=[anywhere] * 2 + [vmem] * 4 + [anywhere] * (2 + len(extra_out)),
+        scratch_shapes=[
+            pltpu.VMEM(gate_up.shape, BF16),
+            pltpu.VMEM((ffn, width), BF16),
+            pltpu.VMEM((2, size, width), BF16),
+            pltpu.VMEM((2, size, width), BF16),
+            pltpu.VMEM((2, size, width), BF16),
+            pltpu.VMEM((NR * size, width), BF16),
+            pltpu.VMEM((NR * size, width), BF16),
+            pltpu.VMEM((NR * 8, nz * 128), F32),
+            pltpu.VMEM((ffn, tokens), BF16),
+            pltpu.VMEM((tokens, 2 * ffn), BF16),
+            pltpu.VMEM((2, tokens, tile), BF16),
+            pltpu.VMEM((2, tokens, tile), BF16),
+            pltpu.VMEM((2, tile, 2 * ffn), BF16),
+            pltpu.VMEM((2, ffn, tile), BF16),
+            DMA((2,)),
+            DMA((1 + nz, 2)),
+            DMA((nz, 2)),
+            DMA((NR + 1, 2)),
+            DMA((2, 2 * parts, 2)),
+        ]
+        + gather_sems(2, nz)
+        + flat(flat(scatter_scratch(s, t, nz, False)) for s, t in scatters)
+        + flat(e.scratch for e in early + late),
+        compiler_params=pltpu.CompilerParams(
+            collective_id=collective_id, has_side_effects=True, vmem_limit_bytes=58 * 2**20
+        ),
+        cost_estimate=SHORT,
+        name="feed_forward",
+    )(raw, inverse, gate_up, grad, *extra_in)
+    return outs[:8], outs[8:]
 
 
 def swap64(v):
@@ -691,9 +1077,7 @@
             jax.ShapeDtypeStruct((n, 1, 2 * BQ), F32),
         ],
         compiler_params=pltpu.CompilerParams(vmem_limit_bytes=40 * 2**20),
-        cost_estimate=pl.CostEstimate(
-            flops=12 * 10**9, bytes_accessed=4 * 2**20, transcendentals=4 * 10**6
-        ),
+        cost_estimate=SHORT,
         name="attend_forward",
     )(low, rot, val, first)
 
@@ -722,11 +1106,40 @@
         ),
         out_shape=[jax.ShapeDtypeStruct((t, 256), F32), jax.ShapeDtypeStruct((t, 128), F32)],
         compiler_params=pltpu.CompilerParams(vmem_limit_bytes=40 * 2**20),
-        cost_estimate=pl.CostEstimate(
-            flops=20 * 10**9, bytes_accessed=8 * 2**20, transcendentals=4 * 10**6
-        ),
+        cost_estimate=SHORT,
         name="attend_backward",
     )(low, rot, val, first, log_all, out, grad)
+
+
+def assemble_kernel(mine_ref, other_ref, gate_ref, up_ref):
+    part = gate_ref.shape[1]
+    is_mine = pl.program_id(1) == lax.axis_index("group")
+
+    @pl.when(is_mine)
+    def _():
+        gate_ref[...] = mine_ref[0, :, :part].astype(F32)
+        up_ref[...] = mine_ref[0, :, part:].astype(F32)
+
+    @pl.when(jnp.logical_not(is_mine))
+    def _():
+        gate_ref[...] = other_ref[0, :, :part].astype(F32)
+        up_ref[...] = other_ref[0, :, part:].astype(F32)
+
+
+def assemble(mine, other):
+    nz, depth, part = mine.shape[0], mine.shape[1], mine.shape[2] // 2
+    block = pl.BlockSpec((1, depth, 2 * part), lambda c, h: (c, 0, 0))
+    out = pl.BlockSpec((depth, part), lambda c, h: (0, 2 * c + h))
+    return pl.pallas_call(
+        assemble_kernel,
+        grid=(nz, 2),
+        in_specs=[block, block],
+        out_specs=[out, out],
+        out_shape=[jax.ShapeDtypeStruct((depth, 2 * nz * part), F32)] * 2,
+        compiler_params=pltpu.CompilerParams(vmem_limit_bytes=40 * 2**20),
+        cost_estimate=SHORT,
+        name="assemble",
+    )(mine, other)
 
 
 def pack(values, rows=8):
@@ -848,12 +1261,18 @@
         [(heads, width)],
         share,
     )
-    (x_all, gain_all, grad_ffn_all), (natural, out_rows) = gather(
-        [hidden_in, jnp.broadcast_to(attn_gain[None, :], (8, cols_dev)), grad_ffn],
+    (x_all, gain_all), (natural, out_rows) = gather(
+        [
+            hidden_in,
+            jnp.concatenate([jnp.broadcast_to(a[None, :], (8, cols_dev)) for a in (attn_gain, ffn_gain)]),
+        ],
         0,
         [spread_heads, spread_out],
     )
     joint = dot(natural, permutation, ((1,), (0,))).astype(BF16)
+    gain_two_all = gain_all[8:]
+    grad_ffn, x_all = lax.optimization_barrier((grad_ffn, x_all))
+    grad_ffn_all = lax.all_gather(grad_ffn, ("row", "col"), axis=0, tiled=False)
 
     wide = x_all.astype(F32)
     scale_one = lax.rsqrt(jnp.mean(wide * wide, axis=1) + NORM_EPS)
@@ -879,10 +1298,6 @@
     spread_gate_up = Spread(
         [gate_weight, up_weight], [units_piece(0), units_piece(1)], [(width, 2 * ffn)], share
     )
-    (attn_sum,), (gate_up,) = reduce_scatter([attn_part], 1, [spread_gate_up])
-    resid_mid = residual + RES_SCALE * attn_sum
-
-    squares = jnp.sum(resid_mid * resid_mid, axis=1)
     spread_down = Spread(
         [down_weight],
         [
@@ -896,42 +1311,49 @@
         [(ffn, width)],
         share,
     )
-    (raw_two, square_all), (down,) = gather(
-        [(resid_mid * ffn_gain[None, :]).astype(BF16), pack(squares)], 2, [spread_down]
-    )
-    square_sum = jnp.sum(square_all.reshape(NR, 8, nz, 128), axis=2)[:, : rows_dev // 128]
-    scale_two = lax.rsqrt(square_sum.reshape(tokens) / width + NORM_EPS)
-
-    both = dot(raw_two, gate_up, ((1,), (0,))) * scale_two[:, None]
-    gate_pre, up_pre = both[:, :ffn], both[:, ffn:]
-    gate_sig = jax.nn.sigmoid(gate_pre)
-    gate_act = gate_pre * gate_sig
-    hidden_act = (gate_act * up_pre).astype(BF16)
-    down_part_sum = dot(hidden_act, down, ((1,), (0,))).astype(BF16)
-    down_grad_part = dot(hidden_act, grad_ffn_all, ((0,), (0,))).astype(BF16)
-    swaps = []
+    (attn_sum,), (gate_up,) = reduce_scatter([attn_part], 1, [spread_gate_up])
+    resid_mid = residual + RES_SCALE * attn_sum
+
+    late = []
     if two:
-        swaps = [
+        late = [
             Swap(
-                down_grad_part,
-                [(lambda h: (at(h * ffn_part, ffn_part), every), (every, every))],
+                jax.ShapeDtypeStruct((parts, ffn_part, width), BF16),
+                [(lambda h: (1, every, every), (every, every))],
                 (ffn_part, width),
             )
         ]
-    (down_sum,), others = reduce_scatter([down_part_sum], 3, swaps)
-    layer_out = (resid_mid + RES_SCALE * down_sum).astype(BF16)
-
-    def half_of(a, axis):
-        size = a.shape[axis] // parts
-        return lax.dynamic_slice_in_dim(a, lax.axis_index("group") * size, size, axis)
+    (_, down_part_sum, scale_wide, grad_a, grad_b, inner_two_sum, pair_grad_part, down_grad_part), others = (
+        feed_forward(
+            (resid_mid * ffn_gain[None, :]).astype(BF16),
+            1.0 / gain_two_all[:1],
+            gate_up,
+            grad_ffn_all,
+            2,
+            [spread_down],
+            late,
+        )
+    )
+    grad_two = jnp.concatenate([grad_a, grad_b], axis=0)
+    scale_two_own = lax.dynamic_slice_in_dim(scale_wide, row * rows_dev, rows_dev)[:, :1]
+    inner_two_own = inner_two_sum[: rows_dev // 128].reshape(rows_dev, 1)
+    grad_mid = (
+        grad_top
+        + scale_two_own * ffn_gain[None, :] * grad_two
+        - resid_mid * (scale_two_own * scale_two_own * inner_two_own / width)
+    )
+    ffn_gain_part = jnp.sum(grad_two * resid_mid * scale_two_own, axis=0)
+    grad_attn = (RES_SCALE * grad_mid).astype(BF16)
 
     def plus(a, b):
         return (a.astype(F32) + b.astype(F32)).astype(BF16)
 
     if two:
-        down_grad_part = plus(half_of(down_grad_part, 0), others[0])
+        down_half = plus(down_grad_part[0], others[-1])
+    else:
+        down_half = down_grad_part[0]
     spread_down_grad = Spread(
-        [down_grad_part],
+        [down_half],
         [
             (
                 0,
@@ -944,66 +1366,32 @@
         "sum" if two else "plain",
     )
 
-    grad_hidden = dot(grad_ffn_all, down, ((1,), (1,)))
-    grad_gate = grad_hidden * up_pre * gate_sig * (1.0 + gate_pre * (1.0 - gate_sig))
-    grad_up = grad_hidden * gate_act
-    inner_two = jnp.sum(grad_gate * gate_pre + grad_up * up_pre, axis=1)
-    grad_pair = jnp.concatenate([grad_gate, grad_up], axis=1)
-    grad_pair_scaled = (grad_pair * scale_two[:, None]).astype(BF16)
-    grad_two_part = dot(grad_pair.astype(BF16), gate_up, ((1,), (1,))).astype(BF16)
-    pair_grad_part = dot(raw_two, grad_pair_scaled, ((0,), (0,))).astype(BF16)
-    stats = jnp.tile(
-        jnp.pad(by_row(inner_two), ((0, 0), (0, 4), (0, 0))).reshape(NR * 8, 128), (1, nz)
-    )
-    extras = [spread_down_grad]
+    (grad_attn_all,), (down_grad,) = gather([grad_attn], 5, [spread_down_grad])
+
+    pair_half = pair_grad_part[0]
     if two:
-        extras.append(
-            Swap(
-                pair_grad_part,
-                [
-                    (
-                        lambda h, m=m: (every, at((2 * m + h) * ffn_part, ffn_part)),
-                        (every, pl.ds(m * ffn_part, ffn_part)),
-                    )
-                    for m in range(2)
-                ],
-                (width, 2 * ffn_part),
-            )
-        )
-    (grad_two, inner_two_sum), others = reduce_scatter([grad_two_part, stats], 4, extras)
-    down_grad = others[0]
-    if two:
-        pair_grad_part = plus(
-            jnp.concatenate(
-                [half_of(pair_grad_part[:, :ffn], 1), half_of(pair_grad_part[:, ffn:], 1)], axis=1
-            ),
-            others[1],
-        )
-    scale_two_own = lax.dynamic_slice_in_dim(scale_two, row * rows_dev, rows_dev)[:, None]
-    inner_two_own = inner_two_sum[: rows_dev // 128].reshape(rows_dev, 1)
-    grad_mid = (
-        grad_top
-        + scale_two_own * ffn_gain[None, :] * grad_two
-        - resid_mid * (scale_two_own * scale_two_own * inner_two_own / width)
-    )
-    ffn_gain_part = jnp.sum(grad_two * resid_mid * scale_two_own, axis=0)
-    grad_attn = (RES_SCALE * grad_mid).astype(BF16)
-
-    def grad_piece(which):
-        return (
-            0,
-            lambda c, h: (at(c * cols_dev, cols_dev), pl.ds(which * ffn_part, ffn_part)),
-            which,
-            lambda c, h: (every, at(c * ffn + h * ffn_part, ffn_part)),
-        )
-
-    spread_pair_grad = Spread(
-        [pair_grad_part],
-        [grad_piece(0), grad_piece(1)],
-        [(cols_dev, ffn * nz)] * 2,
-        "sum" if two else "plain",
-    )
-    (grad_attn_all,), (gate_grad, up_grad) = gather([grad_attn], 5, [spread_pair_grad])
+        pair_half = plus(pair_half, lax.ppermute(pair_grad_part[1], "group", [(0, 1), (1, 0)]))
+
+    pair_half = lax.all_to_all(
+        pair_half.reshape(nz, cols_dev, 2 * ffn_part), "col", 0, 0, tiled=True
+    )
+    pair_other = lax.ppermute(pair_half, "group", [(0, 1), (1, 0)]) if two else pair_half
+
+    def step_over(a, axis, jump):
+        count = lax.axis_size(axis)
+        if jump == 2:
+            pairs = [(m, (m + 2) % count) for m in range(count)]
+        else:
+            pairs = [(m, m + 1 - 2 * (m % 2)) for m in range(count)]
+        return lax.ppermute(a, axis, pairs)
+
+    down_x = plus(down_part_sum[0], step_over(down_part_sum[1], "row", 1))
+    down_x, grad_attn_all = lax.optimization_barrier((down_x, grad_attn_all))
+    down_z = plus(down_x[0], step_over(down_x[1], "row", 2))
+    down_got = step_over(down_z[:2], "col", 1)
+    down_far = step_over(plus(down_z[2], down_got[0]), "col", 2)
+    down_sum = down_z[3].astype(F32) + down_got[1].astype(F32) + down_far.astype(F32)
+    layer_out = (resid_mid + RES_SCALE * down_sum).astype(BF16)
 
     grad_heads = dot(grad_attn_all, out_rows, ((1,), (1,))).astype(BF16)
     out_grad_part = dot(heads_out, grad_attn_all, ((0,), (0,))).astype(BF16)
@@ -1060,7 +1448,9 @@
         [(heads * nz, cols_dev), (cols_dev, heads * nz), (cols_dev, kv * nz)],
         "twin" if two else "plain",
     )
-    (grad_one, last), small = reduce_scatter([grad_one_part, stats], 6, [spread_small])
+    (grad_one, last), small = reduce_scatter(
+        [grad_one_part, stats], 6, [spread_small]
+    )
     scale_one_own = lax.dynamic_slice_in_dim(scale_one, row * rows_dev, rows_dev)[:, None]
     inner_one_own = last[:4].reshape(rows_dev, 1)
     input_grad = (
@@ -1073,12 +1463,17 @@
         out_grad, query_grad, kv_grad = (
             small[m].astype(F32) + small[m + 3].astype(F32) for m in range(3)
         )
-        down_grad, gate_grad, up_grad = (
-            a.astype(F32) for a in (down_grad, gate_grad, up_grad)
+        down_grad = down_grad.astype(F32)
+        gate_grad, up_grad = assemble(pair_half, pair_other)
+    else:
+        out_grad, query_grad, kv_grad, down_grad, pair_grad = (
+            lax.psum(a, "group").astype(F32) for a in (*small, down_grad, pair_half)
         )
-    else:
-        out_grad, query_grad, kv_grad, down_grad, gate_grad, up_grad = (
-            lax.psum(a, "group").astype(F32) for a in (*small, down_grad, gate_grad, up_grad)
+        gate_grad, up_grad = (
+            jnp.transpose(pair_grad[:, :, m * ffn : (m + 1) * ffn], (1, 0, 2)).reshape(
+                cols_dev, nz * ffn
+            )
+            for m in range(2)
         )
     kv_grad = jnp.sum(kv_grad.reshape(cols_dev, 2, nz // 2, 2, HEAD_SIZE), axis=2)
     key_grad = kv_grad[:, :, 0].reshape(cols_dev, 2 * HEAD_SIZE)

time: 824 us -> 731 us (0.89)
  matrix products: 111 us -> 34.5 us
  Pallas kernels: 626 us -> 564 us
  waiting for transfers between devices: 0.01 us -> 19 us
  between operations: 1.84 us -> 15 us
  starting transfers between devices: 2.48 us -> 11.4 us
    pallas_call x0 -> x2, Pallas kernels: none -> 189 us  [the longest x1 181 us: feed_forward(): pl.pallas_call(functools.partial(feed_forward_kernel, nz, early, late), o...]
    pallas_call x3 -> x2, Pallas kernels: 283 us -> 138 us  [gather(): pl.pallas_call(functools.partial(gather_kernel, n, nz, units, extras), ou...]
    pallas_call x4 -> x2, Pallas kernels: 309 us -> 208 us  [reduce_scatter(): pl.pallas_call(functools.partial(scatter_kernel, n, nz, extras), out_shap...]
    dot_general x13 -> x7, matrix products: 111 us -> 34.5 us  [dot(): return lax.dot_general(a, b, (dims, ((), ())), preferred_element_type=F32)]
    ppermute x0 -> x6, waiting for transfers between devices: none -> 18.9 us  [the longest x4 11.3 us: step_over(): return lax.ppermute(a, axis, pairs)]
    convert_element_type x2 -> x5, other arithmetic: 5.62 us -> 14.6 us  [plus(): return (a.astype(F32) + b.astype(F32)).astype(BF16)]
  transfers between devices with their start and end apart: 1 -> 9, of which waited for: 0 -> 3; matrix products, arithmetic and copies ran while one was open for 3% -> 13% of each run, Pallas kernels for 0% -> 15%
where the time goes in v3:
time: 731 us; the launch traced here: 725 us
  Pallas kernels  564 us (77%)
  other arithmetic  50.8 us (7%)
  matrix products  34.5 us (5%)
  local copies, waits for them, and re-layouts  30.4 us (4%)
  waiting for transfers between devices  19 us (3%)
  between operations  15 us (2%)
  starting transfers between devices  11.4 us (2%)
    pallas_call x2, Pallas kernels, reduce_scatter(): pl.pallas_call(functools.partial(scatter_kernel, n, nz, extras), out_shap...  208 us
    pallas_call x1, Pallas kernels, feed_forward(): pl.pallas_call(functools.partial(feed_forward_kernel, nz, early, late), o...  181 us
    pallas_call x2, Pallas kernels, gather(): pl.pallas_call(functools.partial(gather_kernel, n, nz, units, extras), ou...  138 us
    dot_general x7, matrix products, dot(): return lax.dot_general(a, b, (dims, ((), ())), preferred_element_type=F32)  34.5 us
    pallas_call x1, Pallas kernels, attend_backward(): pl.pallas_call(attend_backward_kernel, grid_spec=pltpu.PrefetchScalarGrid...  16.6 us
    convert_element_type x5, other arithmetic, plus(): return (a.astype(F32) + b.astype(F32)).astype(BF16)  14.6 us
  transfers between devices with their start and end apart: 9, of which 3 were waited for; matrix products, arithmetic and copies ran while one was open for 13% of the time, Pallas kernels for 15%

profile of v3, /device:TPU:0, one launch (start us, length us, event | category | flops | bytes accessed | tf_op | source)
XLA Modules:
  0.0 725.4 jit_solution(916014132872667474)
XLA Ops:
  13.3 69.2 %gather.12 = (bf16[2048,2048]{1,0:T(8,128)(2,1)}, f32[64,2048]{1,0:T(8,128)}, bf16[2048,256]{1,0:T(8,128)(2,1)}, bf16[128,2048]{1,0:T(8,128)(2,1)}) custom-call(bf16[512,512]{1,0:T(8,128)(2,1)} %refs_0_.2, f32[16,512]{1,0:T(8,128)} %pad_maximum_fusion.2.refs_1_, bf16[512,512]{1,0:T(8,128)(2,1)} %refs_2_.2, bf16[512,256]{1,0:T(8,128)(2,1)} %pad_maximum_fusion.1.refs_3_, ...), custom_call_target="tpu_custom_call" | custom-call | bytes 1048576 | tf_op jit(solution)/shard_map/gather/pallas_call | solution.py:387
  86.3 5.6 fusion
  93.4 10.2 %fusion.8 = f32[2048,384]{1,0:T(8,128)} fusion(bf16[2048,2048]{1,0:T(8,128)(2,1)} %get-tuple-element.46, f32[2048]{0:T(1024)S(1)} %bitcast.85, f32[2048]{0:T(1024)S(1)} %add_rsqrt_fusion, bf16[2048,256]{1,0:T(8,128)(2,1)S(1)} %copy-done.26, s32[384]{0:T(512)S(1)} %pad_add_fusion), kind=kOutput, calls=%fused_computation.19 | convolution fusion | flops 3641540608 | bytes 12600832 | tf_op jit(solution)/shard_map/dot_general | solution.py:28
  107.9 11.7 %attend_forward.1 = (bf16[2048,128]{1,0:T(8,128)(2,1)S(1)}, f32[8,1,512]{2,1,0:T(1,128)S(1)}) custom-call(s32[8]{0:T(128)S(1)} %and_select_fusion.low_ref, bf16[2048,256]{1,0:T(8,128)(2,1)S(1)} %pad_maximum_fusion.rot_ref, bf16[2048,128]{1,0:T(8,128)(2,1)S(1)} %slice.178.val_ref, s32[8,1,256]{2,1,0:T(1,128)S(1)} %bitcast.68), custom_call_target="tpu_custom_call" | custom-call | bytes 1048576 | tf_op jit(solution)/shard_map/attend_forward/pallas_call | solution.py:1059
  119.7 5.6 convolution_convert_fusion.1.refs_0_
  125.3 109.5 %reduce_scatter.2 = (f32[512,512]{1,0:T(8,128)S(1)}, bf16[2048,1024]{1,0:T(8,128)(2,1)}) custom-call(bf16[2048,2048]{1,0:T(8,128)(2,1)} %convolution_convert_fusion.1.refs_0_, bf16[512,2048]{1,0:T(8,128)(2,1)S(1)} %copy-done, bf16[512,2048]{1,0:T(8,128)(2,1)S(1)} %copy-done.1), custom_call_target="tpu_custom_call" | custom-call | bytes 1048576 | tf_op jit(solution)/shard_map/reduce_scatter/pallas_call | solution.py:589
  235.8 180.8 %feed_forward.1 = (bf16[2048,2048]{1,0:T(8,128)(2,1)}, bf16[2,2,4,512,512]{4,3,2,1,0:T(8,128)(2,1)}, f32[2048,128]{1,0:T(8,128)}, f32[256,512]{1,0:T(8,128)}, f3...) custom-call(bf16[512,512]{1,0:T(8,128)(2,1)} %multiply_convert_fusio, ...), custom_call_target="tpu_custom_call" | custom-call | bytes 1048576 | tf_op jit(solution)/shard_map/feed_forward/pallas_call | solution.py:884
  416.5 4.6 slice_bitcast_fusion
  431.3 68.9 %gather.13 = (bf16[2048,2048]{1,0:T(8,128)(2,1)}, bf16[2048,512]{1,0:T(8,128)(2,1)}) custom-call(bf16[512,512]{1,0:T(8,128)(2,1)} %get-tuple-element.132.refs_0_, bf16[256,2048]{1,0:T(8,128)(2,1)} %fusion.10.refs_1_), custom_call_target="tpu_custom_call" | custom-call | bytes 1048576 | tf_op jit(solution)/shard_map/gather/pallas_call | solution.py:387
  500.2 4.3 convert_element_type.211
  504.6 3.5 fusion.4
  508.1 4.5 all-to-all-start
  512.6 4.8 fusion.3
  517.5 7.3 %convolution_convert_fusion.5.grad_ref = bf16[2048,128]{1,0:T(8,128)(2,1)S(1)} fusion(bf16[2048,2048]{1,0:T(8,128)(2,1)} %get-tuple-element.64, bf16[128,2048]{1,0:T(8,128)(2,1)S(1)} %copy-done.30), kind=kOutput, calls=%fused_computation.21 | convolution fusion | flops 1074003968 | bytes 9437184 | tf_op jit(solution)/shard_map/dot_general | solution.py:28
  524.8 16.6 %attend_backward.1 = (f32[2048,256]{1,0:T(8,128)S(1)}, f32[2048,128]{1,0:T(8,128)S(1)}) custom-call(s32[8]{0:T(128)S(1)} %and_select_fusion.low_ref, bf16[2048,256]{1,0:T(8,128)(2,1)S(1)} %pad_maximum_fusion.rot_ref, bf16[2048,128]{1,0:T(8,128)(2,1)S(1)} %slice.178.val_ref, s32[8,1,256]{2,1,0:T(1,128)S(1)} %bitcast.69, ...), custom_call_target="tpu_custom_call" | custom-call | bytes 1048576 | tf_op jit(solution)/shard_map/attend_backward/pallas_call | solution.py:1091
  547.3 3.7 fusion.28
  551.6 5.7 convolution_convert_fusion.refs_0_
  558.6 98.9 %reduce_scatter.3 = (f32[512,512]{1,0:T(8,128)S(1)}, f32[16,128]{1,0:T(8,128)S(1)}, bf16[512,512]{1,0:T(8,128)(2,1)S(1)}, bf16[512,512]{1,0:T(8,128)(2,1)S(1)}, ...) custom-call(bf16[2048,2048]{1,0:T(8,128)(2,1)} %convolution_convert_, ...), custom_call_target="tpu_custom_call" | custom-call | bytes 1048576 | tf_op jit(solution)/shard_map/reduce_scatter/pallas_call | solution.py:589
  662.8 2.8 fusion.5
  679.0 10.5 %collective-permute-done.2 = bf16[2,512,512]{2,1,0:T(8,128)(2,1)} collective-permute-done((bf16[2,512,512]{2,1,0:T(8,128)(2,1)}, bf16[2,512,512]{2,1,0:T(8,128)(2,1)}, u32[]{:S(2)}, u32[]{:S(2)}) %collective-permute-start.2) | collective-permute-done | bytes 1048608 | tf_op jit(solution)/shard_map/ppermute | solution.py:1386
  691.6 2.9 collective-permute-start.3
  697.8 7.6 %collective-permute-done.6.other_ref = bf16[4,512,512]{2,1,0:T(8,128)(2,1)} collective-permute-done((bf16[4,512,512]{2,1,0:T(8,128)(2,1)}, bf16[4,512,512]{2,1,0:T(8,128)(2,1)}, u32[]{:S(2)}, u32[]{:S(2)}) %collective-permute-start.6) | collective-permute-done | bytes 2097184 | tf_op jit(solution)/shard_map/ppermute | solution.py:1378
  705.4 8.7 %assemble.1 = (f32[512,2048]{1,0:T(8,128)}, f32[512,2048]{1,0:T(8,128)}) custom-call(bf16[4,512,512]{2,1,0:T(8,128)(2,1)} %all-to-all-done.mine_ref, bf16[4,512,512]{2,1,0:T(8,128)(2,1)} %collective-permute-done.6.other_ref), custom_call_target="tpu_custom_call" | custom-call | bytes 1048576 | tf_op jit(solution)/shard_map/assemble/pallas_call | solution.py:1133
  715.0 3.3 fusion.16
  (170 shorter events, 59.1 us)
Async XLA Ops:
  7.2 75.4 %copy-start.31 = (s32[1,2048]{1,0:T(1,128)S(1)}, s32[1,2048]{1,0:T(1,128)}, u32[]{:S(2)}) copy-start(s32[1,2048]{1,0:T(1,128)} %param.15) | copy-start | bytes 24580
  7.2 228.6 %all-gather.3.cloned.1.call-start = ((), (), s32[]{:S(2)}) async-start(), calls=%async_computation.1 | async-start | bytes 8912896 | tf_op jit(solution)/shard_map/all_gather | solution.py:1275
  84.3 20.6 %copy-start.9 = (f32[2048,128]{1,0:T(8,128)}, f32[2048,128]{1,0:T(8,128)S(1)}, u32[]{:S(2)}) copy-start(f32[2048,128]{1,0:T(8,128)S(1)} %copy.89) | copy-start | bytes 3145732
  84.8 20.1 %copy-start.11 = (f32[2048,128]{1,0:T(8,128)}, f32[2048,128]{1,0:T(8,128)S(1)}, u32[]{:S(2)}) copy-start(f32[2048,128]{1,0:T(8,128)S(1)} %copy.87) | copy-start | bytes 3145732
  104.9 14.7 %copy-start.29 = (bf16[128,2048]{1,0:T(8,128)(2,1)S(1)}, bf16[128,2048]{1,0:T(8,128)(2,1)}, u32[]{:S(2)}) copy-start(bf16[128,2048]{1,0:T(8,128)(2,1)} %get-tuple-element.50) | copy-start | bytes 1572868
  125.3 109.5 %copy-start.14 = (bf16[512,512]{1,0:T(8,128)(2,1)S(1)}, bf16[512,512]{1,0:T(8,128)(2,1)}, u32[]{:S(2)}) copy-start(bf16[512,512]{1,0:T(8,128)(2,1)} %refs_0_.2) | copy-start | bytes 1572868
  125.3 109.5 %copy-start.32 = (f32[512]{0:T(512)S(1)}, f32[512]{0:T(512)}, u32[]{:S(2)}) copy-start(f32[512]{0:T(512)} %param.21) | copy-start | bytes 6148
  421.2 91.4 %collective-permute-start = (bf16[2,4,512,512]{3,2,1,0:T(8,128)(2,1)}, bf16[2,4,512,512]{3,2,1,0:T(8,128)(2,1)}, u32[]{:S(2)}, u32[]{:S(2)}) collective-permute-start(bf16[2,4,512,512]{3,2,1,0:T(8,128)(2,1)} %slice_bitcast_fusion), channel_id=1, source_target_pairs={{0,4},{4,0},{8,12},{12,8},{1,5},{5,1},{9,13},{13,9},{2,6},{6,2},{1... | collective-permute-start | bytes 12582920 | tf_op jit(solution)/shard_map/ppermute | solution.py:1386
  422.7 81.9 %collective-permute-start.5 = (bf16[2048,512]{1,0:T(8,128)(2,1)}, bf16[2048,512]{1,0:T(8,128)(2,1)}, u32[]{:S(2)}, u32[]{:S(2)}) collective-permute-start(bf16[2048,512]{1,0:T(8,128)(2,1)} %slice_bitcast_fusion.1), channel_id=1, source_target_pairs={{0,16},{16,0},{1,17},{17,1},{2,18},{18,2},{3,19},{19,3},{4,20},{20... | collective-permute-start | bytes 6291464 | tf_op jit(solution)/shard_map/ppermute | solution.py:1373
  508.1 152.6 %all-to-all-start = ((bf16[4,512,512]{2,1,0:T(8,128)(2,1)}), bf16[4,512,512]{2,1,0:T(8,128)(2,1)}, u32[]{:S(2)}, u32[]{:S(2)}) async-start(bf16[4,512,512]{2,1,0:T(8,128)(2,1)} %bitcast.73), calls=%async_computation | async-start | bytes 4194304 | tf_op jit(solution)/shard_map/all_to_all | solution.py:1375
  517.4 24.3 %copy-start.8 = (bf16[2,4,512,512]{3,2,1,0:T(8,128)(2,1)}, bf16[2,4,512,512]{3,2,1,0:T(8,128)(2,1)S(1)}, u32[]{:S(2)}) copy-start(bf16[2,4,512,512]{3,2,1,0:T(8,128)(2,1)S(1)} %fusion.3) | copy-start | bytes 12582916
  517.5 24.0 %copy-start.10 = (f32[2048,128]{1,0:T(8,128)S(1)}, f32[2048,128]{1,0:T(8,128)}, u32[]{:S(2)}) copy-start(f32[2048,128]{1,0:T(8,128)} %copy-done.9) | copy-start | bytes 3145732
  517.5 24.0 %copy-start.12 = (f32[2048,128]{1,0:T(8,128)S(1)}, f32[2048,128]{1,0:T(8,128)}, u32[]{:S(2)}) copy-start(f32[2048,128]{1,0:T(8,128)} %copy-done.11) | copy-start | bytes 3145732
  543.2 119.6 %collective-permute-start.1 = (bf16[4,512,512]{2,1,0:T(8,128)(2,1)}, bf16[4,512,512]{2,1,0:T(8,128)(2,1)}, u32[]{:S(2)}, u32[]{:S(2)}) collective-permute-start(bf16[4,512,512]{2,1,0:T(8,128)(2,1)} %slice_bitcast_fusion.2), channel_id=1, source_target_pairs={{0,8},{4,12},{8,0},{12,4},{1,9},{5,13},{9,1},{13,5},{2,10},{6,14},... | collective-permute-start | bytes 6291464 | tf_op jit(solution)/shard_map/ppermute | solution.py:1386
  660.7 36.5 %collective-permute-start.4 = (f32[8,128]{1,0:T(8,128)S(1)}, f32[8,128]{1,0:T(8,128)S(1)}, u32[]{:S(2)}, u32[]{:S(2)}) collective-permute-start(f32[8,128]{1,0:T(8,128)S(1)} %slice.131), channel_id=1, source_target_pairs={{0,16},{16,0},{1,17},{17,1},{2,18},{18,2},{3,19},{19,3},{4,20},{20... | collective-permute-start | bytes 12296 | tf_op jit(solution)/shard_map/ppermute | solution.py:1160
  660.7 7.2 copy-start.5
  660.8 7.2 copy-start.7
  660.8 44.7 %collective-permute-start.6 = (bf16[4,512,512]{2,1,0:T(8,128)(2,1)}, bf16[4,512,512]{2,1,0:T(8,128)(2,1)}, u32[]{:S(2)}, u32[]{:S(2)}) collective-permute-start(bf16[4,512,512]{2,1,0:T(8,128)(2,1)} %all-to-all-done.mine_ref), channel_id=1, source_target_pairs={{0,16},{16,0},{1,17},{17,1},{2,18},{18,2},{3,19},{19,3},{4,20},{20... | collective-permute-start | bytes 6291464 | tf_op jit(solution)/shard_map/ppermute | solution.py:1378
  668.0 21.5 %collective-permute-start.2 = (bf16[2,512,512]{2,1,0:T(8,128)(2,1)}, bf16[2,512,512]{2,1,0:T(8,128)(2,1)}, u32[]{:S(2)}, u32[]{:S(2)}) collective-permute-start(bf16[2,512,512]{2,1,0:T(8,128)(2,1)} %slice.147), channel_id=1, source_target_pairs={{0,1},{1,0},{2,3},{3,2},{4,5},{5,4},{6,7},{7,6},{8,9},{9,8},{10,11... | collective-permute-start | bytes 3145736 | tf_op jit(solution)/shard_map/ppermute | solution.py:1386
  677.9 37.1 %copy-start.35 = (f32[512]{0:T(512)S(1)}, f32[512]{0:T(512)}, u32[]{:S(2)}) copy-start(f32[512]{0:T(512)} %param.16) | copy-start | bytes 6148
  679.0 36.0 %copy-start.15 = (bf16[512,512]{1,0:T(8,128)(2,1)S(1)}, bf16[512,512]{1,0:T(8,128)(2,1)}, u32[]{:S(2)}) copy-start(bf16[512,512]{1,0:T(8,128)(2,1)} %refs_0_.2) | copy-start | bytes 1572868
  679.0 36.0 %copy-start.22 = (bf16[512,512]{1,0:T(8,128)(2,1)S(1)}, bf16[512,512]{1,0:T(8,128)(2,1)}, u32[]{:S(2)}) copy-start(bf16[512,512]{1,0:T(8,128)(2,1)} %param.25) | copy-start | bytes 1572868
  691.6 23.3 %collective-permute-start.3 = (bf16[512,512]{1,0:T(8,128)(2,1)}, bf16[512,512]{1,0:T(8,128)(2,1)}, u32[]{:S(2)}, u32[]{:S(2)}) collective-permute-start(bf16[512,512]{1,0:T(8,128)(2,1)} %fusion.22), channel_id=1, source_target_pairs={{0,2},{1,3},{2,0},{3,1},{4,6},{5,7},{6,4},{7,5},{8,10},{9,11},{10,... | collective-permute-start | bytes 1572872 | tf_op jit(solution)/shard_map/ppermute | solution.py:1386
  697.2 17.8 %copy-start.17 = (f32[512,512]{1,0:T(8,128)S(1)}, f32[512,512]{1,0:T(8,128)}, u32[]{:S(2)}) copy-start(f32[512,512]{1,0:T(8,128)} %copy-done.16) | copy-start | bytes 3145732
  (26 other events, 95.1 us)
Sparse Core Ops, SparseCore 0:
  82.7 101.0 all-gather.2

commit v4 on v3

--- a/solution.py
+++ b/solution.py
@@ -216,16 +216,19 @@
         self.right, self.left, self.over_x, self.to_core = 0, nz - 1, 2 * (nz - 1), 3 * nz - 2
 
     def own_part(self, u):
-        i, start, size = self.units[u]
+        i, start, size, reach = self.units[u]
         return self.ins[i].at[pl.ds(start, size), :]
 
     def slot(self, u, row, col):
-        i, start, size = self.units[u]
+        i, start, size, reach = self.units[u]
         b0, b1 = self.ins[i].shape
         return self.outs[i].at[
-            pl.ds(pl.multiple_of(row * b0 + start, size), size),
+            pl.ds(pl.multiple_of((row if reach else 0) * b0 + start, size), size),
             pl.ds(pl.multiple_of(col * b1, b1), b1),
         ]
+
+    def reaches(self, u):
+        return self.units[u][3]
 
     def copy(self, u, src, row, col, where, device):
         return pltpu.make_async_remote_copy(
@@ -264,12 +267,16 @@
             def _():
                 self.own(u, self.left, (g, r, z - 1)).start()
 
-            self.own(u, self.over_x, (g, rx, z)).start()
+            if self.reaches(u):
+                self.own(u, self.over_x, (g, rx, z)).start()
         for u in every:
-            self.own(u, self.to_core, (g, rc, z)).start()
+            if self.reaches(u):
+                self.own(u, self.to_core, (g, rc, z)).start()
             self.local(u).start()
 
     def from_x(self, u, k):
+        if not self.reaches(u):
+            return
         g, r, z, rc, rx, rxc = self.at
         to_core, nz = self.to_core, self.nz
         for near, col, where in (
@@ -298,14 +305,20 @@
                     def _():
                         self.forward(u, r, col, flow + k, device).start()
 
-                self.forward(u, r, col, self.over_x + 1 + self.rank(col), (g, rx, z)).start()
-                self.forward(u, r, col, self.to_core + 2 + self.rank(col), (g, rc, z)).start()
+                if self.reaches(u):
+                    self.forward(u, r, col, self.over_x + 1 + self.rank(col), (g, rx, z)).start()
+                    self.forward(u, r, col, self.to_core + 2 + self.rank(col), (g, rc, z)).start()
+
+    def from_core(self, u, row):
+        g, r, z, rc, rx, rxc = self.at
+        for col in range(self.nz):
+            self.forward(u, row, col, self.to_core, (g, rc, z)).wait_recv()
 
     def finish(self, u):
         g, r, z, rc, rx, rxc = self.at
-        for col in range(self.nz):
-            self.forward(u, rc, col, self.to_core, (g, rc, z)).wait_recv()
-            self.forward(u, rxc, col, self.to_core, (g, rc, z)).wait_recv()
+        if self.reaches(u):
+            self.from_core(u, rc)
+            self.from_core(u, rxc)
         self.local(u).wait()
 
     def sent(self, u):
@@ -319,7 +332,7 @@
                 pl.when(self.has_right & (z - where >= 0))(wait)
             elif where < self.over_x:
                 pl.when(self.has_left & (z + (where - self.left) < self.nz))(wait)
-            else:
+            elif self.reaches(u):
                 wait()
 
 
@@ -376,18 +389,22 @@
     return [item for some in lists for item in some]
 
 
-def gather(arrays, collective_id, extras=()):
+def gather(arrays, collective_id, extras=(), along_col=()):
+    reach = [True] * len(arrays) + [False] * len(along_col)
+    arrays = list(arrays) + list(along_col)
     n, nz = len(arrays), lax.axis_size("col")
     units = []
     for i, a in enumerate(arrays):
         parts = 2 if a.shape[0] % 256 == 0 else 1
-        units += [(i, m * (a.shape[0] // parts), a.shape[0] // parts) for m in range(parts)]
+        size = a.shape[0] // parts
+        units += [(i, m * size, size, reach[i]) for m in range(parts)]
     anywhere = pl.BlockSpec(memory_space=pl.ANY)
     extra_in, extra_out = flat(e.arrays for e in extras), flat(e.outs for e in extras)
     outs = pl.pallas_call(
         functools.partial(gather_kernel, n, nz, units, extras),
         out_shape=[
-            jax.ShapeDtypeStruct((a.shape[0] * NR, a.shape[1] * nz), a.dtype) for a in arrays
+            jax.ShapeDtypeStruct((a.shape[0] * (NR if far else 1), a.shape[1] * nz), a.dtype)
+            for a, far in zip(arrays, reach)
         ]
         + extra_out,
         in_specs=[anywhere] * (n + len(extra_in)),
@@ -606,104 +623,115 @@
 
 def feed_forward_kernel(
     nz,
-    early,
     late,
     raw_ref,
     inverse_ref,
     gate_up_ref,
+    down_ref,
     grad_ref,
     *refs,
 ):
-    n_in, n_out = sum(len(e.arrays) for e in early), sum(len(e.outs) for e in early + late)
-    raw_all, down_out, scale_out, grad_two_a, grad_two_b, inner_out, pair_grad, down_grad = refs[
-        n_in : n_in + 8
-    ]
-    down_ref = refs[n_in + 8]
-    rest = refs[n_in + 8 + n_out :]
+    n_out = sum(len(e.outs) for e in late)
+    raw_all, scale_out, grad_two_a, grad_two_b, inner_out, down_grad = refs[:6]
+    down_outs, pair_grads = refs[6:8], refs[8 : 8 + (2 if late else 1)]
+    n_own = 8 + len(pair_grads)
+    rest = refs[n_own + n_out :]
     gate_up, down, x_buf, g_buf, d_buf, unit_a, unit_b, inner, hidden_t, scaled = rest[:10]
     left_buf, right_buf, pair_buf, down_buf = rest[10:14]
     load_sem, in_sem, out_sem, tile_sem, done_sem = rest[14:19]
     sems, rest = rest[19:22], rest[22:]
-    units = [(0, 0, raw_ref.shape[0] // 2), (0, raw_ref.shape[0] // 2, raw_ref.shape[0] // 2)]
-    size = units[0][2]
+    size = raw_ref.shape[0] // 2
+    units = [(0, 0, size, True), (0, size, size, True)]
     gather_work = Gather(nz, units, [raw_ref], [raw_all], sems)
     works = []
     for source, out in ((unit_a, grad_two_a), (unit_b, grad_two_b), (inner, inner_out)):
         works.append(Scatter(nz, source, out, rest[:5], rest[5:11], False))
         rest = rest[11:]
-    bind_extras(
-        early + late,
-        list(refs[:n_in]) + [down_grad] * len(late),
-        refs[n_in + 8 : n_in + 8 + n_out],
-        rest,
-    )
+    bind_extras(late, [down_grad] * len(late), refs[n_own : n_own + n_out], rest)
     g, r, z, rc, rx, rxc = place()
-    devices = greetings(early + late, nz, [(g, rc, z), (g, rx, z)])
+    devices = [(g, rc, z), (g, rx, z)] + [(g, r, lax.rem(z + k, nz)) for k in range(1, nz)]
+    devices = greetings(late, nz, devices)
     barrier = greet(devices)
     pl.semaphore_wait(barrier, len(devices))
 
     gather_work.begin()
     load_gate_up = pltpu.make_async_copy(gate_up_ref, gate_up, load_sem.at[0])
     load_gate_up.start()
-    load_down = pltpu.make_async_copy(down_ref, down, load_sem.at[1])
-    for extra in early:
-        extra.start(nz)
+    load_down = [
+        pltpu.make_async_copy(
+            down_ref.at[col],
+            down.at[:, pl.ds(col * raw_ref.shape[1], raw_ref.shape[1])],
+            load_sem.at[1 + col],
+        )
+        for col in range(nz)
+    ]
+    for copy in load_down:
+        copy.start()
     inner[...] = jnp.zeros_like(inner)
-    for k in range(1, nz):
+    for k in range(1, nz - 1):
         for u in range(2):
             gather_work.from_z(u, k)
             gather_work.from_x(u, k - 1)
-        if k > 1:
-            for extra in early:
-                extra.step(k - 1, nz)
-    gather_work.from_x(0, nz - 1)
-    for extra in early:
-        extra.step(nz - 1, nz)
     ffn, width = down.shape
     tile, block = left_buf.shape[2], raw_ref.shape[1]
     tiles = width // tile
-    parts = pair_grad.shape[0]
+    parts = len(pair_grads)
+    turns = [
+        (0, 0, 0),
+        (0, 1, 0),
+        (1, 0, 0),
+        (1, 1, 0),
+        (0, 0, 1),
+        (0, 1, 1),
+        (1, 0, 1),
+        (1, 1, 1),
+    ]
+
+    def row_of(turn):
+        return ((r, rx), (rc, rxc))[turns[turn][1]][turns[turn][2]]
 
     def tokens_of(u, row):
-        return pl.ds(row * 2 * size + u * size, size)
-
-    def fetch(u, row):
-        slot = (u * NR + row) % 2
+        return pl.ds(pl.multiple_of(row * 2 * size + u * size, size), size)
+
+    def fetch(turn):
+        slot, u, row = turn % 2, turns[turn][0], row_of(turn)
         return [
             pltpu.make_async_copy(
                 raw_all.at[tokens_of(u, row), :], x_buf.at[slot], in_sem.at[0, slot]
             ),
-        ] + [
             pltpu.make_async_copy(
-                grad_ref.at[row * nz + col, pl.ds(u * size, size), :],
-                g_buf.at[slot, :, pl.ds(col * block, block)],
-                in_sem.at[1 + col, slot],
-            )
-            for col in range(nz)
+                grad_ref.at[tokens_of(u, row), :], g_buf.at[slot], in_sem.at[1, slot]
+            ),
         ]
 
-    def put(u, row):
-        slot = (u * NR + row) % 2
-        same_core, same_x = lax.rem(r + row, 2), lax.rem(r // 2 + row // 2, 2)
+    def put(turn):
+        slot, (u, core, side) = turn % 2, turns[turn]
         return [
             pltpu.make_async_copy(
                 d_buf.at[slot, :, pl.ds(pl.multiple_of(col * block, block), block)],
-                down_out.at[same_core, same_x, step, pl.ds(u * size, size), :],
+                down_outs[core].at[side, step, pl.ds(u * size, size), :],
                 out_sem.at[step, slot],
             )
             for step, col in enumerate(works[0].order)
         ]
 
-    def chunk(u, row):
-        slot = (u * NR + row) % 2
-        for copy in fetch(u, row):
+    def begin(turn):
+        u, core, side = turns[turn]
+        if core == 1:
+            gather_work.from_core(u, row_of(turn))
+        elif side == 0:
+            gather_work.local(u).wait()
+        for copy in fetch(turn):
+            copy.start()
+
+    def chunk(turn):
+        slot, (u, core, side), row = turn % 2, turns[turn], row_of(turn)
+        for copy in fetch(turn):
             copy.wait()
-        if row + 1 < NR:
-            for copy in fetch(u, row + 1):
-                copy.start()
-        if u * NR + row >= 2:
-            before = u * NR + row - 2
-            for copy in put(before // NR, before % NR):
+        if turn + 1 < len(turns):
+            begin(turn + 1)
+        if turn >= 2:
+            for copy in put(turn - 2):
                 copy.wait()
         here = tokens_of(u, row)
         unit = (unit_a, unit_b)[u]
@@ -718,7 +746,7 @@
         hidden = (act * up).astype(BF16)
         hidden_t[:, here] = hidden.T
         d_buf[slot] = dot(hidden, down[...], ((1,), (0,))).astype(BF16)
-        for copy in put(u, row):
+        for copy in put(turn):
             copy.start()
         grad_hidden = dot(g_buf[slot], down[...], ((1,), (1,)))
         grad_gate = grad_hidden * up * sig * (1.0 + gate * (1.0 - sig))
@@ -730,32 +758,23 @@
             at_line = u * (size // 128) + m
             pick = lax.broadcasted_iota(jnp.int32, line.shape, 0) == at_line
             for col in range(nz):
-                part = (slice(row * 8, row * 8 + 8), slice(col * 128, col * 128 + 128))
+                part = (pl.ds(pl.multiple_of(row * 8, 8), 8), pl.ds(col * 128, 128))
                 inner[part] = jnp.where(pick, line, inner[part])
         scaled[here, :ffn] = (grad_gate * scale).astype(BF16)
         scaled[here, ffn:] = (grad_up * scale).astype(BF16)
         back = dot(grad_gate.astype(BF16), gate_up[:, :ffn], ((1,), (1,)))
         back = back + dot(grad_up.astype(BF16), gate_up[:, ffn:], ((1,), (1,)))
-        unit[row * size : (row + 1) * size, :] = back.astype(BF16)
+        unit[pl.ds(pl.multiple_of(row * size, size), size), :] = back.astype(BF16)
 
     def tile_in(kind, n):
         slot = lax.rem(n, 2)
-        if kind == 1:
-            return [
-                pltpu.make_async_copy(
-                    raw_all.at[:, pl.ds(pl.multiple_of(n * tile, tile), tile)],
-                    left_buf.at[slot],
-                    tile_sem.at[NR, slot],
-                )
-            ]
-        col, inside = n // (block // tile), lax.rem(n, block // tile)
+        source, buf = ((grad_ref, right_buf), (raw_all, left_buf))[kind]
         return [
             pltpu.make_async_copy(
-                grad_ref.at[row * nz + col, :, pl.ds(pl.multiple_of(inside * tile, tile), tile)],
-                right_buf.at[slot, pl.ds(row * 2 * size, 2 * size), :],
-                tile_sem.at[row, slot],
+                source.at[:, pl.ds(pl.multiple_of(n * tile, tile), tile)],
+                buf.at[slot],
+                tile_sem.at[kind, slot],
             )
-            for row in range(NR)
         ]
 
     def tile_out(kind, n):
@@ -763,16 +782,22 @@
         where = pl.ds(pl.multiple_of(n * tile, tile), tile)
         half = ffn // parts
         copies = []
-        for h in range(parts):
-            part = lax.rem(h + g, 2) if parts == 2 else 0
+        for part in range(parts):
+            h = lax.rem(part + g, 2) if parts == 2 else 0
             if kind == 0:
-                copies.append((down_buf.at[slot, pl.ds(h * half, half), :], down_grad.at[part, :, where]))
+                copies.append(
+                    (
+                        down_buf.at[slot, pl.ds(pl.multiple_of(h * half, half), half), :],
+                        down_grad.at[part, :, where],
+                    )
+                )
             else:
                 for m in range(2):
+                    start = pl.multiple_of(m * ffn + h * half, half)
                     copies.append(
                         (
-                            pair_buf.at[slot, :, pl.ds(m * ffn + h * half, half)],
-                            pair_grad.at[part, where, pl.ds(m * half, half)],
+                            pair_buf.at[slot, :, pl.ds(start, half)],
+                            pair_grads[part].at[where, pl.ds(m * half, half)],
                         )
                     )
         return [
@@ -806,39 +831,39 @@
 
         lax.fori_loop(low, high, one, 0)
 
-    gather_work.finish(0)
-    for copy in fetch(0, 0):
-        copy.start()
-    for extra in early:
-        extra.finish(nz)
-    load_down.start()
+    first, second, third = works
+    gather_work.from_z(0, nz - 1)
+    gather_work.from_x(0, nz - 2)
+    load_gate_up.wait()
+    for copy in load_down:
+        copy.wait()
+    begin(0)
+    chunk(0)
+    gather_work.from_z(1, nz - 1)
+    gather_work.from_x(1, nz - 2)
+    chunk(1)
+    gather_work.from_x(0, nz - 1)
+    chunk(2)
     gather_work.from_x(1, nz - 1)
-    load_gate_up.wait()
-    load_down.wait()
-    for row in range(NR):
-        chunk(0, row)
-    first, second, third = works
+    chunk(3)
+    chunk(4)
+    chunk(5)
     first.begin()
-    gather_work.finish(1)
-    for copy in fetch(1, 0):
-        copy.start()
+    chunk(6)
     for step in range(4):
         first.to_x(step)
-    chunk(1, 0)
-    chunk(1, 1)
-    first.to_z(0)
-    chunk(1, 2)
-    first.to_z(1)
     for copy in tile_in(0, 0) + tile_in(1, 0):
         copy.start()
-    chunk(1, 3)
+    chunk(7)
     second.begin()
     third.begin()
-    first.to_z(2)
+    first.to_z(0)
     for step in range(4):
         second.to_x(step)
     for step in range(4):
         third.to_x(step)
+    first.to_z(1)
+    first.to_z(2)
     first.to_z(3)
     third.to_z(0)
     third.to_z(1)
@@ -862,8 +887,8 @@
         gather_work.sent(u)
     for work in works:
         work.finish()
-    for row in (NR - 2, NR - 1):
-        for copy in put(1, row):
+    for turn in (len(turns) - 2, len(turns) - 1):
+        for copy in put(turn):
             copy.wait()
     for n in (tiles - 2, tiles - 1):
         for copy in tile_out(1, n):
@@ -872,7 +897,7 @@
         extra.finish(nz)
 
 
-def feed_forward(raw, inverse, gate_up, grad, collective_id, early, late):
+def feed_forward(raw, inverse, gate_up, down, grad, collective_id, late):
     nz = lax.axis_size("col")
     width, ffn = gate_up.shape[0], gate_up.shape[1] // 2
     tokens, size, tile = raw.shape[0] * NR, raw.shape[0] // 2, 256
@@ -880,22 +905,22 @@
     anywhere, vmem = pl.BlockSpec(memory_space=pl.ANY), pl.BlockSpec(memory_space=pltpu.VMEM)
     shape = jax.ShapeDtypeStruct
     scatters = [((NR * size, width), BF16)] * 2 + [((NR * 8, nz * 128), F32)]
-    extra_in, extra_out = flat(e.arrays for e in early), flat(e.outs for e in early + late)
+    extra_out = flat(e.outs for e in late)
     outs = pl.pallas_call(
-        functools.partial(feed_forward_kernel, nz, early, late),
+        functools.partial(feed_forward_kernel, nz, late),
         out_shape=[
             shape((tokens, width), BF16),
-            shape((2, 2, nz) + raw.shape, BF16),
             shape((tokens, 128), F32),
             shape((size, raw.shape[1]), F32),
             shape((size, raw.shape[1]), F32),
             shape((8, 128), F32),
-            shape((parts, width, 2 * ffn // parts), BF16),
             shape((parts, ffn // parts, width), BF16),
         ]
+        + [shape((2, nz) + raw.shape, BF16)] * 2
+        + [shape((width, 2 * ffn // parts), BF16)] * parts
         + extra_out,
-        in_specs=[anywhere, vmem, anywhere, anywhere] + [anywhere] * len(extra_in),
-        out_specs=[anywhere] * 2 + [vmem] * 4 + [anywhere] * (2 + len(extra_out)),
+        in_specs=[anywhere, vmem] + [anywhere] * 3,
+        out_specs=[anywhere] + [vmem] * 4 + [anywhere] * (3 + parts + len(extra_out)),
         scratch_shapes=[
             pltpu.VMEM(gate_up.shape, BF16),
             pltpu.VMEM((ffn, width), BF16),
@@ -911,22 +936,22 @@
             pltpu.VMEM((2, tokens, tile), BF16),
             pltpu.VMEM((2, tile, 2 * ffn), BF16),
             pltpu.VMEM((2, ffn, tile), BF16),
-            DMA((2,)),
-            DMA((1 + nz, 2)),
+            DMA((1 + nz,)),
+            DMA((2, 2)),
             DMA((nz, 2)),
-            DMA((NR + 1, 2)),
+            DMA((2, 2)),
             DMA((2, 2 * parts, 2)),
         ]
         + gather_sems(2, nz)
         + flat(flat(scatter_scratch(s, t, nz, False)) for s, t in scatters)
-        + flat(e.scratch for e in early + late),
+        + flat(e.scratch for e in late),
         compiler_params=pltpu.CompilerParams(
             collective_id=collective_id, has_side_effects=True, vmem_limit_bytes=58 * 2**20
         ),
         cost_estimate=SHORT,
         name="feed_forward",
-    )(raw, inverse, gate_up, grad, *extra_in)
-    return outs[:8], outs[8:]
+    )(raw, inverse, gate_up, down, grad)
+    return outs[1:6], outs[6:8], outs[8 : 8 + parts], outs[8 + parts :]
 
 
 def swap64(v):
@@ -959,14 +984,48 @@
     return (key <= query) & (key >= first)
 
 
-def attend_forward_kernel(low_ref, rot_ref, val_ref, first_ref, out_ref, log_ref, keys_ref):
+def attend_forward_kernel(
+    low_ref,
+    x_ref,
+    gain_ref,
+    natural_ref,
+    permutation_ref,
+    weight_ref,
+    cosine_ref,
+    sine_ref,
+    first_ref,
+    normed_ref,
+    scale_ref,
+    rot_ref,
+    val_ref,
+    out_ref,
+    log_ref,
+    part_ref,
+    joint_ref,
+    keys_ref,
+):
     i = pl.program_id(0)
 
     @pl.when(i == 0)
     def _():
-        keys_ref[...] = swap64(rot_ref[...])
-
-    query = stack_heads(rot_ref[pl.ds(pl.multiple_of(i * BQ, BQ), BQ), :], 32)
+        joint_ref[...] = dot(natural_ref[...], permutation_ref[...], ((1,), (0,))).astype(BF16)
+
+    here = pl.ds(pl.multiple_of(i * BQ, BQ), BQ)
+    x = x_ref[...].astype(F32)
+    scale = lax.rsqrt(jnp.sum(x * x, axis=1, keepdims=True) / x.shape[1] + NORM_EPS)
+    normed = (x * scale * gain_ref[...]).astype(BF16)
+    normed_ref[...] = normed
+    scale_ref[...] = jnp.broadcast_to(scale, scale_ref.shape)
+    pre = dot(normed, joint_ref[...], ((1,), (0,)))
+    one, two = pre[:, :128], pre[:, 128:256]
+    cosine, sine = cosine_ref[...], sine_ref[...]
+    rot = jnp.concatenate([one * cosine - two * sine, two * cosine + one * sine], axis=1)
+    rot = rot.astype(BF16)
+    rot_ref[here, :] = rot
+    keys_ref[here, :] = swap64(rot)
+    val_ref[here, :] = pre[:, 256:].astype(BF16)
+
+    query = stack_heads(rot, 32)
     first = jnp.concatenate([first_ref[0], first_ref[0]], axis=1)
 
     def step(j, state):
@@ -988,38 +1047,55 @@
     )
     top, total, acc = lax.fori_loop(low_ref[i], i, step, step(i, state))
     acc = (acc / total).T
-    out_ref[...] = jnp.where(lane_in((BQ, 128), 0, 64), acc[:BQ], acc[BQ:]).astype(BF16)
+    out = jnp.where(lane_in((BQ, 128), 0, 64), acc[:BQ], acc[BQ:]).astype(BF16)
+    out_ref[...] = out
     log_ref[0] = top + jnp.log(total)
+    part_ref[...] = dot(out, weight_ref[...], ((1,), (0,))).astype(BF16)
 
 
 def attend_backward_kernel(
     low_ref,
+    incoming_ref,
+    normed_ref,
+    natural_ref,
+    permutation_ref,
+    weight_ref,
+    cosine_ref,
+    sine_ref,
     rot_ref,
     val_ref,
     first_ref,
     log_ref,
     out_ref,
-    grad_ref,
-    grot_ref,
-    gval_ref,
+    part_ref,
+    natural_grad_ref,
+    weight_grad_ref,
+    inner_ref,
     keys_ref,
     gkey_ref,
+    gval_ref,
+    wgrad_ref,
 ):
-    i, n = pl.program_id(0), pl.num_programs(0)
-
-    @pl.when(i == 0)
+    n = pl.num_programs(0)
+    i = n - 1 - pl.program_id(0)
+
+    @pl.when(i == n - 1)
     def _():
         keys_ref[...] = swap64(rot_ref[...])
         gkey_ref[...] = jnp.zeros_like(gkey_ref)
         gval_ref[...] = jnp.zeros_like(gval_ref)
+        wgrad_ref[...] = jnp.zeros_like(wgrad_ref)
+        natural_grad_ref[...] = jnp.zeros_like(natural_grad_ref)
 
     here = pl.ds(pl.multiple_of(i * BQ, BQ), BQ)
+    incoming, out = incoming_ref[...], out_ref[...]
+    grad = dot(incoming, weight_ref[...], ((1,), (1,))).astype(BF16)
+    wgrad_ref[...] += dot(out, incoming, ((0,), (0,)))
     query = stack_heads(rot_ref[here, :], 32)
-    grad = grad_ref[...]
     grads = stack_heads(grad, 64)
     first = jnp.concatenate([first_ref[0], first_ref[0]], axis=1)
     log_row = log_ref[0]
-    product = (grad.astype(F32) * out_ref[...].astype(F32)).T
+    product = (grad.astype(F32) * out.astype(F32)).T
     center = jnp.concatenate(
         [
             jnp.sum(product[:64], axis=0, keepdims=True),
@@ -1040,75 +1116,124 @@
         return acc + dot(grad_scores, key, ((0,), (0,)))
 
     acc = lax.fori_loop(low_ref[i], i + 1, step, jnp.zeros((2 * BQ, 256), F32))
-    grot_ref[here, :] = jnp.where(lane_in((BQ, 256), 0, 32), acc[:BQ], acc[BQ:]) * SCORE_SCALE
-
-    @pl.when(i == n - 1)
+    own = jnp.where(lane_in((BQ, 256), 0, 32), acc[:BQ], acc[BQ:])
+    grot = jnp.where(lane_in((BQ, 256), 0, 64), own, swap64(gkey_ref[here, :])) * SCORE_SCALE
+    gval = gval_ref[here, :]
+    total = jnp.sum(grot * rot_ref[here, :].astype(F32), axis=1, keepdims=True)
+    total = total + jnp.sum(gval * val_ref[here, :].astype(F32), axis=1, keepdims=True)
+    turned = jnp.broadcast_to(total, (BQ, 128)).T
+    for m in range(BQ // 128):
+        inner_ref[pl.ds(i * (BQ // 128) + m, 1), :] = turned[:1, m * 128 : (m + 1) * 128]
+    one, two = grot[:, :128], grot[:, 128:]
+    cosine, sine = cosine_ref[...], sine_ref[...]
+    pre = jnp.concatenate([one * cosine + two * sine, two * cosine - one * sine, gval], axis=1)
+    natural = dot(pre.astype(BF16), permutation_ref[...], ((1,), (1,))).astype(BF16)
+    part_ref[...] = dot(natural, natural_ref[...], ((1,), (1,))).astype(BF16)
+    natural_grad_ref[...] += dot(normed_ref[...], natural, ((0,), (0,)))
+
+    @pl.when(i == 0)
     def _():
-        def put(rows):
-            moved = swap64(gkey_ref[rows, :] * SCORE_SCALE)
-            grot_ref[rows, :] = jnp.where(lane_in((BQ, 256), 0, 64), grot_ref[rows, :], moved)
-
-        in_rows(grot_ref.shape[0], BQ, put)
-
-
-def attend_forward(low, rot, val, first):
-    t = rot.shape[0]
+        weight_grad_ref[...] = wgrad_ref[...].astype(BF16)
+
+
+def attend_forward(low, x, gain, natural, permutation, weight, cosine, sine, first):
+    t, width = x.shape
     n = t // BQ
-    whole = lambda i, low: (0, 0)
+    some = lambda i, low: (i, 0)
     row = lambda i, low: (i, 0, 0)
+    whole = lambda a: pl.BlockSpec(a.shape, lambda i, low: (0, 0))
+    shape = jax.ShapeDtypeStruct
     return pl.pallas_call(
         attend_forward_kernel,
         grid_spec=pltpu.PrefetchScalarGridSpec(
             num_scalar_prefetch=1,
             grid=(n,),
             in_specs=[
-                pl.BlockSpec((t, 256), whole),
-                pl.BlockSpec((t, 128), whole),
+                pl.BlockSpec((BQ, width), some),
+                whole(gain),
+                whole(natural),
+                whole(permutation),
+                whole(weight),
+                pl.BlockSpec((BQ, 128), some),
+                pl.BlockSpec((BQ, 128), some),
                 pl.BlockSpec((1, 1, BQ), row),
             ],
             out_specs=[
-                pl.BlockSpec((BQ, 128), lambda i, low: (i, 0)),
+                pl.BlockSpec((BQ, width), some),
+                pl.BlockSpec((BQ, 128), some),
+                pl.BlockSpec((t, 256), lambda i, low: (0, 0)),
+                pl.BlockSpec((t, 128), lambda i, low: (0, 0)),
+                pl.BlockSpec((BQ, 128), some),
                 pl.BlockSpec((1, 1, 2 * BQ), row),
+                pl.BlockSpec((BQ, width), some),
             ],
-            scratch_shapes=[pltpu.VMEM((t, 256), BF16)],
+            scratch_shapes=[
+                pltpu.VMEM((width, permutation.shape[1]), BF16),
+                pltpu.VMEM((t, 256), BF16),
+            ],
         ),
         out_shape=[
-            jax.ShapeDtypeStruct((t, 128), BF16),
-            jax.ShapeDtypeStruct((n, 1, 2 * BQ), F32),
+            shape((t, width), BF16),
+            shape((t, 128), F32),
+            shape((t, 256), BF16),
+            shape((t, 128), BF16),
+            shape((t, 128), BF16),
+            shape((n, 1, 2 * BQ), F32),
+            shape((t, width), BF16),
         ],
-        compiler_params=pltpu.CompilerParams(vmem_limit_bytes=40 * 2**20),
+        compiler_params=pltpu.CompilerParams(vmem_limit_bytes=48 * 2**20),
         cost_estimate=SHORT,
         name="attend_forward",
-    )(low, rot, val, first)
-
-
-def attend_backward(low, rot, val, first, log_all, out, grad):
-    t = rot.shape[0]
+    )(low, x, gain, natural, permutation, weight, cosine, sine, first)
+
+
+def attend_backward(
+    low, incoming, normed, natural, permutation, weight, cosine, sine, rot, val, first, log_all, out
+):
+    t, width = incoming.shape
     n = t // BQ
-    whole = lambda i, low: (0, 0)
-    row = lambda i, low: (i, 0, 0)
-    some = lambda i, low: (i, 0)
+    some = lambda s, low: (n - 1 - s, 0)
+    row = lambda s, low: (n - 1 - s, 0, 0)
+    whole = lambda a: pl.BlockSpec(a.shape, lambda s, low: (0, 0))
+    shape = jax.ShapeDtypeStruct
+    outs = [
+        shape((t, width), BF16),
+        shape(natural.shape, F32),
+        shape(weight.shape, BF16),
+        shape((t // 128, 128), F32),
+    ]
     return pl.pallas_call(
         attend_backward_kernel,
         grid_spec=pltpu.PrefetchScalarGridSpec(
             num_scalar_prefetch=1,
             grid=(n,),
             in_specs=[
-                pl.BlockSpec((t, 256), whole),
-                pl.BlockSpec((t, 128), whole),
+                pl.BlockSpec((BQ, width), some),
+                pl.BlockSpec((BQ, width), some),
+                whole(natural),
+                whole(permutation),
+                whole(weight),
+                pl.BlockSpec((BQ, 128), some),
+                pl.BlockSpec((BQ, 128), some),
+                whole(rot),
+                whole(val),
                 pl.BlockSpec((1, 1, BQ), row),
                 pl.BlockSpec((1, 1, 2 * BQ), row),
                 pl.BlockSpec((BQ, 128), some),
-                pl.BlockSpec((BQ, 128), some),
             ],
-            out_specs=[pl.BlockSpec((t, 256), whole), pl.BlockSpec((t, 128), whole)],
-            scratch_shapes=[pltpu.VMEM((t, 256), BF16), pltpu.VMEM((t, 256), F32)],
+            out_specs=[pl.BlockSpec((BQ, width), some)] + [whole(o) for o in outs[1:]],
+            scratch_shapes=[
+                pltpu.VMEM((t, 256), BF16),
+                pltpu.VMEM((t, 256), F32),
+                pltpu.VMEM((t, 128), F32),
+                pltpu.VMEM(weight.shape, F32),
+            ],
         ),
-        out_shape=[jax.ShapeDtypeStruct((t, 256), F32), jax.ShapeDtypeStruct((t, 128), F32)],
-        compiler_params=pltpu.CompilerParams(vmem_limit_bytes=40 * 2**20),
+        out_shape=outs,
+        compiler_params=pltpu.CompilerParams(vmem_limit_bytes=48 * 2**20),
         cost_estimate=SHORT,
         name="attend_backward",
-    )(low, rot, val, first, log_all, out, grad)
+    )(low, incoming, normed, natural, permutation, weight, cosine, sine, rot, val, first, log_all, out)
 
 
 def assemble_kernel(mine_ref, other_ref, gate_ref, up_ref):
@@ -1137,7 +1262,7 @@
         out_specs=[out, out],
         out_shape=[jax.ShapeDtypeStruct((depth, 2 * nz * part), F32)] * 2,
         compiler_params=pltpu.CompilerParams(vmem_limit_bytes=40 * 2**20),
-        cost_estimate=SHORT,
+        cost_estimate=pl.CostEstimate(flops=0, bytes_accessed=24 * 2**20, transcendentals=0),
         name="assemble",
     )(mine, other)
 
@@ -1205,9 +1330,8 @@
     offset = (places - first).astype(F32)
     half_width = HEAD_SIZE // 2
     inverse = ROPE_BASE ** (-(2.0 * jnp.arange(half_width, dtype=F32)) / HEAD_SIZE)
-    angles = offset[:, None] * inverse[None, :]
-    cosine = jnp.tile(jnp.cos(angles), (1, 4))
-    sine = jnp.tile(jnp.sin(angles), (1, 4))
+    angles = offset[:, None] * jnp.tile(inverse, 4)[None, :]
+    cosine, sine = jnp.cos(angles), jnp.sin(angles)
 
     names = jnp.arange(4 * HEAD_SIZE).reshape(4, 2, half_width)
     order = jnp.concatenate(
@@ -1261,31 +1385,23 @@
         [(heads, width)],
         share,
     )
-    (x_all, gain_all), (natural, out_rows) = gather(
+    (x_all, gain_all, grad_col), (natural, out_rows) = gather(
         [
             hidden_in,
             jnp.concatenate([jnp.broadcast_to(a[None, :], (8, cols_dev)) for a in (attn_gain, ffn_gain)]),
         ],
         0,
         [spread_heads, spread_out],
-    )
-    joint = dot(natural, permutation, ((1,), (0,))).astype(BF16)
+        [grad_ffn],
+    )
     gain_two_all = gain_all[8:]
-    grad_ffn, x_all = lax.optimization_barrier((grad_ffn, x_all))
-    grad_ffn_all = lax.all_gather(grad_ffn, ("row", "col"), axis=0, tiled=False)
-
-    wide = x_all.astype(F32)
-    scale_one = lax.rsqrt(jnp.mean(wide * wide, axis=1) + NORM_EPS)
-    normed_one = (wide * scale_one[:, None] * gain_all[:1]).astype(BF16)
-
-    pre = dot(normed_one, joint, ((1,), (0,)))
-    pre_one, pre_two = pre[:, :128], pre[:, 128:256]
-    rot = jnp.concatenate(
-        [pre_one * cosine - pre_two * sine, pre_two * cosine + pre_one * sine], axis=1
-    ).astype(BF16)
-    val = pre[:, 256:].astype(BF16)
-    heads_out, log_all = attend_forward(low, rot, val, first_rows)
-    attn_part = dot(heads_out, out_rows, ((1,), (0,))).astype(BF16)
+    down_weight, x_all = lax.optimization_barrier((down_weight, x_all))
+    down = lax.all_to_all(down_weight.reshape(nz, ffn, cols_dev), "col", 0, 0, tiled=True)
+    grad_ffn_all = lax.all_gather(grad_col, "row", axis=0, tiled=True)
+
+    normed_one, scale_one, rot, val, heads_out, log_all, attn_part = attend_forward(
+        low, x_all, gain_all[:1], natural, permutation, out_rows, cosine, sine, first_rows
+    )
 
     def units_piece(which):
         return (
@@ -1297,19 +1413,6 @@
 
     spread_gate_up = Spread(
         [gate_weight, up_weight], [units_piece(0), units_piece(1)], [(width, 2 * ffn)], share
-    )
-    spread_down = Spread(
-        [down_weight],
-        [
-            (
-                0,
-                lambda c, h: (at(c * ffn + h * ffn_part, ffn_part), every),
-                0,
-                lambda c, h: (at(h * ffn_part, ffn_part), at(c * cols_dev, cols_dev)),
-            )
-        ],
-        [(ffn, width)],
-        share,
     )
     (attn_sum,), (gate_up,) = reduce_scatter([attn_part], 1, [spread_gate_up])
     resid_mid = residual + RES_SCALE * attn_sum
@@ -1323,14 +1426,14 @@
                 (ffn_part, width),
             )
         ]
-    (_, down_part_sum, scale_wide, grad_a, grad_b, inner_two_sum, pair_grad_part, down_grad_part), others = (
+    (scale_wide, grad_a, grad_b, inner_two_sum, down_grad_part), down_parts, pair_parts, others = (
         feed_forward(
             (resid_mid * ffn_gain[None, :]).astype(BF16),
             1.0 / gain_two_all[:1],
             gate_up,
+            down,
             grad_ffn_all,
             2,
-            [spread_down],
             late,
         )
     )
@@ -1368,46 +1471,47 @@
 
     (grad_attn_all,), (down_grad,) = gather([grad_attn], 5, [spread_down_grad])
 
-    pair_half = pair_grad_part[0]
+    pair_half = pair_parts[0]
     if two:
-        pair_half = plus(pair_half, lax.ppermute(pair_grad_part[1], "group", [(0, 1), (1, 0)]))
-
+        swapped = lax.ppermute(pair_parts[1], "group", [(0, 1), (1, 0)])
+        swapped, grad_attn_all = lax.optimization_barrier((swapped, grad_attn_all))
+        pair_half = plus(pair_half, swapped)
     pair_half = lax.all_to_all(
         pair_half.reshape(nz, cols_dev, 2 * ffn_part), "col", 0, 0, tiled=True
     )
-    pair_other = lax.ppermute(pair_half, "group", [(0, 1), (1, 0)]) if two else pair_half
 
     def step_over(a, axis, jump):
         count = lax.axis_size(axis)
-        if jump == 2:
-            pairs = [(m, (m + 2) % count) for m in range(count)]
-        else:
-            pairs = [(m, m + 1 - 2 * (m % 2)) for m in range(count)]
-        return lax.ppermute(a, axis, pairs)
-
-    down_x = plus(down_part_sum[0], step_over(down_part_sum[1], "row", 1))
-    down_x, grad_attn_all = lax.optimization_barrier((down_x, grad_attn_all))
-    down_z = plus(down_x[0], step_over(down_x[1], "row", 2))
-    down_got = step_over(down_z[:2], "col", 1)
-    down_far = step_over(plus(down_z[2], down_got[0]), "col", 2)
-    down_sum = down_z[3].astype(F32) + down_got[1].astype(F32) + down_far.astype(F32)
-    layer_out = (resid_mid + RES_SCALE * down_sum).astype(BF16)
-
-    grad_heads = dot(grad_attn_all, out_rows, ((1,), (1,))).astype(BF16)
-    out_grad_part = dot(heads_out, grad_attn_all, ((0,), (0,))).astype(BF16)
-    grad_rot, grad_val = attend_backward(
-        low, rot, val, first_rows, log_all, heads_out, grad_heads
-    )
-    inner_one = jnp.sum(grad_rot * rot.astype(F32), axis=1) + jnp.sum(
-        grad_val * val.astype(F32), axis=1
-    )
-    grot_one, grot_two = grad_rot[:, :128], grad_rot[:, 128:]
-    grad_pre = jnp.concatenate(
-        [grot_one * cosine + grot_two * sine, grot_two * cosine - grot_one * sine, grad_val], axis=1
+        near = [m + 1 - 2 * (m % 2) for m in range(count)]
+        goal = [(m + 2) % count if jump == 2 else (near[m] + jump - 1) % count for m in range(count)]
+        return lax.ppermute(a, axis, list(enumerate(goal)))
+
+    from_core = step_over(down_parts[1], "row", 1)
+    from_core, grad_attn_all = lax.optimization_barrier((from_core, grad_attn_all))
+    down_away = plus(down_parts[0][1], from_core[1])
+    from_x = step_over(down_away, "row", 2)
+
+    grad_one_part, natural_grad, out_grad_part, inner_one = attend_backward(
+        low,
+        grad_attn_all,
+        normed_one,
+        natural,
+        permutation,
+        out_rows,
+        cosine,
+        sine,
+        rot,
+        val,
+        first_rows,
+        log_all,
+        heads_out,
+    )
+    grad_one_part, from_x, pair_half = lax.optimization_barrier((grad_one_part, from_x, pair_half))
+    pair_other = lax.ppermute(pair_half, "group", [(0, 1), (1, 0)]) if two else pair_half
+    down_z = (
+        down_parts[0][0].astype(F32) + from_core[0].astype(F32) + from_x.astype(F32)
     ).astype(BF16)
-    grad_natural = dot(grad_pre, permutation, ((1,), (1,))).astype(BF16)
-    grad_one_part = dot(grad_natural, natural, ((1,), (1,))).astype(BF16)
-    natural_grad = dot(normed_one, grad_natural, ((0,), (0,)))
+    down_got = [step_over(down_z[m], "col", jump) for m, jump in enumerate((3, 1, 2))]
     attn_gain_part = jnp.sum(natural_grad * natural.astype(F32), axis=1) / gain_all[0]
     natural_grad = natural_grad.astype(BF16)
     mine = (jnp.arange(nz) == col)[:, None, None]
@@ -1451,7 +1555,7 @@
     (grad_one, last), small = reduce_scatter(
         [grad_one_part, stats], 6, [spread_small]
     )
-    scale_one_own = lax.dynamic_slice_in_dim(scale_one, row * rows_dev, rows_dev)[:, None]
+    scale_one_own = lax.dynamic_slice_in_dim(scale_one, row * rows_dev, rows_dev)[:, :1]
     inner_one_own = last[:4].reshape(rows_dev, 1)
     input_grad = (
         grad_mid
@@ -1465,6 +1569,9 @@
         )
         down_grad = down_grad.astype(F32)
         gate_grad, up_grad = assemble(pair_half, pair_other)
+        gate_grad, up_grad, out_grad, query_grad, kv_grad, down_z = lax.optimization_barrier(
+            (gate_grad, up_grad, out_grad, query_grad, kv_grad, down_z)
+        )
     else:
         out_grad, query_grad, kv_grad, down_grad, pair_grad = (
             lax.psum(a, "group").astype(F32) for a in (*small, down_grad, pair_half)
@@ -1475,9 +1582,14 @@
             )
             for m in range(2)
         )
-    kv_grad = jnp.sum(kv_grad.reshape(cols_dev, 2, nz // 2, 2, HEAD_SIZE), axis=2)
-    key_grad = kv_grad[:, :, 0].reshape(cols_dev, 2 * HEAD_SIZE)
-    value_grad = kv_grad[:, :, 1].reshape(cols_dev, 2 * HEAD_SIZE)
+    down_sum = down_z[3].astype(F32) + sum(a.astype(F32) for a in down_got)
+    layer_out = (resid_mid + RES_SCALE * down_sum).astype(BF16)
+    shared = [
+        sum(kv_grad[:, c * kv : (c + 1) * kv] for c in range(m * nz // 2, (m + 1) * nz // 2))
+        for m in range(2)
+    ]
+    key_grad = jnp.concatenate([a[:, :HEAD_SIZE] for a in shared], axis=1)
+    value_grad = jnp.concatenate([a[:, HEAD_SIZE:] for a in shared], axis=1)
     return (
         layer_out,
         input_grad,

time: 731 us -> 697 us (0.953)
  matrix products: 34.5 us -> 0 us
  local copies, waits for them, and re-layouts: 30.4 us -> 11.6 us
  waiting for transfers between devices: 19 us -> 30.8 us
    pallas_call x2, Pallas kernels: 208 us -> 169 us  [reduce_scatter(): pl.pallas_call(functools.partial(scatter_kernel, n, nz, extras), out_shap...]
    pallas_call x2, Pallas kernels: 138 us -> 174 us  [gather(): pl.pallas_call(functools.partial(gather_kernel, n, nz, units, extras), ou...]
    dot_general x7 -> x0, matrix products: 34.5 us -> none  [dot(): return lax.dot_general(a, b, (dims, ((), ())), preferred_element_type=F32)]
    ppermute x1, waiting for transfers between devices: 0.01 us -> 29.9 us  [sum_over_group(): other = lax.ppermute(operand, 'group', [(0, 1), (1, 0)])]
    pallas_call x1, Pallas kernels: 181 us -> 156 us  [feed_forward(): pl.pallas_call(functools.partial(feed_forward_kernel, nz, late), out_shap...]
    pallas_call x1, Pallas kernels: 16.6 us -> 35.6 us  [attend_backward(): pl.pallas_call(attend_backward_kernel, grid_spec=pltpu.PrefetchScalarGrid...]
    pallas_call x1, Pallas kernels: 11.7 us -> 28.1 us  [attend_forward(): pl.pallas_call(attend_forward_kernel, grid_spec=pltpu.PrefetchScalarGridS...]
    ppermute x5 -> x6, waiting for transfers between devices: 11.3 us -> 0.9 us  [the longest x5 0.9 us: step_over(): return lax.ppermute(a, axis, list(enumerate(goal)))]
  transfers between devices with their start and end apart: 9 -> 11, of which waited for: 3 -> 2; matrix products, arithmetic and copies ran while one was open for 13% -> 7% of each run, Pallas kernels for 15% -> 21%
where the time goes in v4:
time: 697 us; the launch traced here: 691 us
  Pallas kernels  570 us (82%)
  other arithmetic  44.8 us (6%)
  waiting for transfers between devices  30.8 us (4%)
  starting transfers between devices  18.5 us (3%)
  between operations  15.3 us (2%)
  local copies, waits for them, and re-layouts  11.6 us (2%)
    pallas_call x2, Pallas kernels, gather(): pl.pallas_call(functools.partial(gather_kernel, n, nz, units, extras), ou...  174 us
    pallas_call x2, Pallas kernels, reduce_scatter(): pl.pallas_call(functools.partial(scatter_kernel, n, nz, extras), out_shap...  169 us
    pallas_call x1, Pallas kernels, feed_forward(): pl.pallas_call(functools.partial(feed_forward_kernel, nz, late), out_shap...  156 us
    pallas_call x1, Pallas kernels, attend_backward(): pl.pallas_call(attend_backward_kernel, grid_spec=pltpu.PrefetchScalarGrid...  35.6 us
    ppermute x1, waiting for transfers between devices, sum_over_group(): other = lax.ppermute(operand, 'group', [(0, 1), (1, 0)])  29.9 us
    pallas_call x1, Pallas kernels, attend_forward(): pl.pallas_call(attend_forward_kernel, grid_spec=pltpu.PrefetchScalarGridS...  28.1 us
  transfers between devices with their start and end apart: 11, of which 2 were waited for; matrix products, arithmetic and copies ran while one was open for 7% of the time, Pallas kernels for 21%

profile of v4, /device:TPU:0, one launch (start us, length us, event | category | flops | bytes accessed | tf_op | source)
XLA Modules:
  0.0 690.5 jit_solution(15427212341078296678)
XLA Ops:
  7.2 1.9 fusion.4.refs_2_
  12.0 100.6 %gather.12 = (bf16[2048,2048]{1,0:T(8,128)(2,1)}, f32[64,2048]{1,0:T(8,128)}, bf16[512,2048]{1,0:T(8,128)(2,1)}, bf16[2048,256]{1,0:T(8,128)(2,1)}, bf16[128,2048]{1,0:T(8,128)(2,1)}) custom-call(bf16[512,512]{1,0:T(8,128)(2,1)} %refs_0_.1, f32[16,512]{1,0:T(8,128)} %pad_maximum_fusion.3.refs_1_, bf16[512,512]{1,0:T(8,128)(2,1)} %fusion.4.refs_2_, ...), custom_call_target="tpu_custom_call" | custom-call | bytes 1048576 | tf_op jit(solution)/shard_map/gather/pallas_call | solution.py:403
  112.7 4.6 all-to-all-start
  119.4 1.5 slice_divide_fusion
  120.9 5.3 multiply_sine_fusion
  126.2 28.1 %attend_forward.1 = (bf16[2048,2048]{1,0:T(8,128)(2,1)}, f32[2048,128]{1,0:T(8,128)S(1)}, bf16[2048,256]{1,0:T(8,128)(2,1)S(1)}, bf16[2048,128]{1,0:T(8,128)(2,1...) custom-call(s32[8]{0:T(128)S(1)} %and_select_fusion.low_ref, ...), custom_call_target="tpu_custom_call" | custom-call | bytes 1048576 | tf_op jit(solution)/shard_map/attend_forward/pallas_call | solution.py:1146
  155.1 90.5 %reduce_scatter.2 = (f32[512,512]{1,0:T(8,128)S(1)}, bf16[2048,1024]{1,0:T(8,128)(2,1)}) custom-call(bf16[2048,2048]{1,0:T(8,128)(2,1)} %get-tuple-element.71.refs_0_, bf16[512,2048]{1,0:T(8,128)(2,1)S(1)} %copy-done.2, bf16[512,2048]{1,0:T(8,128)(2,1)S(1)} %copy-done.3), custom_call_target="tpu_custom_call" | custom-call | bytes 1048576 | tf_op jit(solution)/shard_map/reduce_scatter/pallas_call | solution.py:606
  246.7 155.9 %feed_forward.1 = (bf16[2048,2048]{1,0:T(8,128)(2,1)}, f32[2048,128]{1,0:T(8,128)}, f32[256,512]{1,0:T(8,128)}, f32[256,512]{1,0:T(8,128)}, f32[8,128]{1,0:T(8,1...) custom-call(bf16[512,512]{1,0:T(8,128)(2,1)} %multiply_convert_fusio, ...), custom_call_target="tpu_custom_call" | custom-call | bytes 1048576 | tf_op jit(solution)/shard_map/feed_forward/pallas_call | solution.py:909
  406.6 1.5 dynamic-slice_reduce_fusion.1
  410.9 73.1 %gather.13 = (bf16[2048,2048]{1,0:T(8,128)(2,1)}, bf16[2048,512]{1,0:T(8,128)(2,1)}) custom-call(bf16[512,512]{1,0:T(8,128)(2,1)} %get-tuple-element.126.refs_0_, bf16[256,2048]{1,0:T(8,128)(2,1)} %fusion.2.refs_1_), custom_call_target="tpu_custom_call" | custom-call | bytes 1048576 | tf_op jit(solution)/shard_map/gather/pallas_call | solution.py:403
  483.9 4.2 add_convert_fusion
  488.1 4.4 all-to-all-start.1
  492.6 4.2 fusion.1
  498.1 4.3 convert_element_type.159
  502.6 35.6 %attend_backward.1 = (bf16[2048,2048]{1,0:T(8,128)(2,1)}, f32[2048,256]{1,0:T(8,128)}, bf16[128,2048]{1,0:T(8,128)(2,1)S(1)}, f32[16,128]{1,0:T(8,128)S(1)}) custom-call(s32[8]{0:T(128)S(1)} %and_select_fusion.low_ref, bf16[2048,2048]{1,0:T(8,128)(2,1)} %get-tuple-element.86.incoming_ref, bf16[2048,2048]{1,0:T(8,128)(2,1)} %get-tuple-element.87.normed_ref, ...), custom_call_target="tpu_custom_call" | custom-call | bytes 1048576 | tf_op jit(solution)/shard_map/attend_backward/pallas_call | solution.py:1205
  538.2 2.8 fusion.10
  543.2 78.7 %reduce_scatter.3 = (f32[512,512]{1,0:T(8,128)S(1)}, f32[16,128]{1,0:T(8,128)S(1)}, bf16[512,512]{1,0:T(8,128)(2,1)S(1)}, bf16[512,512]{1,0:T(8,128)(2,1)S(1)}, ...) custom-call(bf16[2048,2048]{1,0:T(8,128)(2,1)} %get-tuple-element.10, ...), custom_call_target="tpu_custom_call" | custom-call | bytes 1048576 | tf_op jit(solution)/shard_map/reduce_scatter/pallas_call | solution.py:606
  622.6 1.5 collective-permute-start.7
  624.1 3.1 fusion
  629.1 5.3 collective-permute-start.4
  635.2 1.5 convert_add_fusion.4
  640.1 29.9 %collective-permute-done.7 = f32[8,128]{1,0:T(8,128)S(1)} collective-permute-done((f32[8,128]{1,0:T(8,128)S(1)}, f32[8,128]{1,0:T(8,128)S(1)}, u32[]{:S(2)}, u32[]{:S(2)}) %collective-permute-start.7) | collective-permute-done | bytes 4128 | tf_op jit(solution)/shard_map/ppermute | solution.py:1285
  670.6 7.0 %assemble.1 = (f32[512,2048]{1,0:T(8,128)}, f32[512,2048]{1,0:T(8,128)}) custom-call(bf16[4,512,512]{2,1,0:T(8,128)(2,1)} %all-to-all-done.1.mine_ref, bf16[4,512,512]{2,1,0:T(8,128)(2,1)S(1)} %collective-permute-done.3.other_ref), custom_call_target="tpu_custom_call" | custom-call | bytes 25165824 | tf_op jit(solution)/shard_map/assemble/pallas_call | solution.py:1258
  679.8 3.5 fusion.3
  (158 shorter events, 26.0 us)
Async XLA Ops:
  7.2 239.5 %all-gather.2.cloned.1.call-start = ((), (), s32[]{:S(2)}) async-start(), calls=%async_computation.2 | async-start | bytes 10485760 | tf_op jit(solution)/shard_map/all_gather | solution.py:1400
  112.6 5.4 copy-start.41
  112.7 6.2 copy-start.38
  112.7 134.0 %all-to-all-start = ((bf16[4,512,512]{2,1,0:T(8,128)(2,1)}), bf16[4,512,512]{2,1,0:T(8,128)(2,1)}, u32[]{:S(2)}, u32[]{:S(2)}) async-start(bf16[4,512,512]{2,1,0:T(8,128)(2,1)} %bitcast.2), calls=%async_computation | async-start | bytes 4194304 | tf_op jit(solution)/shard_map/all_to_all | solution.py:1399
  117.3 8.9 %copy-start.1 = (bf16[2048,256]{1,0:T(8,128)(2,1)S(1)}, bf16[2048,256]{1,0:T(8,128)(2,1)}, u32[]{:S(2)}) copy-start(bf16[2048,256]{1,0:T(8,128)(2,1)} %get-tuple-element.69.natural_ref) | copy-start | bytes 3145732
  117.3 8.9 %copy-start.4 = (bf16[128,2048]{1,0:T(8,128)(2,1)S(1)}, bf16[128,2048]{1,0:T(8,128)(2,1)}, u32[]{:S(2)}) copy-start(bf16[128,2048]{1,0:T(8,128)(2,1)} %get-tuple-element.70.weight_ref) | copy-start | bytes 1572868
  126.2 28.9 %copy-start.2 = (bf16[512,2048]{1,0:T(8,128)(2,1)S(1)}, bf16[512,2048]{1,0:T(8,128)(2,1)}, u32[]{:S(2)}) copy-start(bf16[512,2048]{1,0:T(8,128)(2,1)} %refs_1_.1) | copy-start | bytes 6291460
  126.2 28.9 %copy-start.3 = (bf16[512,2048]{1,0:T(8,128)(2,1)S(1)}, bf16[512,2048]{1,0:T(8,128)(2,1)}, u32[]{:S(2)}) copy-start(bf16[512,2048]{1,0:T(8,128)(2,1)} %refs_2_.1) | copy-start | bytes 6291460
  155.1 90.6 %copy-start.8 = (bf16[2048,256]{1,0:T(8,128)(2,1)}, bf16[2048,256]{1,0:T(8,128)(2,1)S(1)}, u32[]{:S(2)}) copy-start(bf16[2048,256]{1,0:T(8,128)(2,1)S(1)} %get-tuple-element.88.rot_ref) | copy-start | bytes 3145732
  155.1 90.6 %copy-start.23 = (bf16[2048,128]{1,0:T(8,128)(2,1)}, bf16[2048,128]{1,0:T(8,128)(2,1)S(1)}, u32[]{:S(2)}) copy-start(bf16[2048,128]{1,0:T(8,128)(2,1)S(1)} %get-tuple-element.91.out_ref) | copy-start | bytes 1572868
  155.1 90.6 %copy-start.25 = (f32[2048,128]{1,0:T(8,128)}, f32[2048,128]{1,0:T(8,128)S(1)}, u32[]{:S(2)}) copy-start(f32[2048,128]{1,0:T(8,128)S(1)} %get-tuple-element.112) | copy-start | bytes 3145732
  155.1 90.6 %copy-start.26 = (bf16[512,512]{1,0:T(8,128)(2,1)S(1)}, bf16[512,512]{1,0:T(8,128)(2,1)}, u32[]{:S(2)}) copy-start(bf16[512,512]{1,0:T(8,128)(2,1)} %refs_0_.1) | copy-start | bytes 1572868
  402.6 90.0 %collective-permute-start = (bf16[2,4,512,512]{3,2,1,0:T(8,128)(2,1)}, bf16[2,4,512,512]{3,2,1,0:T(8,128)(2,1)}, u32[]{:S(2)}, u32[]{:S(2)}) collective-permute-start(bf16[2,4,512,512]{3,2,1,0:T(8,128)(2,1)} %get-tuple-element.76), channel_id=1, source_target_pairs={{0,4},{4,0},{8,12},{12,8},{1,5},{5,1},{9,13},{13,9},{2,6},{6,2},{1... | collective-permute-start | bytes 12582920 | tf_op jit(solution)/shard_map/ppermute | solution.py:1487
  402.7 81.3 %collective-permute-start.1 = (bf16[2048,512]{1,0:T(8,128)(2,1)}, bf16[2048,512]{1,0:T(8,128)(2,1)}, u32[]{:S(2)}, u32[]{:S(2)}) collective-permute-start(bf16[2048,512]{1,0:T(8,128)(2,1)} %get-tuple-element.77), channel_id=1, source_target_pairs={{0,16},{16,0},{1,17},{17,1},{2,18},{18,2},{3,19},{19,3},{4,20},{20... | collective-permute-start | bytes 6291464 | tf_op jit(solution)/shard_map/ppermute | solution.py:1476
  488.1 53.1 %all-to-all-start.1 = ((bf16[4,512,512]{2,1,0:T(8,128)(2,1)}), bf16[4,512,512]{2,1,0:T(8,128)(2,1)}, u32[]{:S(2)}, u32[]{:S(2)}) async-start(bf16[4,512,512]{2,1,0:T(8,128)(2,1)} %bitcast.43), calls=%async_computation.1 | async-start | bytes 4194304 | tf_op jit(solution)/shard_map/all_to_all | solution.py:1479
  496.8 45.4 %collective-permute-start.2 = (bf16[4,512,512]{2,1,0:T(8,128)(2,1)}, bf16[4,512,512]{2,1,0:T(8,128)(2,1)}, u32[]{:S(2)}, u32[]{:S(2)}) collective-permute-start(bf16[4,512,512]{2,1,0:T(8,128)(2,1)} %fusion.1), channel_id=1, source_target_pairs={{0,8},{4,12},{8,0},{12,4},{1,9},{5,13},{9,1},{13,5},{2,10},{6,14},... | collective-permute-start | bytes 6291464 | tf_op jit(solution)/shard_map/ppermute | solution.py:1487
  543.2 80.9 %copy-start.34 = (bf16[2,4,512,512]{3,2,1,0:T(8,128)(2,1)S(1)}, bf16[2,4,512,512]{3,2,1,0:T(8,128)(2,1)}, u32[]{:S(2)}) copy-start(bf16[2,4,512,512]{3,2,1,0:T(8,128)(2,1)} %get-tuple-element.93) | copy-start | bytes 12582916
  621.9 5.3 copy-start.6
  621.9 5.3 copy-start.11
  622.0 48.6 %collective-permute-start.3 = (bf16[4,512,512]{2,1,0:T(8,128)(2,1)}, bf16[4,512,512]{2,1,0:T(8,128)(2,1)S(1)}, u32[]{:S(2)}, u32[]{:S(2)}) collective-permute-start(bf16[4,512,512]{2,1,0:T(8,128)(2,1)} %all-to-all-done.1.mine_ref), channel_id=1, source_target_pairs={{0,16},{16,0},{1,17},{17,1},{2,18},{18,2},{3,19},{19,3},{4,20},{20... | collective-permute-start | bytes 6291464 | tf_op jit(solution)/shard_map/ppermute | solution.py:1510
  622.6 47.4 %collective-permute-start.7 = (f32[8,128]{1,0:T(8,128)S(1)}, f32[8,128]{1,0:T(8,128)S(1)}, u32[]{:S(2)}, u32[]{:S(2)}) collective-permute-start(f32[8,128]{1,0:T(8,128)S(1)} %slice.122), channel_id=1, source_target_pairs={{0,16},{16,0},{1,17},{17,1},{2,18},{18,2},{3,19},{19,3},{4,20},{20... | collective-permute-start | bytes 12296 | tf_op jit(solution)/shard_map/ppermute | solution.py:1285
  629.1 50.6 %collective-permute-start.4 = (bf16[512,512]{1,0:T(8,128)(2,1)}, bf16[512,512]{1,0:T(8,128)(2,1)}, u32[]{:S(2)}, u32[]{:S(2)}) collective-permute-start(bf16[512,512]{1,0:T(8,128)(2,1)} %get-tuple-element.129), channel_id=1, source_target_pairs={{0,3},{1,2},{2,1},{3,0},{4,7},{5,6},{6,5},{7,4},{8,11},{9,10},{10,... | collective-permute-start | bytes 1572872 | tf_op jit(solution)/shard_map/ppermute | solution.py:1487
  634.4 45.3 %collective-permute-start.5 = (bf16[512,512]{1,0:T(8,128)(2,1)}, bf16[512,512]{1,0:T(8,128)(2,1)}, u32[]{:S(2)}, u32[]{:S(2)}) collective-permute-start(bf16[512,512]{1,0:T(8,128)(2,1)} %get-tuple-element.131), channel_id=1, source_target_pairs={{0,1},{1,0},{2,3},{3,2},{4,5},{5,4},{6,7},{7,6},{8,9},{9,8},{10,11... | collective-permute-start | bytes 1572872 | tf_op jit(solution)/shard_map/ppermute | solution.py:1487
  634.4 45.3 %collective-permute-start.6 = (bf16[512,512]{1,0:T(8,128)(2,1)}, bf16[512,512]{1,0:T(8,128)(2,1)}, u32[]{:S(2)}, u32[]{:S(2)}) collective-permute-start(bf16[512,512]{1,0:T(8,128)(2,1)} %get-tuple-element.130), channel_id=1, source_target_pairs={{0,2},{1,3},{2,0},{3,1},{4,6},{5,7},{6,4},{7,5},{8,10},{9,11},{10,... | collective-permute-start | bytes 1572872 | tf_op jit(solution)/shard_map/ppermute | solution.py:1487
  (30 other events, 97.3 us)
Sparse Core Ops, SparseCore 0:
  112.8 60.7 all-gather.1
